TPU v7x, 32 devices: a whole 2x2x4 slice. The times are simulated.
32 devices in a mesh: rep: 4 (over x, core), shard: 8 (over z, y).
Axes of the slice: x: 2, y: 2, z: 4, core: 2. Of those that a mesh axis runs over, the one named last changes fastest.
Arguments:
- tokens: bfloat16 [64, 320, 1024], P(('rep', 'shard')), may hold values from -6 to 6
- lengths: int32 [64], P(('rep', 'shard')), may hold values from 192 to 320, as said below
- cotangent: bfloat16 [64, 320, 1024], P(('rep', 'shard')), may hold values from -6 to 6
- norm_gain: float32 [1024], P('shard'), may hold values from 0.5 to 1.5
- norm_shift: float32 [1024], P('shard'), may hold values from -4 to 4
- joint_weight: float32 [1024, 3072], P('shard'), may hold values from -0.1875 to 0.1875
- joint_bias: float32 [2048], P('shard'), may hold values from -6 to 6
- mixer_weight: float32 [1024, 1024], P('shard'), may hold values from -1.5 to 1.5
- mixer_bias: float32 [1024], P('shard'), may hold values from -4 to 4
- ffnorm_gain: float32 [1024], P('shard'), may hold values from 0.5 to 1.5
- ffnorm_shift: float32 [1024], P('shard'), may hold values from -4 to 4
- expand_weight: float32 [1024, 4096], P('shard'), may hold values from -0.1875 to 0.1875
- expand_bias: float32 [4096], P('shard'), may hold values from -6 to 6
- reduce_weight: float32 [4096, 1024], P('shard'), may hold values from -0.09375 to 0.09375
- reduce_bias: float32 [1024], P('shard'), may hold values from -4 to 4
Outputs:
- layer_out: bfloat16 [64, 320, 1024], P(('rep', 'shard'))
- input_grad: bfloat16 [64, 320, 1024], P(('rep', 'shard'))
- dnorm_gain: float32 [1024], P('shard')
- dnorm_shift: float32 [1024], P('shard')
- djoint_weight: float32 [1024, 3072], P('shard')
- djoint_bias: float32 [2048], P('shard')
- dmixer_weight: float32 [1024, 1024], P('shard')
- dmixer_bias: float32 [1024], P('shard')
- dffnorm_gain: float32 [1024], P('shard')
- dffnorm_shift: float32 [1024], P('shard')
- dexpand_weight: float32 [1024, 4096], P('shard')
- dexpand_bias: float32 [4096], P('shard')
- dreduce_weight: float32 [4096, 1024], P('shard')
- dreduce_bias: float32 [1024], P('shard')
Inputs may be any that keep to these rules, and one draw needn't show every extreme that they name: `lengths`: kept tokens of each sequence; some sequence keeps all 320 slots and some keeps 192 in every draw.
All inputs are finite; a program needn't handle non-finite values.
Results may differ from a plain program's by a relative error of at most 0.018.
Values may be sent and summed in bfloat16 or wider, within the bound.
No kernel may reach another device: no remote copies, remote signals or barrier semaphores. Data moves between devices by JAX's collectives and lax.ppermute only.
A program may use at most 192 MiB of HBM per device.

v0:
```python
import jax
import jax.numpy as jnp
from jax import lax
from jax.sharding import PartitionSpec as P

H = 16
HD = 64


epsilon = 1e-06


def layer_norm(matrix, gain_vec, shift_vec):
    average = jnp.mean(matrix, axis=-1, keepdims=True)
    centred = matrix - average
    spread = jnp.mean(centred * centred, axis=-1, keepdims=True)
    return centred * lax.rsqrt(spread + epsilon) * gain_vec + shift_vec


def outer_sum(left_side, right_side):
    return lax.dot_general(
        left_side, right_side, (((0,), (0,)), ((), ())), preferred_element_type=jnp.float32
    )


def back_product(cotan, weight):
    return lax.dot_general(
        cotan, weight, (((1,), (1,)), ((), ())), preferred_element_type=jnp.float32
    )


def masked_scores(queries, key_block, length):
    factor = queries.shape[-1] ** (-0.5)
    raw_scores = jnp.einsum("qhd,khd->hqk", queries, key_block, preferred_element_type=jnp.float32)
    kept_keys = jnp.arange(key_block.shape[0]) < length
    return jnp.where(kept_keys[None, None, :], raw_scores * factor, -1e30)


def attend_forward(element):
    queries, key_block, values, length = element
    scores = masked_scores(queries, key_block, length)
    peak_score = jnp.max(scores, axis=-1, keepdims=True)
    raised = jnp.exp(scores - peak_score)
    totals = jnp.sum(raised, axis=-1, keepdims=True)
    shares = (raised / totals).astype(jnp.bfloat16)
    attended = jnp.einsum("hqk,khd->qhd", shares, values, preferred_element_type=jnp.float32)
    return (attended.astype(jnp.bfloat16), (peak_score + jnp.log(totals))[..., 0])


def attend_backward(element):
    queries, key_block, values, log_total, grad_attended, length = element
    factor = queries.shape[-1] ** (-0.5)
    shares = jnp.exp(masked_scores(queries, key_block, length) - log_total[..., None])
    grad_shares = jnp.einsum(
        "qhd,khd->hqk", grad_attended, values, preferred_element_type=jnp.float32
    )
    inner_sum = jnp.sum(shares * grad_shares, axis=-1, keepdims=True)
    grad_raw = (shares * (grad_shares - inner_sum) * factor).astype(jnp.bfloat16)
    grad_query = jnp.einsum("hqk,khd->qhd", grad_raw, key_block, preferred_element_type=jnp.float32)
    grad_keys = jnp.einsum("hqk,qhd->khd", grad_raw, queries, preferred_element_type=jnp.float32)
    grad_values = jnp.einsum(
        "hqk,qhd->khd",
        shares.astype(jnp.bfloat16),
        grad_attended,
        preferred_element_type=jnp.float32,
    )
    return (
        grad_query.astype(jnp.bfloat16),
        grad_keys.astype(jnp.bfloat16),
        grad_values.astype(jnp.bfloat16),
    )


def narrow(master):
    return master.astype(jnp.bfloat16)


def on_device(
    tokens,
    lengths,
    cotangent,
    norm_gain,
    norm_shift,
    joint_weight,
    joint_bias,
    mixer_weight,
    mixer_bias,
    ffnorm_gain,
    ffnorm_shift,
    expand_weight,
    expand_bias,
    reduce_weight,
    reduce_bias,
):
    gathered = (
        lax.all_gather(narrow(norm_gain), "shard", axis=0, tiled=True),
        lax.all_gather(narrow(norm_shift), "shard", axis=0, tiled=True),
        lax.all_gather(narrow(joint_weight), "shard", axis=0, tiled=True),
        lax.all_gather(narrow(joint_bias), "shard", axis=0, tiled=True),
        lax.all_gather(narrow(mixer_weight), "shard", axis=0, tiled=True),
        lax.all_gather(narrow(mixer_bias), "shard", axis=0, tiled=True),
        lax.all_gather(narrow(ffnorm_gain), "shard", axis=0, tiled=True),
        lax.all_gather(narrow(ffnorm_shift), "shard", axis=0, tiled=True),
        lax.all_gather(narrow(expand_weight), "shard", axis=0, tiled=True),
        lax.all_gather(narrow(expand_bias), "shard", axis=0, tiled=True),
        lax.all_gather(narrow(reduce_weight), "shard", axis=0, tiled=True),
        lax.all_gather(narrow(reduce_bias), "shard", axis=0, tiled=True),
    )
    (
        gain_one,
        shift_one,
        joint_matrix,
        joint_vector,
        mixer_matrix,
        mixer_vector,
        gain_two,
        shift_two,
        expand_matrix,
        expand_vector,
        reduce_matrix,
        reduce_vector,
    ) = gathered
    seq_count, seq_length, model_width = tokens.shape
    row_count = seq_count * seq_length
    flat_rows = tokens.astype(jnp.float32).reshape(row_count, model_width)
    positions = jnp.arange(seq_length)
    kept_rows = (positions[None, :] < lengths[:, None]).reshape(row_count, 1).astype(jnp.float32)
    normed, first_pull = jax.vjp(
        layer_norm, flat_rows, gain_one.astype(jnp.float32), shift_one.astype(jnp.float32)
    )
    normed_low = normed.astype(jnp.bfloat16)
    bias_full = jnp.concatenate(
        [
            joint_vector[:model_width].astype(jnp.float32),
            jnp.zeros((model_width,), jnp.float32),
            joint_vector[model_width:].astype(jnp.float32),
        ]
    )
    joint_rows = (
        jnp.dot(normed_low, joint_matrix, preferred_element_type=jnp.float32) + bias_full
    ).astype(jnp.bfloat16)
    joint_rows = joint_rows.reshape(seq_count, seq_length, 3, H, HD)
    queries = joint_rows[:, :, 0]
    key_block = joint_rows[:, :, 1]
    values = joint_rows[:, :, 2]
    attended, log_total = lax.map(attend_forward, (queries, key_block, values, lengths))
    attended_rows = attended.reshape(row_count, model_width)
    hidden = (
        flat_rows
        + jnp.dot(attended_rows, mixer_matrix, preferred_element_type=jnp.float32)
        + mixer_vector.astype(jnp.float32)
    )
    normed_two, second_pull = jax.vjp(
        layer_norm, hidden, gain_two.astype(jnp.float32), shift_two.astype(jnp.float32)
    )
    second_low = normed_two.astype(jnp.bfloat16)
    before = jnp.dot(
        second_low, expand_matrix, preferred_element_type=jnp.float32
    ) + expand_vector.astype(jnp.float32)
    active, gelu_pull = jax.vjp(jax.nn.gelu, before)
    active_low = active.astype(jnp.bfloat16)
    branch = jnp.dot(
        active_low, reduce_matrix, preferred_element_type=jnp.float32
    ) + reduce_vector.astype(jnp.float32)
    layer_out = ((hidden + branch) * kept_rows).astype(jnp.bfloat16).reshape(tokens.shape)
    regathered = (
        lax.all_gather(narrow(joint_weight), "shard", axis=0, tiled=True),
        lax.all_gather(narrow(mixer_weight), "shard", axis=0, tiled=True),
        lax.all_gather(narrow(expand_weight), "shard", axis=0, tiled=True),
        lax.all_gather(narrow(reduce_weight), "shard", axis=0, tiled=True),
    )
    joint_back, mixer_back, expand_back, reduce_back = regathered
    grad_out = cotangent.astype(jnp.float32).reshape(row_count, model_width) * kept_rows
    grad_branch = grad_out.astype(jnp.bfloat16)
    dreduce_weight = outer_sum(active_low, grad_branch)
    dreduce_bias = jnp.sum(grad_branch.astype(jnp.float32), axis=0)
    grad_before = gelu_pull(back_product(grad_branch, reduce_back))[0].astype(jnp.bfloat16)
    dexpand_weight = outer_sum(second_low, grad_before)
    dexpand_bias = jnp.sum(grad_before.astype(jnp.float32), axis=0)
    grad_normed, dffnorm_gain, dffnorm_shift = second_pull(back_product(grad_before, expand_back))
    grad_hidden = grad_out + grad_normed
    grad_attn = grad_hidden.astype(jnp.bfloat16)
    dmixer_weight = outer_sum(attended_rows, grad_attn)
    dmixer_bias = jnp.sum(grad_attn.astype(jnp.float32), axis=0)
    grad_attended = (
        back_product(grad_attn, mixer_back)
        .astype(jnp.bfloat16)
        .reshape(seq_count, seq_length, H, HD)
    )
    grad_query, grad_keys, grad_values = lax.map(
        attend_backward, (queries, key_block, values, log_total, grad_attended, lengths)
    )
    grad_joint = jnp.stack([grad_query, grad_keys, grad_values], axis=2).reshape(
        row_count, 3 * model_width
    )
    djoint_weight = outer_sum(normed_low, grad_joint)
    joint_sums = jnp.sum(grad_joint.astype(jnp.float32), axis=0)
    djoint_bias = jnp.concatenate([joint_sums[:model_width], joint_sums[2 * model_width :]])
    grad_rows, dnorm_gain, dnorm_shift = first_pull(back_product(grad_joint, joint_back))
    input_grad = (grad_hidden + grad_rows).astype(jnp.bfloat16).reshape(tokens.shape)
    owned_grads = (
        lax.psum_scatter(
            dnorm_gain.astype(jnp.bfloat16), "shard", scatter_dimension=0, tiled=True
        ).astype(jnp.float32),
        lax.psum_scatter(
            dnorm_shift.astype(jnp.bfloat16), "shard", scatter_dimension=0, tiled=True
        ).astype(jnp.float32),
        lax.psum_scatter(
            djoint_weight.astype(jnp.bfloat16), "shard", scatter_dimension=0, tiled=True
        ).astype(jnp.float32),
        lax.psum_scatter(
            djoint_bias.astype(jnp.bfloat16), "shard", scatter_dimension=0, tiled=True
        ).astype(jnp.float32),
        lax.psum_scatter(
            dmixer_weight.astype(jnp.bfloat16), "shard", scatter_dimension=0, tiled=True
        ).astype(jnp.float32),
        lax.psum_scatter(
            dmixer_bias.astype(jnp.bfloat16), "shard", scatter_dimension=0, tiled=True
        ).astype(jnp.float32),
        lax.psum_scatter(
            dffnorm_gain.astype(jnp.bfloat16), "shard", scatter_dimension=0, tiled=True
        ).astype(jnp.float32),
        lax.psum_scatter(
            dffnorm_shift.astype(jnp.bfloat16), "shard", scatter_dimension=0, tiled=True
        ).astype(jnp.float32),
        lax.psum_scatter(
            dexpand_weight.astype(jnp.bfloat16), "shard", scatter_dimension=0, tiled=True
        ).astype(jnp.float32),
        lax.psum_scatter(
            dexpand_bias.astype(jnp.bfloat16), "shard", scatter_dimension=0, tiled=True
        ).astype(jnp.float32),
        lax.psum_scatter(
            dreduce_weight.astype(jnp.bfloat16), "shard", scatter_dimension=0, tiled=True
        ).astype(jnp.float32),
        lax.psum_scatter(
            dreduce_bias.astype(jnp.bfloat16), "shard", scatter_dimension=0, tiled=True
        ).astype(jnp.float32),
    )
    summed = (
        lax.psum(owned_grads[0].astype(jnp.bfloat16), "rep").astype(jnp.float32),
        lax.psum(owned_grads[1].astype(jnp.bfloat16), "rep").astype(jnp.float32),
        lax.psum(owned_grads[2].astype(jnp.bfloat16), "rep").astype(jnp.float32),
        lax.psum(owned_grads[3].astype(jnp.bfloat16), "rep").astype(jnp.float32),
        lax.psum(owned_grads[4].astype(jnp.bfloat16), "rep").astype(jnp.float32),
        lax.psum(owned_grads[5].astype(jnp.bfloat16), "rep").astype(jnp.float32),
        lax.psum(owned_grads[6].astype(jnp.bfloat16), "rep").astype(jnp.float32),
        lax.psum(owned_grads[7].astype(jnp.bfloat16), "rep").astype(jnp.float32),
        lax.psum(owned_grads[8].astype(jnp.bfloat16), "rep").astype(jnp.float32),
        lax.psum(owned_grads[9].astype(jnp.bfloat16), "rep").astype(jnp.float32),
        lax.psum(owned_grads[10].astype(jnp.bfloat16), "rep").astype(jnp.float32),
        lax.psum(owned_grads[11].astype(jnp.bfloat16), "rep").astype(jnp.float32),
    )
    return (
        layer_out,
        input_grad,
        summed[0],
        summed[1],
        summed[2],
        summed[3],
        summed[4],
        summed[5],
        summed[6],
        summed[7],
        summed[8],
        summed[9],
        summed[10],
        summed[11],
    )


def solution(mesh):
    return jax.shard_map(
        on_device,
        mesh=mesh,
        in_specs=(
            P(("rep", "shard"), None, None),
            P(("rep", "shard")),
            P(("rep", "shard"), None, None),
            P("shard"),
            P("shard"),
            P("shard", None),
            P("shard"),
            P("shard", None),
            P("shard"),
            P("shard"),
            P("shard"),
            P("shard", None),
            P("shard"),
            P("shard", None),
            P("shard"),
        ),
        out_specs=(
            P(("rep", "shard"), None, None),
            P(("rep", "shard"), None, None),
            P("shard"),
            P("shard"),
            P("shard", None),
            P("shard"),
            P("shard", None),
            P("shard"),
            P("shard"),
            P("shard"),
            P("shard", None),
            P("shard"),
            P("shard", None),
            P("shard"),
        ),
        check_vma=False,
    )
```

profile of v0, /device:TPU:0, one launch (start us, length us, event | category | flops | bytes accessed | tf_op | source)
XLA Modules:
  0.0 1089.4 jit_solution(13900846472972458376)
XLA Ops:
  15.2 22.5 %all-gather.5 = bf16[8,1,128]{2,1,0:T(2,128)(2,1)S(1)} all-gather(bf16[1,1,128]{2,1,0:T(2,128)(2,1)S(1)} %convert_bitcast_fusion.1), channel_id=1, replica_groups=mesh['rep'=4,'shard'=8] {'shard'}, dimensions={0}, use_global_device_ids=true | all-gather | bytes 2304 | tf_op jit(solution)/shard_map/all_gather | solution.py:103
  37.7 16.5 %all-gather.4 = bf16[8,1,128]{2,1,0:T(2,128)(2,1)S(1)} all-gather(bf16[1,1,128]{2,1,0:T(2,128)(2,1)S(1)} %convert_bitcast_fusion.2), channel_id=1, replica_groups=mesh['rep'=4,'shard'=8] {'shard'}, dimensions={0}, use_global_device_ids=true | all-gather | bytes 2304 | tf_op jit(solution)/shard_map/all_gather | solution.py:102
  54.2 18.3 %all-gather.3 = bf16[8,1,128]{2,1,0:T(2,128)(2,1)S(1)} all-gather(bf16[1,1,128]{2,1,0:T(2,128)(2,1)S(1)} %convert_bitcast_fusion.3), channel_id=1, replica_groups=mesh['rep'=4,'shard'=8] {'shard'}, dimensions={0}, use_global_device_ids=true | all-gather | bytes 2304 | tf_op jit(solution)/shard_map/all_gather | solution.py:101
  72.5 16.7 %all-gather.1 = bf16[8,1,128]{2,1,0:T(2,128)(2,1)S(1)} all-gather(bf16[1,1,128]{2,1,0:T(2,128)(2,1)S(1)} %convert_bitcast_fusion.4), channel_id=1, replica_groups=mesh['rep'=4,'shard'=8] {'shard'}, dimensions={0}, use_global_device_ids=true | all-gather | bytes 2304 | tf_op jit(solution)/shard_map/all_gather | solution.py:97
  89.2 18.0 %all-gather = bf16[8,1,128]{2,1,0:T(2,128)(2,1)S(1)} all-gather(bf16[1,1,128]{2,1,0:T(2,128)(2,1)S(1)} %convert_bitcast_fusion.5), channel_id=1, replica_groups=mesh['rep'=4,'shard'=8] {'shard'}, dimensions={0}, use_global_device_ids=true | all-gather | bytes 2304 | tf_op jit(solution)/shard_map/all_gather | solution.py:96
  108.7 26.1 %all-gather.6 = bf16[8,1,512]{2,1,0:T(2,128)(2,1)S(1)} all-gather(bf16[1,1,512]{2,1,0:T(2,128)(2,1)S(1)} %reshape.242), channel_id=1, replica_groups=mesh['rep'=4,'shard'=8] {'shard'}, dimensions={0}, use_global_device_ids=true | all-gather | bytes 9216 | tf_op jit(solution)/shard_map/all_gather | solution.py:105
  134.8 16.4 %all-gather.2 = bf16[8,1,256]{2,1,0:T(2,128)(2,1)S(1)} all-gather(bf16[1,1,256]{2,1,0:T(2,128)(2,1)S(1)} %reshape.234), channel_id=1, replica_groups=mesh['rep'=4,'shard'=8] {'shard'}, dimensions={0}, use_global_device_ids=true | all-gather | bytes 4608 | tf_op jit(solution)/shard_map/all_gather | solution.py:99
  154.8 8.7 add_convert_fusion
  163.5 6.2 copy.56
  169.7 10.6 reshape.222
  180.4 5.5 slice_bitcast_fusion
  189.3 17.9 %while.26 = (s32[]{:T(128)}, bf16[2,320,16,64]{1,3,2,0:T(8,128)(2,1)}, f32[2,16,320]{2,1,0:T(8,128)S(1)}, bf16[2,320,16,64]{1,3,2,0:T(8,128)(2,1)}, s32[2]{0:T(1...) while((s32[]{:T(128)}, ...), condition=%wide.region_5.6_spmd, body=%wide.region_2.5_spmd.sunk | while | flops 439414080 | bytes 40034116 | solution.py:146
  207.2 4.2 copy.60
  211.4 4.4 reshape.223
  215.9 4.4 fusion.145
  222.2 66.6 %all-gather.17.cloned.1.call-done = bf16[1024,4096]{1,0:T(8,128)(2,1)} async-done(((bf16[128,4096]{1,0:T(8,128)(2,1)}), bf16[1024,4096]{1,0:T(8,128)(2,1)}) %all-gather.17.cloned.1.call-update) | async-done | bytes 8388624 | tf_op jit(solution)/shard_map/all_gather | solution.py:104
  288.8 11.4 %fusion.136 = f32[640,4096]{1,0:T(8,128)} fusion(bf16[1024,4096]{1,0:T(8,128)(2,1)} %all-gather.17.cloned.1.call-done, f32[640,1024]{1,0:T(8,128)} %copy-done.10, f32[1024]{0:T(1024)S(1)} %bitcast.217, f32[1024]{0:T(1024)S(1)} %bitcast.208, f32[640]{0:T(1024)S(1)} %fusion.133, f32[640]{0:T(1024)S(1)} %broadcast_multiply_fusion), kind=kOutput, calls=%fused_computation.156 | convolution fusion | flops 5371985920 | bytes 21509120 | tf_op jit(solution)/shard_map/dot_general | solution.py:157
  300.2 113.7 %all-gather.19.cloned.1.call-done = bf16[4096,1024]{1,0:T(8,128)(2,1)} async-done(((bf16[512,1024]{1,0:T(8,128)(2,1)}), bf16[4096,1024]{1,0:T(8,128)(2,1)}) %all-gather.19.cloned.1.call-update) | async-done | bytes 8388624 | tf_op jit(solution)/shard_map/all_gather | solution.py:106
  413.9 18.6 %fusion.138 = (bf16[4096]{0:T(1024)(128)(2,1)}, bf16[640,4096]{1,0:T(8,128)(2,1)}) fusion(f32[640,4096]{1,0:T(8,128)} %fusion.136, f32[4096]{0:T(1024)S(1)} %bitcast.212, bf16[640,1024]{1,0:T(8,128)(2,1)} %fusion.130, bf16[4096,1024]{1,0:T(8,128)(2,1)} %all-gather.19.cloned.1.call-done), kind=kOutput, calls=%fused_computation.158 | convolution fusion | flops 5426376704 | bytes 25452544 | tf_op jit(solution)/shard_map/dot_general | solution.py:27
  432.6 9.5 multiply_reduce_fusion.1
  445.6 3.1 convolution_convert_fusion.3
  448.7 4.6 convolution_convert_fusion.4
  453.4 4.6 reshape.257
  458.0 4.8 copy.64
  467.1 83.5 %while.27 = (s32[]{:T(128)}, bf16[2,320,16,64]{1,3,2,0:T(8,128)(2,1)}, bf16[2,320,16,64]{1,3,2,0:T(8,128)(2,1)}, bf16[2,320,16,64]{1,3,2,0:T(8,128)(2,1)}, bf16[...) while((s32[]{:T(128)}, ...), condition=%wide.region_12.13_spmd, body=%wide.region_10.12_spmd.sunk | while | flops 1092168704 | bytes 128622624 | solution.py:190
  469.8 3.5 fusion.203
  473.3 4.4 fusion.199
  477.6 15.6 %fusion.202 = bf16[2,320,16,64]{1,3,2,0:T(8,128)(2,1)} fusion(bf16[2,320,16,64]{1,3,2,0:T(8,128)(2,1)} %get-tuple-element.384, s32[]{:T(128)S(6)} %copy.91, f32[16,320,320]{1,2,0:T(8,128)} %fusion.199, f32[16,320,320]{1,2,0:T(8,128)} %copy-done, f32[16,320]{1,0:T(8,128)S(1)} %dynamic-slice_bitcast_fusion.2, ...), kind=kOutput, calls=%fused_computation.44.clone.1 | convolution fusion | flops 228070720 | bytes 33081344 | tf_op jit(solution)/shard_map/while/body/eval_jaxpr/hqk,qhd->khd/dot_general | solution.py:60
  493.2 15.6 %fusion.201 = bf16[2,320,16,64]{1,3,2,0:T(8,128)(2,1)} fusion(bf16[2,320,16,64]{1,3,2,0:T(8,128)(2,1)} %get-tuple-element.383, s32[]{:T(128)S(6)} %copy.91, f32[16,320,320]{1,2,0:T(8,128)} %fusion.199, f32[16,320,320]{1,2,0:T(8,128)} %copy-done, f32[16,320]{1,0:T(8,128)S(1)} %dynamic-slice_bitcast_fusion.2, ...), kind=kOutput, calls=%fused_computation.46.clone.1 | convolution fusion | flops 228070720 | bytes 33081344 | tf_op jit(solution)/shard_map/while/body/eval_jaxpr/hqk,khd->qhd/dot_general | solution.py:59
  511.5 3.5 fusion.203
  515.0 4.4 fusion.199
  519.3 15.6 %fusion.202 = bf16[2,320,16,64]{1,3,2,0:T(8,128)(2,1)} fusion(bf16[2,320,16,64]{1,3,2,0:T(8,128)(2,1)} %get-tuple-element.384, s32[]{:T(128)S(6)} %copy.91, f32[16,320,320]{1,2,0:T(8,128)} %fusion.199, f32[16,320,320]{1,2,0:T(8,128)} %copy-done, f32[16,320]{1,0:T(8,128)S(1)} %dynamic-slice_bitcast_fusion.2, ...), kind=kOutput, calls=%fused_computation.44.clone.1 | convolution fusion | flops 228070720 | bytes 33081344 | tf_op jit(solution)/shard_map/while/body/eval_jaxpr/hqk,qhd->khd/dot_general | solution.py:60
  534.9 15.6 %fusion.201 = bf16[2,320,16,64]{1,3,2,0:T(8,128)(2,1)} fusion(bf16[2,320,16,64]{1,3,2,0:T(8,128)(2,1)} %get-tuple-element.383, s32[]{:T(128)S(6)} %copy.91, f32[16,320,320]{1,2,0:T(8,128)} %fusion.199, f32[16,320,320]{1,2,0:T(8,128)} %copy-done, f32[16,320]{1,0:T(8,128)S(1)} %dynamic-slice_bitcast_fusion.2, ...), kind=kOutput, calls=%fused_computation.46.clone.1 | convolution fusion | flops 228070720 | bytes 33081344 | tf_op jit(solution)/shard_map/while/body/eval_jaxpr/hqk,khd->qhd/dot_general | solution.py:59
  550.5 4.5 fusion.142
  555.0 9.4 copy.66
  564.4 10.1 reshape.227
  574.6 9.2 convolution_convert_fusion.2
  585.1 17.3 %convolution_convert_fusion.1 = bf16[4096,1024]{1,0:T(8,128)(2,1)} fusion(bf16[640,1024]{1,0:T(8,128)(2,1)S(1)} %copy-done.18, f32[640,4096]{1,0:T(8,128)} %fusion.136, f32[4096]{0:T(1024)S(1)} %bitcast.213), kind=kOutput, calls=%fused_computation.92 | convolution fusion | flops 5399117824 | bytes 20201472 | tf_op jit(solution)/shard_map/dot_general | solution.py:21
  604.1 11.7 %convolution_convert_fusion = bf16[1024,4096]{1,0:T(8,128)(2,1)} fusion(bf16[640,4096]{1,0:T(8,128)(2,1)} %get-tuple-element.217, f32[640,1024]{1,0:T(8,128)S(1)} %copy-done.12, f32[1024]{0:T(1024)S(1)} %bitcast.218, f32[1024]{0:T(1024)S(1)} %bitcast.211, f32[640]{0:T(1024)S(1)} %fusion.133, f32[640]{0:T(1024)S(1)} %broadcast_multiply_fusion), kind=kOutput, calls=%fused_computation.91 | convolution fusion | flops 5376180224 | bytes 16266240 | tf_op jit(solution)/shard_map/dot_general | solution.py:21
  619.0 18.1 %all-gather.7 = bf16[8,1,128]{2,1,0:T(2,128)(2,1)S(1)} all-gather(bf16[1,1,128]{2,1,0:T(2,128)(2,1)S(1)} %convert_bitcast_fusion), channel_id=1, replica_groups=mesh['rep'=4,'shard'=8] {'shard'}, dimensions={0}, use_global_device_ids=true | all-gather | bytes 2304 | tf_op jit(solution)/shard_map/all_gather | solution.py:107
  637.7 8.4 fusion.137
  648.9 34.2 %all-reduce.8 = (bf16[1024]{0:T(1024)(128)(2,1)S(1)}, bf16[1024]{0:T(1024)(128)(2,1)S(1)}, bf16[2048]{0:T(1024)(128)(2,1)S(1)}, bf16[1024]{0:T(1024)(128)(2,1)S(...) all-reduce(bf16[1024]{0:T(1024)(128)(2,1)S(1)} %get-tuple-element.1, ...), channel_id=2, replica_groups=mesh['rep'=4,'shard'=8] {'shard'}, use_global_device_ids=true, to_apply=%region_16.17.clone | all-reduce | flops 12288 | bytes 49152
  683.7 6.1 all-reduce.9
  694.1 4.1 add_convert_fusion.1
  699.8 152.7 %reduce-scatter.11.cloned.1.call-done = bf16[512,1024]{1,0:T(8,128)(2,1)} async-done(((bf16[4096,1024]{1,0:T(8,128)(2,1)}), bf16[512,1024]{1,0:T(8,128)(2,1)}) %reduce-scatter.11.cloned.1.call-update) | async-done | bytes 1048592 | tf_op jit(solution)/shard_map/reduce_scatter | solution.py:232
  852.4 152.1 %reduce-scatter.9.cloned.1.call-done = bf16[128,4096]{1,0:T(8,128)(2,1)} async-done(((bf16[1024,4096]{1,0:T(8,128)(2,1)}), bf16[128,4096]{1,0:T(8,128)(2,1)}) %reduce-scatter.9.cloned.1.call-update) | async-done | bytes 1048592 | tf_op jit(solution)/shard_map/reduce_scatter | solution.py:226
  1004.6 12.9 %multiply_convert_fusion.3 = bf16[640,1024]{1,0:T(8,128)(2,1)} fusion(f32[640,1024]{1,0:T(8,128)S(1)} %copy-done.13, bf16[4096,1024]{1,0:T(8,128)(2,1)} %all-gather.19.cloned.1.call-done, f32[640]{0:T(1024)S(1)} %copy-done.29, f32[1024]{0:T(1024)S(1)} %bitcast.219, f32[640,4096]{1,0:T(8,128)} %fusion.136, f32[4096]{0:T(1024)S(1)} %bitcast.214), kind=kOutput, calls=%fused_computation.123 | convolution fusion | flops 5397544960 | bytes 22829568 | tf_op jit(solution)/shard_map/dot_general | solution.py:162
  1017.5 57.7 %all-reduce.13.cloned.1.call-done = (bf16[128,3072]{1,0:T(8,128)(2,1)}, bf16[128,1024]{1,0:T(8,128)(2,1)}, bf16[128,4096]{1,0:T(8,128)(2,1)}, bf16[512,1024]{1,0:T(8,128)(2,1)}) async-done(((bf16[128,3072]{1,0:T(8,128)(2,1)}, bf16[128,1024]{1,0:T(8,128)(2,1)}, bf16[128,4096]{1,0:T(8,128)(2,1)}, bf16[512,1024]{1,0:T(8,128)(2,1)}), (bf16[128,3072]{1,0:T(8,128)(2,1)}, bf16[128,1024]{1,0:T(8,128)(2,1)}, ...) | async-done | bytes 3145744 | tf_op jit(solution)/shard_map/psum | solution.py:242
  (248 shorter events, 70.5 us)
Async XLA Ops:
  7.2 3.5 copy-start.17
  7.2 147.6 %all-gather.13.cloned.1.call-start = ((), (), s32[]{:S(2)}) async-start(), calls=%async_computation.4 | async-start | bytes 7077888 | tf_op jit(solution)/shard_map/all_gather | solution.py:98
  9.8 206.1 %all-gather.15.cloned.1.call-start = ((), (), s32[]{:S(2)}) async-start(), calls=%async_computation.5 | async-start | bytes 2359296 | tf_op jit(solution)/shard_map/all_gather | solution.py:100
  10.6 278.1 %all-gather.17.cloned.1.call-start = ((), (), s32[]{:S(2)}) async-start(), calls=%async_computation.6 | async-start | bytes 9437184 | tf_op jit(solution)/shard_map/all_gather | solution.py:104
  11.9 3.1 copy-start.49
  11.9 3.1 copy-start.46
  11.9 3.1 copy-start.47
  11.9 3.3 copy-start.50
  11.9 25.8 %copy-start.51 = (f32[128]{0:T(128)S(1)}, f32[128]{0:T(128)}, u32[]{:S(2)}) copy-start(f32[128]{0:T(128)} %param.28) | copy-start | bytes 1540
  11.9 42.3 %copy-start.52 = (f32[128]{0:T(128)S(1)}, f32[128]{0:T(128)}, u32[]{:S(2)}) copy-start(f32[128]{0:T(128)} %param.27) | copy-start | bytes 1540
  11.9 60.6 %copy-start.53 = (f32[128]{0:T(128)S(1)}, f32[128]{0:T(128)}, u32[]{:S(2)}) copy-start(f32[128]{0:T(128)} %param.23) | copy-start | bytes 1540
  11.9 77.3 %copy-start.54 = (f32[128]{0:T(128)S(1)}, f32[128]{0:T(128)}, u32[]{:S(2)}) copy-start(f32[128]{0:T(128)} %param.22) | copy-start | bytes 1540
  11.9 95.3 %copy-start.1 = (bf16[2,320,1024]{2,1,0:T(8,128)(2,1)S(1)}, bf16[2,320,1024]{2,1,0:T(8,128)(2,1)}, u32[]{:S(2)}) copy-start(bf16[2,320,1024]{2,1,0:T(8,128)(2,1)} %param.19) | copy-start | bytes 3932164
  12.0 401.9 %all-gather.19.cloned.1.call-start = ((), (), s32[]{:S(2)}) async-start(), calls=%async_computation.7 | async-start | bytes 9437184 | tf_op jit(solution)/shard_map/all_gather | solution.py:106
  14.9 136.4 %copy-start.4 = (bf16[2,320,1024]{2,1,0:T(8,128)(2,1)S(1)}, bf16[2,320,1024]{2,1,0:T(8,128)(2,1)}, u32[]{:S(2)}) copy-start(bf16[2,320,1024]{2,1,0:T(8,128)(2,1)} %param.21) | copy-start | bytes 3932164
  14.9 683.3 %reduce-scatter.7.cloned.1.call-start = ((), (), s32[]{:S(2)}) async-start(), calls=%async_computation.9 | async-start | bytes 2359296 | tf_op jit(solution)/shard_map/reduce_scatter | solution.py:214
  15.1 74.1 %copy-start.38 = (f32[2,320]{1,0:T(2,128)}, f32[2,320]{1,0:T(2,128)S(1)}, u32[]{:S(2)}) copy-start(f32[2,320]{1,0:T(2,128)S(1)} %compare_convert_fusion) | copy-start | bytes 7684
  15.2 137.4 %copy-start.27 = (f32[640]{0:T(1024)}, f32[640]{0:T(1024)S(1)}, u32[]{:S(2)}) copy-start(f32[640]{0:T(1024)S(1)} %reshape.229) | copy-start | bytes 7684
  37.7 251.1 %copy-start.42 = (f32[8,1,128]{2,1,0:T(1,128)}, f32[8,1,128]{2,1,0:T(1,128)S(1)}, u32[]{:S(2)}) copy-start(f32[8,1,128]{2,1,0:T(1,128)S(1)} %convert_element_type.318) | copy-start | bytes 12292
  107.2 47.0 %copy-start.25 = (f32[8,1,128]{2,1,0:T(1,128)}, f32[8,1,128]{2,1,0:T(1,128)S(1)}, u32[]{:S(2)}) copy-start(f32[8,1,128]{2,1,0:T(1,128)S(1)} %convert_element_type.314) | copy-start | bytes 12292
  107.5 46.7 %copy-start.30 = (f32[640]{0:T(1024)}, f32[640]{0:T(1024)S(1)}, u32[]{:S(2)}) copy-start(f32[640]{0:T(1024)S(1)} %div.47) | copy-start | bytes 7684
  108.7 45.5 %copy-start.32 = (f32[640]{0:T(1024)}, f32[640]{0:T(1024)S(1)}, u32[]{:S(2)}) copy-start(f32[640]{0:T(1024)S(1)} %rsqrt.23) | copy-start | bytes 7684
  413.9 18.7 %copy-start.11 = (f32[640,1024]{1,0:T(8,128)S(1)}, f32[640,1024]{1,0:T(8,128)}, u32[]{:S(2)}) copy-start(f32[640,1024]{1,0:T(8,128)} %copy-done.10) | copy-start | bytes 7864324
  413.9 18.7 %copy-start.48 = (bf16[1024,4096]{1,0:T(8,128)(2,1)S(1)}, bf16[1024,4096]{1,0:T(8,128)(2,1)}, u32[]{:S(2)}) copy-start(bf16[1024,4096]{1,0:T(8,128)(2,1)} %all-gather.17.cloned.1.call-done) | copy-start | bytes 25165828
  448.7 251.1 %reduce-scatter.5.cloned.1.call-start = ((), (), s32[]{:S(2)}) async-start(), calls=%async_computation.8 | async-start | bytes 7077888 | tf_op jit(solution)/shard_map/reduce_scatter | solution.py:208
  469.7 3.5 copy-start
  469.7 3.5 copy-start.8
  511.5 3.5 copy-start
  511.5 3.5 copy-start.8
  564.4 10.1 copy-start.19
  583.8 268.7 %reduce-scatter.11.cloned.1.call-start = ((), (), s32[]{:S(2)}) async-start(), calls=%async_computation.11 | async-start | bytes 9437184 | tf_op jit(solution)/shard_map/reduce_scatter | solution.py:232
  602.4 402.2 %reduce-scatter.9.cloned.1.call-start = ((), (), s32[]{:S(2)}) async-start(), calls=%async_computation.10 | async-start | bytes 9437184 | tf_op jit(solution)/shard_map/reduce_scatter | solution.py:226
  615.8 3.2 copy-start.55
  615.8 21.3 %copy-start.6 = (bf16[2,320,1024]{2,1,0:T(8,128)(2,1)S(1)}, bf16[2,320,1024]{2,1,0:T(8,128)(2,1)}, u32[]{:S(2)}) copy-start(bf16[2,320,1024]{2,1,0:T(8,128)(2,1)} %param.21) | copy-start | bytes 3932164
  615.8 21.3 %copy-start.39 = (f32[2,320]{1,0:T(2,128)S(1)}, f32[2,320]{1,0:T(2,128)}, u32[]{:S(2)}) copy-start(f32[2,320]{1,0:T(2,128)} %copy-done.38) | copy-start | bytes 7684
  615.8 21.8 %copy-start.2 = (bf16[2,320,1024]{2,1,0:T(8,128)(2,1)S(1)}, bf16[2,320,1024]{2,1,0:T(8,128)(2,1)}, u32[]{:S(2)}) copy-start(bf16[2,320,1024]{2,1,0:T(8,128)(2,1)} %param.19) | copy-start | bytes 3932164
  615.8 21.8 %copy-start.26 = (f32[8,1,128]{2,1,0:T(1,128)S(1)}, f32[8,1,128]{2,1,0:T(1,128)}, u32[]{:S(2)}) copy-start(f32[8,1,128]{2,1,0:T(1,128)} %copy-done.25) | copy-start | bytes 12292
  615.8 21.8 %copy-start.31 = (f32[640]{0:T(1024)S(1)}, f32[640]{0:T(1024)}, u32[]{:S(2)}) copy-start(f32[640]{0:T(1024)} %copy-done.30) | copy-start | bytes 7684
  615.9 459.3 %all-reduce.13.cloned.1.call-start = ((), (), s32[]{:S(2)}) async-start(), calls=%async_computation.12 | async-start | bytes 6291456 | tf_op jit(solution)/shard_map/psum | solution.py:242
  637.6 8.5 copy-start.37
  637.6 10.0 copy-start.33
  646.0 2.8 copy-start.40
  646.0 2.8 copy-start.41
  646.1 48.0 %copy-start.29 = (f32[640]{0:T(1024)S(1)}, f32[640]{0:T(1024)}, u32[]{:S(2)}) copy-start(f32[640]{0:T(1024)} %copy-done.27) | copy-start | bytes 7684
  646.1 48.0 %copy-start.35 = (f32[640]{0:T(1024)S(1)}, f32[640]{0:T(1024)}, u32[]{:S(2)}) copy-start(f32[640]{0:T(1024)} %copy-done.34) | copy-start | bytes 7684
  698.1 306.5 %copy-start.13 = (f32[640,1024]{1,0:T(8,128)S(1)}, f32[640,1024]{1,0:T(8,128)}, u32[]{:S(2)}) copy-start(f32[640,1024]{1,0:T(8,128)} %copy-done.10) | copy-start | bytes 7864324
  1075.2 4.4 copy-start.23
  1077.1 4.1 copy-start.22
  (24 other events, 38.9 us)
Sparse Core Ops, SparseCore 0:
  10.8 101.9 all-gather.12
  115.5 47.6 all-gather.14
  165.3 123.4 all-gather.16
  290.8 123.1 all-gather.18
  448.8 65.9 reduce-scatter.6
  583.9 115.8 reduce-scatter.4
  703.4 148.9 reduce-scatter.10
  856.5 148.0 reduce-scatter.8
  1007.2 67.9 all-reduce.12
where the time goes:
time: 1090 us
  waiting for transfers between devices  545 us (50%)
  matrix products  209 us (19%)
  blocking collectives  193 us (18%)
  local copies, waits for them, and re-layouts  83.1 us (8%)
  other arithmetic  42 us (4%)
  between operations  16.6 us (2%)
    reduce_scatter x1, waiting for transfers between devices, on_device(): lax.psum_scatter(dreduce_weight.astype(jnp.bfloat16), 'shard', scatter_di...  153 us
    reduce_scatter x1, waiting for transfers between devices, on_device(): lax.psum_scatter(dexpand_weight.astype(jnp.bfloat16), 'shard', scatter_di...  152 us
    all_gather x1, waiting for transfers between devices, on_device(): lax.all_gather(narrow(reduce_weight), 'shard', axis=0, tiled=True)  114 us
    all_gather x1, waiting for transfers between devices, on_device(): lax.all_gather(narrow(expand_weight), 'shard', axis=0, tiled=True)  66.6 us
    psum x1, waiting for transfers between devices, on_device(): lax.psum(owned_grads[2].astype(jnp.bfloat16), 'rep').astype(jnp.float32)  57.7 us
    dot_general x4, matrix products, outer_sum(): lax.dot_general(left_side, right_side, (((0,), (0,)), ((), ())), preferre...  41.3 us
    dot_general x4, matrix products, back_product(): lax.dot_general(cotan, weight, (((1,), (1,)), ((), ())), preferred_elemen...  41.1 us
    unnamed x1, blocking collectives  34.2 us
  transfers between devices with their start and end apart: 9, of which 6 were waited for; matrix products, arithmetic and copies ran while one was open for 26% of the time, Pallas kernels for 0%

commit v1 on v0

--- a/solution.py
+++ b/solution.py
@@ -73,6 +73,42 @@
 
 def narrow(master):
     return master.astype(jnp.bfloat16)
+
+
+def gather_matrix(weight):
+    part_rows = weight.shape[0] // lax.axis_size("rep")
+    part = lax.dynamic_slice_in_dim(weight, lax.axis_index("rep") * part_rows, part_rows, 0)
+    return lax.all_gather(narrow(part), ("shard", "rep"), axis=0, tiled=True)
+
+
+def scatter_matrix(grad):
+    part = lax.psum_scatter(
+        grad.astype(jnp.bfloat16), ("shard", "rep"), scatter_dimension=0, tiled=True
+    )
+    return lax.all_gather(part, "rep", axis=0, tiled=True).astype(jnp.float32)
+
+
+def gather_vectors(vectors):
+    packed = narrow(jnp.concatenate(vectors))
+    every = lax.all_gather(packed, "shard", axis=0, tiled=False)
+    pieces, start = [], 0
+    for vector in vectors:
+        pieces.append(every[:, start : start + vector.shape[0]].reshape(-1))
+        start += vector.shape[0]
+    return pieces
+
+
+def scatter_vectors(grads):
+    shards = lax.axis_size("shard")
+    packed = jnp.concatenate([grad.reshape(shards, -1) for grad in grads], axis=1)
+    total = lax.psum(packed, ("rep", "shard"))
+    own = lax.dynamic_index_in_dim(total, lax.axis_index("shard"), 0, keepdims=False)
+    pieces, start = [], 0
+    for grad in grads:
+        size = grad.shape[0] // shards
+        pieces.append(own[start : start + size])
+        start += size
+    return pieces
 
 
 def on_device(
@@ -92,34 +128,13 @@
     reduce_weight,
     reduce_bias,
 ):
-    gathered = (
-        lax.all_gather(narrow(norm_gain), "shard", axis=0, tiled=True),
-        lax.all_gather(narrow(norm_shift), "shard", axis=0, tiled=True),
-        lax.all_gather(narrow(joint_weight), "shard", axis=0, tiled=True),
-        lax.all_gather(narrow(joint_bias), "shard", axis=0, tiled=True),
-        lax.all_gather(narrow(mixer_weight), "shard", axis=0, tiled=True),
-        lax.all_gather(narrow(mixer_bias), "shard", axis=0, tiled=True),
-        lax.all_gather(narrow(ffnorm_gain), "shard", axis=0, tiled=True),
-        lax.all_gather(narrow(ffnorm_shift), "shard", axis=0, tiled=True),
-        lax.all_gather(narrow(expand_weight), "shard", axis=0, tiled=True),
-        lax.all_gather(narrow(expand_bias), "shard", axis=0, tiled=True),
-        lax.all_gather(narrow(reduce_weight), "shard", axis=0, tiled=True),
-        lax.all_gather(narrow(reduce_bias), "shard", axis=0, tiled=True),
-    )
-    (
-        gain_one,
-        shift_one,
-        joint_matrix,
-        joint_vector,
-        mixer_matrix,
-        mixer_vector,
-        gain_two,
-        shift_two,
-        expand_matrix,
-        expand_vector,
-        reduce_matrix,
-        reduce_vector,
-    ) = gathered
+    gain_one, shift_one, joint_vector, mixer_vector, gain_two, shift_two, expand_vector, reduce_vector = gather_vectors(
+        (norm_gain, norm_shift, joint_bias, mixer_bias, ffnorm_gain, ffnorm_shift, expand_bias, reduce_bias)
+    )
+    joint_matrix = gather_matrix(joint_weight)
+    mixer_matrix = gather_matrix(mixer_weight)
+    expand_matrix = gather_matrix(expand_weight)
+    reduce_matrix = gather_matrix(reduce_weight)
     seq_count, seq_length, model_width = tokens.shape
     row_count = seq_count * seq_length
     flat_rows = tokens.astype(jnp.float32).reshape(row_count, model_width)
@@ -163,13 +178,7 @@
         active_low, reduce_matrix, preferred_element_type=jnp.float32
     ) + reduce_vector.astype(jnp.float32)
     layer_out = ((hidden + branch) * kept_rows).astype(jnp.bfloat16).reshape(tokens.shape)
-    regathered = (
-        lax.all_gather(narrow(joint_weight), "shard", axis=0, tiled=True),
-        lax.all_gather(narrow(mixer_weight), "shard", axis=0, tiled=True),
-        lax.all_gather(narrow(expand_weight), "shard", axis=0, tiled=True),
-        lax.all_gather(narrow(reduce_weight), "shard", axis=0, tiled=True),
-    )
-    joint_back, mixer_back, expand_back, reduce_back = regathered
+    joint_back, mixer_back, expand_back, reduce_back = joint_matrix, mixer_matrix, expand_matrix, reduce_matrix
     grad_out = cotangent.astype(jnp.float32).reshape(row_count, model_width) * kept_rows
     grad_branch = grad_out.astype(jnp.bfloat16)
     dreduce_weight = outer_sum(active_low, grad_branch)
@@ -198,73 +207,28 @@
     djoint_bias = jnp.concatenate([joint_sums[:model_width], joint_sums[2 * model_width :]])
     grad_rows, dnorm_gain, dnorm_shift = first_pull(back_product(grad_joint, joint_back))
     input_grad = (grad_hidden + grad_rows).astype(jnp.bfloat16).reshape(tokens.shape)
-    owned_grads = (
-        lax.psum_scatter(
-            dnorm_gain.astype(jnp.bfloat16), "shard", scatter_dimension=0, tiled=True
-        ).astype(jnp.float32),
-        lax.psum_scatter(
-            dnorm_shift.astype(jnp.bfloat16), "shard", scatter_dimension=0, tiled=True
-        ).astype(jnp.float32),
-        lax.psum_scatter(
-            djoint_weight.astype(jnp.bfloat16), "shard", scatter_dimension=0, tiled=True
-        ).astype(jnp.float32),
-        lax.psum_scatter(
-            djoint_bias.astype(jnp.bfloat16), "shard", scatter_dimension=0, tiled=True
-        ).astype(jnp.float32),
-        lax.psum_scatter(
-            dmixer_weight.astype(jnp.bfloat16), "shard", scatter_dimension=0, tiled=True
-        ).astype(jnp.float32),
-        lax.psum_scatter(
-            dmixer_bias.astype(jnp.bfloat16), "shard", scatter_dimension=0, tiled=True
-        ).astype(jnp.float32),
-        lax.psum_scatter(
-            dffnorm_gain.astype(jnp.bfloat16), "shard", scatter_dimension=0, tiled=True
-        ).astype(jnp.float32),
-        lax.psum_scatter(
-            dffnorm_shift.astype(jnp.bfloat16), "shard", scatter_dimension=0, tiled=True
-        ).astype(jnp.float32),
-        lax.psum_scatter(
-            dexpand_weight.astype(jnp.bfloat16), "shard", scatter_dimension=0, tiled=True
-        ).astype(jnp.float32),
-        lax.psum_scatter(
-            dexpand_bias.astype(jnp.bfloat16), "shard", scatter_dimension=0, tiled=True
-        ).astype(jnp.float32),
-        lax.psum_scatter(
-            dreduce_weight.astype(jnp.bfloat16), "shard", scatter_dimension=0, tiled=True
-        ).astype(jnp.float32),
-        lax.psum_scatter(
-            dreduce_bias.astype(jnp.bfloat16), "shard", scatter_dimension=0, tiled=True
-        ).astype(jnp.float32),
-    )
-    summed = (
-        lax.psum(owned_grads[0].astype(jnp.bfloat16), "rep").astype(jnp.float32),
-        lax.psum(owned_grads[1].astype(jnp.bfloat16), "rep").astype(jnp.float32),
-        lax.psum(owned_grads[2].astype(jnp.bfloat16), "rep").astype(jnp.float32),
-        lax.psum(owned_grads[3].astype(jnp.bfloat16), "rep").astype(jnp.float32),
-        lax.psum(owned_grads[4].astype(jnp.bfloat16), "rep").astype(jnp.float32),
-        lax.psum(owned_grads[5].astype(jnp.bfloat16), "rep").astype(jnp.float32),
-        lax.psum(owned_grads[6].astype(jnp.bfloat16), "rep").astype(jnp.float32),
-        lax.psum(owned_grads[7].astype(jnp.bfloat16), "rep").astype(jnp.float32),
-        lax.psum(owned_grads[8].astype(jnp.bfloat16), "rep").astype(jnp.float32),
-        lax.psum(owned_grads[9].astype(jnp.bfloat16), "rep").astype(jnp.float32),
-        lax.psum(owned_grads[10].astype(jnp.bfloat16), "rep").astype(jnp.float32),
-        lax.psum(owned_grads[11].astype(jnp.bfloat16), "rep").astype(jnp.float32),
-    )
+    vectors = scatter_vectors(
+        (dnorm_gain, dnorm_shift, djoint_bias, dmixer_bias, dffnorm_gain, dffnorm_shift, dexpand_bias, dreduce_bias)
+    )
+    dreduce = scatter_matrix(dreduce_weight)
+    dexpand = scatter_matrix(dexpand_weight)
+    dmixer = scatter_matrix(dmixer_weight)
+    djoint = scatter_matrix(djoint_weight)
     return (
         layer_out,
         input_grad,
-        summed[0],
-        summed[1],
-        summed[2],
-        summed[3],
-        summed[4],
-        summed[5],
-        summed[6],
-        summed[7],
-        summed[8],
-        summed[9],
-        summed[10],
-        summed[11],
+        vectors[0],
+        vectors[1],
+        djoint,
+        vectors[2],
+        dmixer,
+        vectors[3],
+        vectors[4],
+        vectors[5],
+        dexpand,
+        vectors[6],
+        dreduce,
+        vectors[7],
     )
 
 

time: 1090 us -> 926 us (0.85)
  blocking collectives: 193 us -> 84.7 us
  waiting for transfers between devices: 545 us -> 488 us
    all_gather x8 -> x3, blocking collectives: 152 us -> 47.2 us  [the longest x1 32.4 us: gather_vectors(): every = lax.all_gather(packed, 'shard', axis=0, tiled=False)]
    psum x1 -> x0, waiting for transfers between devices: 57.7 us -> none  [on_device(): lax.psum(owned_grads[2].astype(jnp.bfloat16), 'rep').astype(jnp.float32)]
    unnamed x1 -> x0, blocking collectives: 34.2 us -> none
    psum x1, blocking collectives: 6.13 us -> 37.5 us  [scatter_vectors(): total = lax.psum(packed, ('rep', 'shard'))]
    convert_element_type x25 -> x4, other arithmetic: 19.1 us -> 7.69 us  [scatter_matrix(): return lax.all_gather(part, 'rep', axis=0, tiled=True).astype(jnp.float32)]
    all_gather x4 -> x6, waiting for transfers between devices: 180 us -> 189 us  [the longest x4 166 us: gather_matrix(): return lax.all_gather(narrow(part), ('shard', 'rep'), axis=0, tiled=True)]
  transfers between devices with their start and end apart: 9 -> 10, of which waited for: 6 -> 8; matrix products, arithmetic and copies ran while one was open for 26% -> 31% of each run, Pallas kernels for 0% -> 0%
where the time goes in v1:
time: 926 us; the launch traced here: 922 us
  waiting for transfers between devices  488 us (53%)
  matrix products  209 us (23%)
  local copies, waits for them, and re-layouts  91.4 us (10%)
  blocking collectives  84.7 us (9%)
  other arithmetic  32.6 us (4%)
  between operations  15.1 us (2%)
    reduce_scatter x4, waiting for transfers between devices, scatter_matrix(): lax.psum_scatter(grad.astype(jnp.bfloat16), ('shard', 'rep'), scatter_dim...  299 us
    all_gather x4, waiting for transfers between devices, gather_matrix(): return lax.all_gather(narrow(part), ('shard', 'rep'), axis=0, tiled=True)  166 us
    dot_general x4, matrix products, back_product(): lax.dot_general(cotan, weight, (((1,), (1,)), ((), ())), preferred_elemen...  38.2 us
    dot_general x4, matrix products, outer_sum(): lax.dot_general(left_side, right_side, (((0,), (0,)), ((), ())), preferre...  37.6 us
    psum x1, blocking collectives, scatter_vectors(): total = lax.psum(packed, ('rep', 'shard'))  37.5 us
    all_gather x1, blocking collectives, gather_vectors(): every = lax.all_gather(packed, 'shard', axis=0, tiled=False)  32.4 us
    dot_general x2, matrix products, attend_backward(): jnp.einsum('hqk,qhd->khd', grad_raw, queries, preferred_element_type=jnp....  32.2 us
    dot_general x2, matrix products, attend_backward(): jnp.einsum('hqk,khd->qhd', grad_raw, key_block, preferred_element_type=jn...  31.6 us
  transfers between devices with their start and end apart: 10, of which 8 were waited for; matrix products, arithmetic and copies ran while one was open for 31% of the time, Pallas kernels for 0%

profile of v1, /device:TPU:0, one launch (start us, length us, event | category | flops | bytes accessed | tf_op | source)
XLA Modules:
  0.0 921.7 jit_solution(8985787234171400653)
XLA Ops:
  17.3 32.4 %all-gather = bf16[8,1,1536]{2,1,0:T(2,128)(2,1)S(1)} all-gather(bf16[1,1,1536]{2,1,0:T(2,128)(2,1)S(1)} %bitcast.268), channel_id=1, replica_groups=mesh['rep'=4,'shard'=8] {'shard'}, dimensions={0}, use_global_device_ids=true | all-gather | bytes 27648 | tf_op jit(solution)/shard_map/all_gather | solution.py:93
  52.4 31.4 %all-gather.8.cloned.1.call-done = bf16[1024,3072]{1,0:T(8,128)(2,1)} async-done(((bf16[32,3072]{1,0:T(8,128)(2,1)}), bf16[1024,3072]{1,0:T(8,128)(2,1)}) %all-gather.8.cloned.1.call-update) | async-done | bytes 6291472 | tf_op jit(solution)/shard_map/all_gather | solution.py:81
  83.8 9.0 add_convert_fusion
  92.8 6.1 copy.56
  98.9 10.6 %reshape.433 = bf16[2,320,3,16,64]{1,0,4,3,2:T(2,128)(2,1)} reshape(bf16[640,3072]{0,1:T(8,128)(2,1)} %copy.56) | data formatting | bytes 7864320 | tf_op jit(solution)/shard_map/reshape | solution.py:157
  109.5 5.4 slice_bitcast_fusion
  119.6 20.0 %while.26 = (s32[]{:T(128)}, bf16[2,320,16,64]{1,3,2,0:T(8,128)(2,1)}, f32[2,16,320]{2,1,0:T(8,128)S(1)}, bf16[2,320,16,64]{1,3,2,0:T(8,128)(2,1)}, s32[2]{0:T(1...) while((s32[]{:T(128)}, ...), condition=%wide.region_5.6_spmd, body=%wide.region_2.5_spmd.sunk | while | flops 439414080 | bytes 40034116 | solution.py:161
  120.8 3.3 fusion.189
  130.7 3.3 fusion.189
  139.6 4.2 copy.60
  143.8 4.4 reshape.434
  148.2 3.7 fusion.148
  153.9 66.9 %all-gather.12.cloned.1.call-done = bf16[1024,4096]{1,0:T(8,128)(2,1)} async-done(((bf16[32,4096]{1,0:T(8,128)(2,1)}), bf16[1024,4096]{1,0:T(8,128)(2,1)}) %all-gather.12.cloned.1.call-update) | async-done | bytes 8388624 | tf_op jit(solution)/shard_map/all_gather | solution.py:81
  220.8 11.4 %fusion.142 = f32[640,4096]{1,0:T(8,128)} fusion(bf16[1024,4096]{1,0:T(8,128)(2,1)} %all-gather.12.cloned.1.call-done, f32[640,1024]{1,0:T(8,128)} %copy-done.11, f32[1024]{0:T(1024)S(1)} %get-tuple-element.219, f32[1024]{0:T(1024)S(1)} %get-tuple-element.217, f32[640]{0:T(1024)S(1)} %fusion.132, f32[640]{0:T(1024)S(1)} %broadcast_multiply_fusion), kind=kOutput, calls=%fused_computation.193 | convolution fusion | flops 5371985920 | bytes 21509120 | tf_op jit(solution)/shard_map/dot_general | solution.py:172
  232.2 68.0 %all-gather.14.cloned.1.call-done = bf16[4096,1024]{1,0:T(8,128)(2,1)} async-done(((bf16[128,1024]{1,0:T(8,128)(2,1)}), bf16[4096,1024]{1,0:T(8,128)(2,1)}) %all-gather.14.cloned.1.call-update) | async-done | bytes 8388624 | tf_op jit(solution)/shard_map/all_gather | solution.py:81
  300.1 17.0 %convert_reduce_fusion = (f32[4096]{0:T(1024)}, bf16[640,4096]{1,0:T(8,128)(2,1)S(1)}) fusion(f32[640,4096]{1,0:T(8,128)} %fusion.142, f32[4096]{0:T(1024)S(1)} %bitcast.263, bf16[640,1024]{1,0:T(8,128)(2,1)} %fusion.130, bf16[4096,1024]{1,0:T(8,128)(2,1)} %all-gather.14.cloned.1.call-done), kind=kOutput, calls=%fused_computation.89 | convolution fusion | flops 5428998144 | bytes 25460736 | tf_op jit(solution)/shard_map/dot_general | solution.py:27
  319.4 9.6 %convolution_convert_fusion = bf16[1024,4096]{1,0:T(8,128)(2,1)} fusion(bf16[640,4096]{1,0:T(8,128)(2,1)S(1)} %get-tuple-element.197, f32[640,1024]{1,0:T(8,128)S(1)} %copy-done.12, f32[1024]{0:T(1024)S(1)} %get-tuple-element.219, f32[1024]{0:T(1024)S(1)} %get-tuple-element.217, f32[640]{0:T(1024)S(1)} %fusion.132, f32[640]{0:T(1024)S(1)} %broadcast_multiply_fusion), kind=kOutput, calls=%fused_computation.93 | convolution fusion | flops 5376180224 | bytes 16266240 | tf_op jit(solution)/shard_map/dot_general | solution.py:21
  329.1 14.0 %convolution_convert_fusion.1 = bf16[4096,1024]{1,0:T(8,128)(2,1)} fusion(bf16[640,1024]{1,0:T(8,128)(2,1)} %fusion.130, f32[640,4096]{1,0:T(8,128)} %fusion.142, f32[4096]{0:T(1024)S(1)} %bitcast.264), kind=kOutput, calls=%fused_computation.94 | convolution fusion | flops 5399117824 | bytes 20201472 | tf_op jit(solution)/shard_map/dot_general | solution.py:21
  345.4 10.2 %multiply_reduce_fusion.1 = (f32[1024]{0:T(1024)S(1)}, f32[640]{0:T(1024)S(1)}, f32[1024]{0:T(1024)S(1)}, f32[640,1024]{1,0:T(8,128)S(1)}) fusion(f32[640,1024]{1,0:T(8,128)S(1)} %copy-done.13, f32[640]{0:T(1024)S(1)} %fusion.132, f32[640]{0:T(1024)S(1)} %broadcast_multiply_fusion, f32[1024]{0:T(1024)S(1)} %get-tuple-element.217, ...), kind=kOutput, calls=%fused_computation.122 | convolution fusion | flops 5373949440 | bytes 18894336 | tf_op jit(solution)/shard_map/dot_general | solution.py:27
  361.8 4.4 reshape.459
  366.2 4.8 copy.64
  371.0 4.8 convolution_convert_fusion.3
  380.1 87.3 %while.27 = (s32[]{:T(128)}, bf16[2,320,16,64]{1,3,2,0:T(8,128)(2,1)}, bf16[2,320,16,64]{1,3,2,0:T(8,128)(2,1)}, bf16[2,320,16,64]{1,3,2,0:T(8,128)(2,1)}, bf16[...) while((s32[]{:T(128)}, ...), condition=%wide.region_12.13_spmd, body=%wide.region_10.12_spmd.sunk | while | flops 1092168704 | bytes 128622624 | solution.py:199
  384.1 3.4 fusion.206
  387.6 4.4 fusion.202
  392.0 16.1 %fusion.205 = bf16[2,320,16,64]{1,3,2,0:T(8,128)(2,1)} fusion(bf16[2,320,16,64]{1,3,2,0:T(8,128)(2,1)} %get-tuple-element.376, s32[]{:T(128)S(6)} %copy.104, f32[16,320,320]{1,2,0:T(8,128)} %fusion.202, f32[16,320,320]{1,2,0:T(8,128)} %copy-done.2, f32[16,320]{1,0:T(8,128)S(1)} %dynamic-slice_bitcast_fusion.7, ...), kind=kOutput, calls=%fused_computation.44.clone.1 | convolution fusion | flops 228070720 | bytes 33081344 | tf_op jit(solution)/shard_map/while/body/eval_jaxpr/hqk,qhd->khd/dot_general | solution.py:60
  408.1 15.8 %fusion.204 = bf16[2,320,16,64]{1,3,2,0:T(8,128)(2,1)} fusion(bf16[2,320,16,64]{1,3,2,0:T(8,128)(2,1)} %get-tuple-element.375, s32[]{:T(128)S(6)} %copy.104, f32[16,320,320]{1,2,0:T(8,128)} %fusion.202, f32[16,320,320]{1,2,0:T(8,128)} %copy-done.2, f32[16,320]{1,0:T(8,128)S(1)} %dynamic-slice_bitcast_fusion.7, ...), kind=kOutput, calls=%fused_computation.46.clone.1 | convolution fusion | flops 228070720 | bytes 33081344 | tf_op jit(solution)/shard_map/while/body/eval_jaxpr/hqk,khd->qhd/dot_general | solution.py:59
  427.7 3.4 fusion.206
  431.1 4.4 fusion.202
  435.5 16.1 %fusion.205 = bf16[2,320,16,64]{1,3,2,0:T(8,128)(2,1)} fusion(bf16[2,320,16,64]{1,3,2,0:T(8,128)(2,1)} %get-tuple-element.376, s32[]{:T(128)S(6)} %copy.104, f32[16,320,320]{1,2,0:T(8,128)} %fusion.202, f32[16,320,320]{1,2,0:T(8,128)} %copy-done.2, f32[16,320]{1,0:T(8,128)S(1)} %dynamic-slice_bitcast_fusion.7, ...), kind=kOutput, calls=%fused_computation.44.clone.1 | convolution fusion | flops 228070720 | bytes 33081344 | tf_op jit(solution)/shard_map/while/body/eval_jaxpr/hqk,qhd->khd/dot_general | solution.py:60
  451.6 15.8 %fusion.204 = bf16[2,320,16,64]{1,3,2,0:T(8,128)(2,1)} fusion(bf16[2,320,16,64]{1,3,2,0:T(8,128)(2,1)} %get-tuple-element.375, s32[]{:T(128)S(6)} %copy.104, f32[16,320,320]{1,2,0:T(8,128)} %fusion.202, f32[16,320,320]{1,2,0:T(8,128)} %copy-done.2, f32[16,320]{1,0:T(8,128)S(1)} %dynamic-slice_bitcast_fusion.7, ...), kind=kOutput, calls=%fused_computation.46.clone.1 | convolution fusion | flops 228070720 | bytes 33081344 | tf_op jit(solution)/shard_map/while/body/eval_jaxpr/hqk,khd->qhd/dot_general | solution.py:59
  467.4 4.5 convert_reduce_fusion.1
  471.9 9.3 %copy.66 = bf16[2,320,3,16,64]{1,0,4,3,2:T(2,128)(2,1)} copy(bf16[2,320,3,16,64]{1,4,3,0,2:T(8,128)(2,1)} %get-tuple-element.201) | data formatting | bytes 7864320 | tf_op jit(solution)/shard_map/stack | solution.py:202
  481.3 10.2 %reshape.438 = bf16[640,3072]{0,1:T(8,128)(2,1)} reshape(bf16[2,320,3,16,64]{1,0,4,3,2:T(2,128)(2,1)} %copy.66) | data formatting | bytes 7864320 | tf_op jit(solution)/shard_map/reshape | solution.py:202
  491.4 9.2 convolution_convert_fusion.2
  502.4 8.3 fusion.143
  513.7 13.5 %multiply_convert_fusion.3 = bf16[640,1024]{1,0:T(8,128)(2,1)} fusion(f32[640,1024]{1,0:T(8,128)} %copy-done.11, bf16[4096,1024]{1,0:T(8,128)(2,1)} %all-gather.14.cloned.1.call-done, f32[640]{0:T(1024)S(1)} %copy-done.24, f32[1024]{0:T(1024)S(1)} %copy-done.41, f32[640,4096]{1,0:T(8,128)} %fusion.142, f32[4096]{0:T(1024)S(1)} %bitcast.265), kind=kOutput, calls=%fused_computation.127 | convolution fusion | flops 5397544960 | bytes 22829568 | tf_op jit(solution)/shard_map/dot_general | solution.py:177
  527.2 96.4 %reduce-scatter.11.cloned.1.call-done = bf16[128,1024]{1,0:T(8,128)(2,1)} async-done(((bf16[4096,1024]{1,0:T(8,128)(2,1)}), bf16[128,1024]{1,0:T(8,128)(2,1)}) %reduce-scatter.11.cloned.1.call-update) | async-done | bytes 262160 | tf_op jit(solution)/shard_map/reduce_scatter | solution.py:85
  623.7 37.5 %psum.7 = f32[8,1536]{1,0:T(8,128)S(1)} all-reduce(f32[8,1536]{1,0:T(8,128)S(1)} %constant_dynamic-update-slice_fusion.8), channel_id=1, replica_groups=mesh['rep'=4,'shard'=8] {'rep','shard'}, use_global_device_ids=true, to_apply=%region_23.24 | all-reduce | flops 12288 | bytes 98304 | tf_op jit(solution)/shard_map/psum | solution.py:104
  663.1 4.0 add_convert_fusion.1
  667.1 92.1 %reduce-scatter.7.cloned.1.call-done = bf16[32,1024]{1,0:T(8,128)(2,1)} async-done(((bf16[1024,1024]{1,0:T(8,128)(2,1)}), bf16[32,1024]{1,0:T(8,128)(2,1)}) %reduce-scatter.7.cloned.1.call-update) | async-done | bytes 65552 | tf_op jit(solution)/shard_map/reduce_scatter | solution.py:85
  759.2 6.0 all_gather.34
  766.0 110.0 %reduce-scatter.5.cloned.1.call-done = bf16[32,3072]{1,0:T(8,128)(2,1)} async-done(((bf16[1024,3072]{1,0:T(8,128)(2,1)}), bf16[32,3072]{1,0:T(8,128)(2,1)}) %reduce-scatter.5.cloned.1.call-update) | async-done | bytes 196624 | tf_op jit(solution)/shard_map/reduce_scatter | solution.py:85
  876.0 8.8 all_gather.33
  886.1 7.6 all-gather.16.cloned.1.call-done
  893.6 2.8 convert_element_type.280
  896.4 15.4 %all-gather.18.cloned.1.call-done = bf16[512,1024]{1,0:T(8,128)(2,1)} async-done(((bf16[128,1024]{1,0:T(8,128)(2,1)}), bf16[512,1024]{1,0:T(8,128)(2,1)}) %all-gather.18.cloned.1.call-update) | async-done | bytes 1048592 | tf_op jit(solution)/shard_map/all_gather | solution.py:88
  911.8 2.8 convert_element_type.282
  (226 shorter events, 63.4 us)
Async XLA Ops:
  7.2 3.7 copy-start
  7.2 7.8 copy-start.3
  7.2 8.2 copy-start.42
  7.2 9.5 %copy-start.44 = (f32[128]{0:T(128)S(1)}, f32[128]{0:T(128)}, u32[]{:S(2)}) copy-start(f32[128]{0:T(128)} %param.22) | copy-start | bytes 1540
  7.2 9.5 %copy-start.45 = (f32[128]{0:T(128)S(1)}, f32[128]{0:T(128)}, u32[]{:S(2)}) copy-start(f32[128]{0:T(128)} %param.23) | copy-start | bytes 1540
  7.2 9.5 %copy-start.46 = (f32[128]{0:T(128)S(1)}, f32[128]{0:T(128)}, u32[]{:S(2)}) copy-start(f32[128]{0:T(128)} %param.27) | copy-start | bytes 1540
  7.2 9.5 %copy-start.47 = (f32[128]{0:T(128)S(1)}, f32[128]{0:T(128)}, u32[]{:S(2)}) copy-start(f32[128]{0:T(128)} %param.28) | copy-start | bytes 1540
  7.3 9.6 %copy-start.48 = (f32[128]{0:T(128)S(1)}, f32[128]{0:T(128)}, u32[]{:S(2)}) copy-start(f32[128]{0:T(128)} %param.29) | copy-start | bytes 1540
  7.3 9.6 %copy-start.49 = (f32[128]{0:T(128)S(1)}, f32[128]{0:T(128)}, u32[]{:S(2)}) copy-start(f32[128]{0:T(128)} %param.33) | copy-start | bytes 1540
  7.3 76.5 %all-gather.8.cloned.1.call-start = ((), (), s32[]{:S(2)}) async-start(), calls=%async_computation.4 | async-start | bytes 6488064 | tf_op jit(solution)/shard_map/all_gather | solution.py:81
  9.2 139.0 %all-gather.10.cloned.1.call-start = ((), (), s32[]{:S(2)}) async-start(), calls=%async_computation.5 | async-start | bytes 2162688 | tf_op jit(solution)/shard_map/all_gather | solution.py:81
  10.8 210.0 %all-gather.12.cloned.1.call-start = ((), (), s32[]{:S(2)}) async-start(), calls=%async_computation.6 | async-start | bytes 8650752 | tf_op jit(solution)/shard_map/all_gather | solution.py:81
  11.6 38.8 %copy-start.5 = (bf16[2,320,1024]{2,1,0:T(8,128)(2,1)S(1)}, bf16[2,320,1024]{2,1,0:T(8,128)(2,1)}, u32[]{:S(2)}) copy-start(bf16[2,320,1024]{2,1,0:T(8,128)(2,1)} %param.21) | copy-start | bytes 3932164
  11.6 288.5 %all-gather.14.cloned.1.call-start = ((), (), s32[]{:S(2)}) async-start(), calls=%async_computation.7 | async-start | bytes 8650752 | tf_op jit(solution)/shard_map/all_gather | solution.py:81
  13.6 500.0 %reduce-scatter.9.cloned.1.call-start = ((), (), s32[]{:S(2)}) async-start(), calls=%async_computation.10 | async-start | bytes 8650752 | tf_op jit(solution)/shard_map/reduce_scatter | solution.py:85
  15.4 36.9 %copy-start.21 = (f32[640]{0:T(1024)}, f32[640]{0:T(1024)S(1)}, u32[]{:S(2)}) copy-start(f32[640]{0:T(1024)S(1)} %div.47) | copy-start | bytes 7684
  15.5 36.8 %copy-start.23 = (f32[640]{0:T(1024)}, f32[640]{0:T(1024)S(1)}, u32[]{:S(2)}) copy-start(f32[640]{0:T(1024)S(1)} %reshape.456) | copy-start | bytes 7684
  16.7 35.6 %copy-start.25 = (f32[640]{0:T(1024)}, f32[640]{0:T(1024)S(1)}, u32[]{:S(2)}) copy-start(f32[640]{0:T(1024)S(1)} %rsqrt.23) | copy-start | bytes 7684
  49.8 279.3 %copy-start.37 = (f32[1,4,8,128]{3,1,2,0:T(4,128)}, f32[1,4,8,128]{3,1,2,0:T(4,128)S(1)}, u32[]{:S(2)}) copy-start(f32[1,4,8,128]{3,1,2,0:T(4,128)S(1)} %copy.76) | copy-start | bytes 49156
  50.4 1.9 copy-start.19
  50.4 1.9 copy-start.31
  124.1 1.8 copy-start.8
  124.1 1.9 copy-start.15
  134.1 1.8 copy-start.8
  134.1 1.9 copy-start.15
  300.1 19.3 %copy-start.12 = (f32[640,1024]{1,0:T(8,128)S(1)}, f32[640,1024]{1,0:T(8,128)}, u32[]{:S(2)}) copy-start(f32[640,1024]{1,0:T(8,128)} %copy-done.11) | copy-start | bytes 7864324
  317.1 2.3 copy-start.50
  329.0 294.6 %reduce-scatter.11.cloned.1.call-start = ((), (), s32[]{:S(2)}) async-start(), calls=%async_computation.12 | async-start | bytes 8650752 | tf_op jit(solution)/shard_map/reduce_scatter | solution.py:85
  343.1 416.1 %reduce-scatter.7.cloned.1.call-start = ((), (), s32[]{:S(2)}) async-start(), calls=%async_computation.9 | async-start | bytes 2162688 | tf_op jit(solution)/shard_map/reduce_scatter | solution.py:85
  343.2 2.2 copy-start.13
  357.0 2.2 copy-start.43
  375.9 500.2 %reduce-scatter.5.cloned.1.call-start = ((), (), s32[]{:S(2)}) async-start(), calls=%async_computation.8 | async-start | bytes 6488064 | tf_op jit(solution)/shard_map/reduce_scatter | solution.py:85
  381.5 2.5 copy-start.10
  384.1 3.5 copy-start.2
  384.1 3.5 copy-start.9
  425.1 2.5 copy-start.10
  427.6 3.5 copy-start.2
  427.6 3.5 copy-start.9
  481.3 10.2 %copy-start.17 = (bf16[2,320,1024]{2,1,0:T(8,128)(2,1)S(1)}, bf16[2,320,1024]{2,1,0:T(8,128)(2,1)}, u32[]{:S(2)}) copy-start(bf16[2,320,1024]{2,1,0:T(8,128)(2,1)} %fusion.127) | copy-start | bytes 3932164
  500.6 1.8 copy-start.22
  500.6 393.0 %all-gather.16.cloned.1.call-start = ((), (), s32[]{:S(2)}) async-start(), calls=%async_computation.11 | async-start | bytes 1310720 | tf_op jit(solution)/shard_map/all_gather | solution.py:88
  502.4 8.4 copy-start.34
  502.4 9.8 %copy-start.26 = (f32[640]{0:T(1024)S(1)}, f32[640]{0:T(1024)}, u32[]{:S(2)}) copy-start(f32[640]{0:T(1024)} %copy-done.25) | copy-start | bytes 7684
  510.8 2.9 copy-start.38
  510.8 2.9 copy-start.41
  513.6 398.2 %all-gather.18.cloned.1.call-start = ((), (), s32[]{:S(2)}) async-start(), calls=%async_computation.13 | async-start | bytes 1310720 | tf_op jit(solution)/shard_map/all_gather | solution.py:88
  513.7 149.4 %copy-start.30 = (f32[640]{0:T(1024)S(1)}, f32[640]{0:T(1024)}, u32[]{:S(2)}) copy-start(f32[640]{0:T(1024)} %copy-done.29) | copy-start | bytes 7684
  884.8 29.8 %copy-start.1 = (f32[128,4096]{1,0:T(8,128)S(1)}, f32[128,4096]{1,0:T(8,128)}, u32[]{:S(2)}) copy-start(f32[128,4096]{1,0:T(8,128)} %param.30) | copy-start | bytes 6291460
  (19 other events, 22.3 us)
Sparse Core Ops, SparseCore 0:
  11.6 72.1 all-gather.7
  86.7 54.8 all-gather.9
  144.4 76.2 all-gather.11
  224.1 76.0 all-gather.13
  329.2 147.7 reduce-scatter.8
  479.1 144.4 reduce-scatter.10
  626.5 132.6 reduce-scatter.6
  765.8 110.1 reduce-scatter.4
  877.6 15.9 all-gather.15
  895.0 16.7 all-gather.17

commit v2 on v1

v2 whole, which is shorter than its diff:
```python
import functools

import jax
import jax.numpy as jnp
from jax import lax
from jax.experimental import pallas as pl
from jax.experimental.pallas import tpu as pltpu
from jax.sharding import Mesh
from jax.sharding import PartitionSpec as P

HD = 64
EPSILON = 1e-06
KEEP_MIN = 192
BF = jnp.bfloat16
F32 = jnp.float32
ALL = ("x", "core", "shard")
ANY = pl.BlockSpec(memory_space=pl.ANY)


def nn(a, b):
    return lax.dot_general(a, b, (((1,), (0,)), ((), ())), preferred_element_type=F32)


def nt(a, b):
    return lax.dot_general(a, b, (((1,), (1,)), ((), ())), preferred_element_type=F32)


def tn(a, b):
    return lax.dot_general(a, b, (((0,), (0,)), ((), ())), preferred_element_type=F32)


def whole(array, buffered=False):
    rank = len(array.shape)
    return pl.BlockSpec(tuple(array.shape), lambda *_: (0,) * rank)


def shape_of(shape, dtype):
    return jax.ShapeDtypeStruct(shape, dtype)


def params(mib=56, steps=1):
    return pltpu.CompilerParams(
        vmem_limit_bytes=mib * 2**20, dimension_semantics=("arbitrary",) * steps
    )


def cost(flops, moved, exps=0):
    return pl.CostEstimate(flops=int(flops), bytes_accessed=int(moved), transcendentals=int(exps))


def load_pieces(table, pieces, target, sem, first, last):
    slot = 0
    for piece in pieces:
        rows = piece.shape[1]
        for index in range(piece.shape[0]):
            start = pl.multiple_of(table[slot], 32)
            pltpu.make_async_copy(
                piece.at[index, :, first:last], target.at[pl.ds(start, rows)], sem
            ).start()
            slot += 1


def wait_all(target, sem):
    pltpu.make_async_copy(target, target, sem).wait()


def store_pieces(table, source, pieces, sem, first_slot=0):
    slot = first_slot
    for piece in pieces:
        rows = piece.shape[1]
        for index in range(piece.shape[0]):
            start = pl.multiple_of(table[slot], 32)
            pltpu.make_async_copy(
                source.at[pl.ds(start, rows)], piece.at[index], sem
            ).start()
            slot += 1


def joint_kernel(table, tokens, gain, shift, bias, *rest):
    pieces = rest[:-6]
    normed_ref, joint_ref, mixer_ref, weight, sem, mixer_sem = rest[-6:]
    width = weight.shape[1]
    step = pl.program_id(0)

    @pl.when(step == 0)
    def _():
        load_pieces(table, pieces, weight, sem, 0, width)
        load_pieces(table, pieces, mixer_ref, mixer_sem, width, pieces[0].shape[2])

    value = tokens[...].astype(F32)
    centred = value - jnp.mean(value, axis=-1, keepdims=True)
    spread = jnp.mean(centred * centred, axis=-1, keepdims=True)
    normed = (centred * lax.rsqrt(spread + EPSILON) * gain[...] + shift[...]).astype(BF)
    normed_ref[...] = normed

    @pl.when(step == 0)
    def _():
        wait_all(weight, sem)
        wait_all(mixer_ref, mixer_sem)

    joint_ref[...] = (nn(normed, weight[...]) + bias[...]).astype(BF)


def joint_call(table, tokens, gain, shift, bias, pieces, length):
    rows, width = tokens.shape
    columns = bias.shape[1]
    mixer_columns = pieces[0].shape[2] - columns
    row = lambda i, *_: (i, 0)
    return pl.pallas_call(
        joint_kernel,
        grid_spec=pltpu.PrefetchScalarGridSpec(
            num_scalar_prefetch=1,
            grid=(rows // length,),
            in_specs=[
                pl.BlockSpec((length, width), row),
                whole(gain),
                whole(shift),
                whole(bias),
            ]
            + [ANY] * len(pieces),
            out_specs=[
                pl.BlockSpec((length, width), row),
                pl.BlockSpec((length, columns), row),
                pl.BlockSpec((width, mixer_columns), lambda *_: (0, 0)),
            ],
            scratch_shapes=[
                pltpu.VMEM((width, columns), BF),
                pltpu.SemaphoreType.DMA,
                pltpu.SemaphoreType.DMA,
            ],
        ),
        out_shape=[
            shape_of((rows, width), BF),
            shape_of((rows, columns), BF),
            shape_of((width, mixer_columns), BF),
        ],
        compiler_params=params(),
        cost_estimate=cost(2 * rows * width * columns, 2 * (2 * rows * width + (rows + width) * columns)),
        name="joint_rows",
    )(table, tokens, gain, shift, bias, *pieces)


def attend_kernel(base, lengths, q_ref, k_ref, v_ref, out_ref, log_ref):
    length = lengths[base + pl.program_id(0)]
    q, k, v = q_ref[...], k_ref[...], v_ref[...]
    slots, pair = q.shape
    head_of_lane = lax.broadcasted_iota(jnp.int32, (1, pair), 1) // HD
    kept = lax.broadcasted_iota(jnp.int32, (slots, 1), 0) < length
    v_turned = v.T
    scaled = q * jnp.asarray(HD**-0.5, BF)
    turned = []
    for head in range(pair // HD):
        own = jnp.where(head_of_lane == head, scaled, jnp.zeros_like(scaled))
        scores = jnp.where(kept, nt(k, own), -1e30)
        peak = jnp.max(scores, axis=0, keepdims=True)
        raised = jnp.exp(scores - peak)
        total = jnp.sum(raised, axis=0, keepdims=True)
        turned.append(nn(v_turned, raised.astype(BF)) * (1.0 / total))
        log_ref[0, 0, head : head + 1, :] = peak + jnp.log(total)
    head_of_row = lax.broadcasted_iota(jnp.int32, (pair, 1), 0) // HD
    mixed = turned[0]
    for head in range(1, len(turned)):
        mixed = jnp.where(head_of_row == head, turned[head], mixed)
    out_ref[...] = mixed.T.astype(BF)


def attend_call(lengths, joint, base, count, slots):
    pair = 2 * HD
    width = joint.shape[1] // 3
    pairs = width // pair
    part = lambda which: pl.BlockSpec(
        (slots, pair), lambda i, j, *_: (base + i, which * pairs + j)
    )
    return pl.pallas_call(
        functools.partial(attend_kernel, base),
        grid_spec=pltpu.PrefetchScalarGridSpec(
            num_scalar_prefetch=1,
            grid=(count, pairs),
            in_specs=[part(0), part(1), part(2)],
            out_specs=[
                pl.BlockSpec((slots, pair), lambda i, j, *_: (i, j)),
                pl.BlockSpec((1, 1, 2, slots), lambda i, j, *_: (i, j, 0, 0)),
            ],
        ),
        out_shape=[
            shape_of((count * slots, width), BF),
            shape_of((count, pairs, 2, slots), F32),
        ],
        compiler_params=params(steps=2),
        cost_estimate=cost(
            8 * count * slots * slots * width, 8 * count * slots * width, count * slots * slots * width // HD
        ),
        name="attend",
    )(lengths, joint, joint, joint)


def mixer_kernel(core, mine, other, m_mine, m_other, tokens, bias, gain, shift, hidden_ref, normed_ref):
    half = mine.shape[1]
    own = pl.ds(pl.multiple_of(core[0] * half, half), half)
    far = pl.ds(pl.multiple_of((1 - core[0]) * half, half), half)
    hidden_ref[:, own] = nn(mine[...], m_mine[own, :]) + nn(other[...], m_mine[far, :])
    hidden_ref[:, far] = nn(mine[...], m_other[own, :]) + nn(other[...], m_other[far, :])
    hidden = tokens[...].astype(F32) + hidden_ref[...] + bias[...]
    hidden_ref[...] = hidden
    centred = hidden - jnp.mean(hidden, axis=-1, keepdims=True)
    spread = jnp.mean(centred * centred, axis=-1, keepdims=True)
    normed_ref[...] = (centred * lax.rsqrt(spread + EPSILON) * gain[...] + shift[...]).astype(BF)


def mixer_call(core, mine, other, m_mine, m_other, tokens, bias, gain, shift, block):
    rows, half = mine.shape
    width = 2 * half
    row = lambda i, *_: (i, 0)
    return pl.pallas_call(
        mixer_kernel,
        grid_spec=pltpu.PrefetchScalarGridSpec(
            num_scalar_prefetch=1,
            grid=(rows // block,),
            in_specs=[
                pl.BlockSpec((block, half), row),
                pl.BlockSpec((block, half), row),
                whole(m_mine),
                whole(m_other),
                pl.BlockSpec((block, width), row),
                whole(bias),
                whole(gain),
                whole(shift),
            ],
            out_specs=[pl.BlockSpec((block, width), row), pl.BlockSpec((block, width), row)],
        ),
        out_shape=[shape_of((rows, width), F32), shape_of((rows, width), BF)],
        compiler_params=params(),
        cost_estimate=cost(2 * rows * width * width, 10 * rows * width),
        name="mixer",
    )(core, mine, other, m_mine, m_other, tokens, bias, gain, shift)


def make_expand_kernel(n_load, n_store):
    def kernel(load_table, store_table, n_own, n_far, grad, bias, *rest):
        pieces = rest[:n_load]
        active_ref, slope_ref = rest[n_load : n_load + 2]
        stores = rest[n_load + 2 : n_load + 2 + n_store]
        weight, total, sem, out_sem = rest[n_load + 2 + n_store :]
        step = pl.program_id(0)
        rows = n_own.shape[0]
        tile = bias.shape[1]

        @pl.when(step == 0)
        def _():
            load_pieces(load_table, pieces, weight, sem, 0, weight.shape[1])
            wait_all(weight, sem)

        columns = pl.ds(pl.multiple_of(step * tile, tile), tile)
        part = weight[:, columns]
        kept = None
        for index, source in enumerate((n_own, n_far)):
            before = nn(source[...], part) + bias[...]
            square = before * before
            inner = 0.7978845608028654 * before * (1.0 + 0.044715 * square)
            curve = jnp.tanh(inner)
            half = 0.5 + 0.5 * curve
            active = (before * half).astype(BF)
            slope = half + before * (0.5 - 0.5 * curve * curve) * (
                0.7978845608028654 + 0.1070322243 * square
            )
            span = slice(index * rows, (index + 1) * rows)
            active_ref[span, :] = active
            slope_ref[span, :] = slope.astype(BF)
            product = tn(active, grad[span, :])
            kept = product if kept is None else kept + product
        total[columns, :] = kept.astype(BF)

        @pl.when(step == pl.num_programs(0) - 1)
        def _():
            store_pieces(store_table, total, stores, out_sem)
            wait_all(total, out_sem)

    return kernel


def expand_call(load_table, store_table, n_own, n_far, grad, bias, pieces, store_shapes, tile):
    rows, width = grad.shape
    columns = bias.shape[1]
    column = lambda i, *_: (0, i)
    return pl.pallas_call(
        make_expand_kernel(len(pieces), len(store_shapes)),
        grid_spec=pltpu.PrefetchScalarGridSpec(
            num_scalar_prefetch=2,
            grid=(columns // tile,),
            in_specs=[whole(n_own), whole(n_far), whole(grad), pl.BlockSpec((1, tile), column)]
            + [ANY] * len(pieces),
            out_specs=[pl.BlockSpec((rows, tile), column), pl.BlockSpec((rows, tile), column)]
            + [ANY] * len(store_shapes),
            scratch_shapes=[
                pltpu.VMEM((width, columns), BF),
                pltpu.VMEM((columns, width), BF),
                pltpu.SemaphoreType.DMA,
                pltpu.SemaphoreType.DMA,
            ],
        ),
        out_shape=[shape_of((rows, columns), BF), shape_of((rows, columns), BF)]
        + [shape_of(s, BF) for s in store_shapes],
        compiler_params=params(),
        cost_estimate=cost(4 * rows * width * columns, 4 * rows * (columns + width) + 4 * width * columns),
        name="expand_and_dreduce",
    )(load_table, store_table, n_own, n_far, grad, bias, *pieces)


def make_back_kernel(n_expand, n_reduce):
    def kernel(expand_table, reduce_table, grad, slope, *rest):
        expand_pieces = rest[:n_expand]
        reduce_pieces = rest[n_expand : n_expand + n_reduce]
        (before_ref, bias_ref, far_ref, own_ref, expand, reduce, total, sem, reduce_sem) = rest[
            n_expand + n_reduce :
        ]
        step = pl.program_id(0)
        tile = slope.shape[1]
        rows = own_ref.shape[0]

        @pl.when(step == 0)
        def _():
            load_pieces(reduce_table, reduce_pieces, reduce, reduce_sem, 0, reduce.shape[1])
            load_pieces(expand_table, expand_pieces, expand, sem, 0, expand.shape[1])
            wait_all(reduce, reduce_sem)
            wait_all(expand, sem)

        columns = pl.ds(pl.multiple_of(step * tile, tile), tile)
        part = reduce[columns, :]
        expand_part = expand[:, columns]
        sums = None
        for index in range(2):
            span = slice(index * rows, (index + 1) * rows)
            before = slope[span, :].astype(F32) * nt(grad[span, :], part)
            low = before.astype(BF)
            before_ref[span, :] = low
            column_sum = jnp.sum(low.astype(F32), axis=0, keepdims=True)
            sums = column_sum if sums is None else sums + column_sum
            product = nt(low, expand_part)

            @pl.when(step == 0)
            def _():
                total[span, :] = product

            @pl.when(step > 0)
            def _():
                total[span, :] += product

        bias_ref[...] = sums

        @pl.when(step == pl.num_programs(0) - 1)
        def _():
            own_ref[...] = total[:rows, :]
            far_ref[...] = total[rows:, :].astype(BF)

    return kernel


def back_call(expand_table, reduce_table, grad, slope, expand_pieces, reduce_pieces, tile):
    rows, width = grad.shape
    columns = slope.shape[1]
    column = lambda i, *_: (0, i)
    fixed = lambda *_: (0, 0)
    return pl.pallas_call(
        make_back_kernel(len(expand_pieces), len(reduce_pieces)),
        grid_spec=pltpu.PrefetchScalarGridSpec(
            num_scalar_prefetch=2,
            grid=(columns // tile,),
            in_specs=[whole(grad), pl.BlockSpec((rows, tile), column)]
            + [ANY] * (len(expand_pieces) + len(reduce_pieces)),
            out_specs=[
                pl.BlockSpec((rows, tile), column),
                pl.BlockSpec((1, tile), column),
                pl.BlockSpec((rows // 2, width), fixed),
                pl.BlockSpec((rows // 2, width), fixed),
            ],
            scratch_shapes=[
                pltpu.VMEM((width, columns), BF),
                pltpu.VMEM((columns, width), BF),
                pltpu.VMEM((rows, width), F32),
                pltpu.SemaphoreType.DMA,
                pltpu.SemaphoreType.DMA,
            ],
        ),
        out_shape=[
            shape_of((rows, columns), BF),
            shape_of((1, columns), F32),
            shape_of((rows // 2, width), BF),
            shape_of((rows // 2, width), F32),
        ],
        compiler_params=params(),
        cost_estimate=cost(4 * rows * width * columns, 4 * rows * (columns + width) + 4 * width * columns),
        name="grad_before",
    )(expand_table, reduce_table, grad, slope, *expand_pieces, *reduce_pieces)


def make_dexpand_kernel(n_store):
    def kernel(store_table, n_own, n_far, before, *rest):
        stores = rest[:n_store]
        total, out_sem = rest[n_store:]
        step = pl.program_id(0)
        rows = n_own.shape[0]
        tile = before.shape[1]
        columns = pl.ds(pl.multiple_of(step * tile, tile), tile)
        total[:, columns] = (
            tn(n_own[...], before[:rows, :]) + tn(n_far[...], before[rows:, :])
        ).astype(BF)

        @pl.when(step == pl.num_programs(0) - 1)
        def _():
            store_pieces(store_table, total, stores, out_sem)
            wait_all(total, out_sem)

    return kernel


def dexpand_call(store_table, n_own, n_far, before, store_shapes, tile):
    rows, columns = before.shape
    width = n_own.shape[1]
    return pl.pallas_call(
        make_dexpand_kernel(len(store_shapes)),
        grid_spec=pltpu.PrefetchScalarGridSpec(
            num_scalar_prefetch=1,
            grid=(columns // tile,),
            in_specs=[whole(n_own), whole(n_far), pl.BlockSpec((rows, tile), lambda i, *_: (0, i))],
            out_specs=[ANY] * len(store_shapes),
            scratch_shapes=[pltpu.VMEM((width, columns), BF), pltpu.SemaphoreType.DMA],
        ),
        out_shape=[shape_of(s, BF) for s in store_shapes],
        compiler_params=params(),
        cost_estimate=cost(2 * rows * width * columns, 2 * (rows * width + rows * columns + width * columns)),
        name="dexpand",
    )(store_table, n_own, n_far, before)


def attn_grad_kernel(
    core, g_own, g_far, hidden, cotangent, kept, gain, m_mine, m_other,
    hidden_grad_ref, low_ref, mine_ref, other_ref, sums_ref,
):
    half = mine_ref.shape[1]
    step = pl.program_id(0)
    own = pl.ds(pl.multiple_of(core[0] * half, half), half)
    far = pl.ds(pl.multiple_of((1 - core[0]) * half, half), half)
    g = g_own[...] + g_far[...].astype(F32)
    value = hidden[...]
    centred = value - jnp.mean(value, axis=-1, keepdims=True)
    spread = jnp.mean(centred * centred, axis=-1, keepdims=True)
    inverse = lax.rsqrt(spread + EPSILON)
    unit = centred * inverse
    scaled = g * gain[...]
    back = inverse * (
        scaled
        - jnp.mean(scaled, axis=-1, keepdims=True)
        - unit * jnp.mean(scaled * unit, axis=-1, keepdims=True)
    )
    total = cotangent[...].astype(F32) * kept[...] + back
    low = total.astype(BF)
    hidden_grad_ref[...] = total
    low_ref[...] = low
    sums = jnp.concatenate(
        [
            jnp.sum(g * unit, axis=0, keepdims=True),
            jnp.sum(g, axis=0, keepdims=True),
            jnp.sum(low.astype(F32), axis=0, keepdims=True),
        ],
        axis=0,
    )

    @pl.when(step == 0)
    def _():
        sums_ref[...] = sums

    @pl.when(step > 0)
    def _():
        sums_ref[...] += sums

    left, right = low_ref[:, own], low_ref[:, far]
    mine_ref[...] = (nt(left, m_mine[own, :]) + nt(right, m_other[own, :])).astype(BF)
    other_ref[...] = (nt(left, m_mine[far, :]) + nt(right, m_other[far, :])).astype(BF)


def attn_grad_call(core, g_own, g_far, hidden, cotangent, kept, gain, m_mine, m_other, block):
    rows, width = hidden.shape
    half = width // 2
    row = lambda i, *_: (i, 0)
    wide = pl.BlockSpec((block, width), row)
    narrow_block = pl.BlockSpec((block, half), row)
    return pl.pallas_call(
        attn_grad_kernel,
        grid_spec=pltpu.PrefetchScalarGridSpec(
            num_scalar_prefetch=1,
            grid=(rows // block,),
            in_specs=[wide, wide, wide, wide, pl.BlockSpec((block, 1), row), whole(gain), whole(m_mine), whole(m_other)],
            out_specs=[wide, wide, narrow_block, narrow_block, pl.BlockSpec((3, width), lambda *_: (0, 0))],
        ),
        out_shape=[
            shape_of((rows, width), F32),
            shape_of((rows, width), BF),
            shape_of((rows, half), BF),
            shape_of((rows, half), BF),
            shape_of((3, width), F32),
        ],
        compiler_params=params(),
        cost_estimate=cost(2 * rows * width * width, 18 * rows * width),
        name="grad_attended",
    )(core, g_own, g_far, hidden, cotangent, kept, gain, m_mine, m_other)


def dmixer_kernel(core, mine, other, low, keep_ref, send_ref):
    half = mine.shape[1]
    own = pl.ds(pl.multiple_of(core[0] * half, half), half)
    far = pl.ds(pl.multiple_of((1 - core[0]) * half, half), half)
    for source, rows in ((mine, own), (other, far)):
        keep_ref[rows, :] = tn(source[...], low[:, own]).astype(BF)
        send_ref[rows, :] = tn(source[...], low[:, far]).astype(BF)


def dmixer_call(core, mine, other, low):
    rows, width = low.shape
    half = width // 2
    target = pl.BlockSpec((width, half), lambda *_: (0, 0))
    return pl.pallas_call(
        dmixer_kernel,
        grid_spec=pltpu.PrefetchScalarGridSpec(
            num_scalar_prefetch=1,
            grid=(1,),
            in_specs=[whole(mine), whole(other), whole(low)],
            out_specs=[target, target],
        ),
        out_shape=[shape_of((width, half), BF)] * 2,
        compiler_params=params(),
        cost_estimate=cost(2 * rows * width * width, 4 * rows * width + 2 * width * width),
        name="dmixer",
    )(core, mine, other, low)


def attend_back_kernel(base, lengths, q_ref, k_ref, v_ref, g_ref, log_ref, dq_ref, dk_ref, dv_ref):
    length = lengths[base + pl.program_id(0)]
    q, k, v, g = q_ref[...], k_ref[...], v_ref[...], g_ref[...]
    slots, pair = q.shape
    head_of_lane = lax.broadcasted_iota(jnp.int32, (1, pair), 1) // HD
    kept = lax.broadcasted_iota(jnp.int32, (slots, 1), 0) < length
    factor = jnp.asarray(HD**-0.5, BF)
    k_turned = k.T
    zero = jnp.zeros_like(q)
    turned, dk, dv = [], None, None
    for head in range(pair // HD):
        own_q = jnp.where(head_of_lane == head, q, zero)
        own_g = jnp.where(head_of_lane == head, g, zero)
        scores = nt(k, own_q * factor)
        probs = jnp.where(kept, jnp.exp(scores - log_ref[0, 0, head : head + 1, :]), 0.0)
        shares = nt(v, own_g * factor)
        inner = jnp.sum(probs * shares, axis=0, keepdims=True)
        raw = (probs * (shares - inner)).astype(BF)
        turned.append(nn(k_turned, raw))
        dk_head = nn(raw, own_q)
        dv_head = nn(probs.astype(BF), own_g)
        dk = dk_head if dk is None else dk + dk_head
        dv = dv_head if dv is None else dv + dv_head
    head_of_row = lax.broadcasted_iota(jnp.int32, (pair, 1), 0) // HD
    mixed = turned[0]
    for head in range(1, len(turned)):
        mixed = jnp.where(head_of_row == head, turned[head], mixed)
    dq_ref[...] = mixed.T.astype(BF)
    dk_ref[...] = dk.astype(BF)
    dv_ref[...] = dv.astype(BF)


def attend_back_call(lengths, joint, grad, logs, base, slots):
    count, pairs = logs.shape[:2]
    pair = 2 * HD
    width = joint.shape[1] // 3
    part = lambda which: pl.BlockSpec(
        (slots, pair), lambda i, j, *_: (base + i, which * pairs + j)
    )
    block = pl.BlockSpec((slots, pair), lambda i, j, *_: (i, j))
    return pl.pallas_call(
        functools.partial(attend_back_kernel, base),
        grid_spec=pltpu.PrefetchScalarGridSpec(
            num_scalar_prefetch=1,
            grid=(count, pairs),
            in_specs=[part(0), part(1), part(2), block, pl.BlockSpec((1, 1, 2, slots), lambda i, j, *_: (i, j, 0, 0))],
            out_specs=[block, block, block],
        ),
        out_shape=[shape_of((count * slots, width), BF)] * 3,
        compiler_params=params(steps=2),
        cost_estimate=cost(
            20 * count * slots * slots * width, 14 * count * slots * width, count * slots * slots * width // HD
        ),
        name="attend_back",
    )(lengths, joint, joint, joint, grad, logs)


def make_djoint_kernel(n_store):
    def kernel(store_table, normed, *rest):
        own, far = rest[0:3], rest[3:6]
        mixer_own, mixer_far = rest[6:8]
        sums_ref = rest[8]
        stores = rest[9 : 9 + n_store]
        total, out_sem = rest[9 + n_store :]
        step = pl.program_id(0)
        rows = own[0].shape[0]
        half = own[0].shape[1]
        for which in range(3):
            @pl.when(step == which)
            def _(which=which):
                a, b = own[which][...], far[which][...]
                total[:, which * half : (which + 1) * half] = (
                    tn(normed[:rows, :], a) + tn(normed[rows:, :], b)
                ).astype(BF)
                sums_ref[which : which + 1, :] = jnp.sum(a.astype(F32), axis=0, keepdims=True) + jnp.sum(
                    b.astype(F32), axis=0, keepdims=True
                )

        @pl.when(step == 2)
        def _():
            total[:, 3 * half :] = (mixer_own[...].astype(F32) + mixer_far[...].astype(F32)).astype(BF)
            store_pieces(store_table, total, stores, out_sem)
            wait_all(total, out_sem)

    return kernel


def djoint_call(store_table, normed, own, far, mixer_own, mixer_far, store_shapes):
    rows, width = normed.shape
    half = own[0].shape[1]
    columns = 3 * half + mixer_own.shape[1]
    return pl.pallas_call(
        make_djoint_kernel(len(store_shapes)),
        grid_spec=pltpu.PrefetchScalarGridSpec(
            num_scalar_prefetch=1,
            grid=(3,),
            in_specs=[whole(normed)] + [whole(a) for a in own + far] + [whole(mixer_own), whole(mixer_far)],
            out_specs=[pl.BlockSpec((3, half), lambda *_: (0, 0))] + [ANY] * len(store_shapes),
            scratch_shapes=[pltpu.VMEM((width, columns), BF), pltpu.SemaphoreType.DMA],
        ),
        out_shape=[shape_of((3, half), F32)] + [shape_of(s, BF) for s in store_shapes],
        compiler_params=params(),
        cost_estimate=cost(6 * rows * width * half, 2 * (rows * width + 3 * rows * half + width * columns)),
        name="djoint",
    )(store_table, normed, *own, *far, mixer_own, mixer_far)


def make_split_kernel(n_sources, n_pieces, turned):
    def kernel(table, *rest):
        sources = rest[:n_sources]
        pieces = rest[n_sources : n_sources + n_pieces]
        out_ref, weight, sem = rest[-3:]
        step = pl.program_id(0)

        @pl.when(step == 0)
        def _():
            load_pieces(table, pieces, weight, sem, 0, weight.shape[1])
            wait_all(weight, sem)

        total, start = None, 0
        for source in sources:
            size = source.shape[1]
            if turned:
                product = nt(source[...], weight[:, start : start + size])
            else:
                product = nn(source[...], weight[start : start + size, :])
            total = product if total is None else total + product
            start += size
        out_ref[...] = total.astype(out_ref.dtype)

    return kernel


def split_call(table, sources, pieces, weight_shape, turned, dtype, block, first, count, extra, name):
    inner = weight_shape[1] if turned else weight_shape[0]
    width = weight_shape[0] if turned else weight_shape[1]
    rows = count * block
    kernel = make_split_kernel(len(sources), len(pieces), turned)
    if extra:
        base = kernel
        kernel = lambda table, *rest: base(table, *rest[len(extra):])
    return pl.pallas_call(
        kernel,
        grid_spec=pltpu.PrefetchScalarGridSpec(
            num_scalar_prefetch=1,
            grid=(count,),
            in_specs=[ANY] * len(extra)
            + [pl.BlockSpec((block, a.shape[1]), lambda i, *_: (first + i, 0)) for a in sources]
            + [ANY] * len(pieces),
            out_specs=pl.BlockSpec((block, width), lambda i, *_: (i, 0)),
            scratch_shapes=[pltpu.VMEM(weight_shape, BF), pltpu.SemaphoreType.DMA],
        ),
        out_shape=shape_of((rows, width), dtype),
        compiler_params=params(),
        cost_estimate=cost(2 * rows * inner * width, 2 * (rows * inner + inner * width) + 4 * rows * width),
        name=name,
    )(table, *extra, *sources, *pieces)


class Ring:
    def __init__(self, nx, ns):
        self.nx, self.ns = nx, ns
        self.x, self.core = lax.axis_index("x"), lax.axis_index("core")
        shard = lax.axis_index("shard")
        self.z, self.y = shard // 2, shard % 2
        self.turn = jnp.where(self.core == 0, 1, -1)

    def send(self, array, step):
        pairs = []
        for x in range(2):
            for core in range(2):
                for z in range(4):
                    for y in range(2):
                        d = 1 - 2 * core
                        to = {
                            "xy": (1 - x, z, y) if core == 0 else (x, z, 1 - y),
                            "yx": (x, z, 1 - y) if core == 0 else (1 - x, z, y),
                            "z1": (x, (z + d) % 4, y),
                            "z2": (x, (z - d) % 4, y),
                            "x": (1 - x, z, y),
                        }[step]
                        index = lambda a, b, e: (a * 2 + core) * 8 + b * 2 + e
                        pairs.append((index(x, z, y), index(*to)))
        return lax.ppermute(array, ALL, pairs)

    def start_of(self, x, z, y, rows, offset):
        return (((z % 4) * 2 + y) * 2 + x) * rows + offset

    def pick(self, first, second):
        swap_x = jnp.where(self.core == 0, first, second)
        swap_y = jnp.where(self.core == 0, second, first)
        return (self.x + swap_x) % 2, (self.y + swap_y) % 2


    def gather_first(self, part):
        across = self.send(part, "xy")
        two = jnp.stack([part, across])
        four = jnp.concatenate([two, self.send(two, "yx")])
        near = self.send(four, "z1")
        back = self.send(four, "z2")
        far = self.send(near, "z1")
        return [four, near, back, far]

    def table_first(self, rows, offset):
        found = []
        for dz in (0, -self.turn, self.turn, 2):
            for second in (0, 1):
                for first in (0, 1):
                    x, y = self.pick(first, second)
                    found.append(self.start_of(x, self.z + dz, y, rows, offset))
        return found

    def gather_second(self, part):
        near = self.send(part, "z1")
        back = self.send(part, "z2")
        far = self.send(near, "z1")
        four = jnp.stack([part, near, back, far])
        eight = jnp.concatenate([four, self.send(four, "yx")])
        return [eight, self.send(eight, "xy")]

    def table_second(self, rows, offset):
        found = []
        for first in (0, 1):
            for second in (0, 1):
                for dz in (0, -self.turn, self.turn, 2):
                    x, y = self.pick(first, second)
                    found.append(self.start_of(x, self.z + dz, y, rows, offset))
        return found


    def out_first(self, rows, offset):
        found = []
        for dz in (2, -self.turn, self.turn, 0):
            for second in (1, 0):
                for first in (1, 0):
                    x, y = self.pick(first, second)
                    found.append(self.start_of(x, self.z + dz, y, rows, offset))
        return found

    def sum_first(self, parts):
        far, back, near, own = parts
        near = add(near, self.send(far, "z1"))
        came_back = self.send(back, "z2")
        came = self.send(near, "z1")
        give = add(own[:2], came[:2], came_back[:2])
        keep = add(own[2:], came[2:], came_back[2:])
        came = self.send(give, "yx")
        give = add(keep[0], came[0])
        keep = add(keep[1], came[1])
        return add(keep, self.send(give, "xy"))

    def out_second(self, rows, offset):
        found = []
        for first in (1, 0):
            for second in (1, 0):
                for dz in (2, -self.turn, self.turn, 0):
                    x, y = self.pick(first, second)
                    found.append(self.start_of(x, self.z + dz, y, rows, offset))
        return found

    def sum_second(self, parts):
        give, keep = parts
        came = self.send(give, "xy")
        give = add(keep[:4], came[:4])
        keep = add(keep[4:], came[4:])
        came = self.send(give, "yx")
        far = add(keep[0], came[0])
        back = add(keep[1], came[1])
        near = add(keep[2], came[2], self.send(far, "z1"))
        came_back = self.send(back, "z2")
        return add(keep[3], came[3], came_back, self.send(near, "z1"))

    def spread(self, final):
        both = self.order(final, self.send(final, "x"), self.x)
        return self.order(both, swap(both), self.core)

    @staticmethod
    def order(mine, other, index):
        return jnp.stack([jnp.where(index == 0, mine, other), jnp.where(index == 0, other, mine)])


def add(*terms):
    total = terms[0].astype(F32)
    for term in terms[1:]:
        total = total + term.astype(F32)
    return total.astype(BF)


def swap(array):
    return lax.ppermute(array, "core", [(0, 1), (1, 0)])


class Plain:
    def __init__(self, nx, ns):
        self.nx, self.ns = nx, ns

    def gather(self, part):
        return [lax.all_gather(part, ("shard", "x"), axis=0, tiled=True)[None]]

    def sums(self, parts):
        return lax.psum_scatter(parts[0][0], ("shard", "x"), scatter_dimension=0, tiled=True)

    def spread(self, final):
        both = lax.all_gather(final, "x", axis=0, tiled=False)
        return lax.all_gather(both, "core", axis=0, tiled=False)


def numbers(values):
    return jnp.stack([jnp.asarray(v, jnp.int32) for v in values])


def gather_vectors(vectors):
    packed = jnp.concatenate(vectors).astype(BF)
    every = lax.all_gather(packed, "shard", axis=0, tiled=False).astype(F32)
    pieces, start = [], 0
    for vector in vectors:
        pieces.append(every[:, start : start + vector.shape[0]].reshape(-1))
        start += vector.shape[0]
    return pieces


def sum_vectors(grads, shards):
    packed = jnp.concatenate([grad.reshape(shards, -1) for grad in grads], axis=1)
    total = lax.psum(packed, ALL)
    own = lax.dynamic_index_in_dim(total, lax.axis_index("shard"), 0, keepdims=False)
    pieces, start = [], 0
    for grad in grads:
        size = grad.size // shards
        pieces.append(own[start : start + size])
        start += size
    return pieces


def on_device(
    nx,
    ns,
    tokens,
    lengths,
    cotangent,
    norm_gain,
    norm_shift,
    joint_weight,
    joint_bias,
    mixer_weight,
    mixer_bias,
    ffnorm_gain,
    ffnorm_shift,
    expand_weight,
    expand_bias,
    reduce_weight,
    reduce_bias,
):
    count, slots, width = tokens.shape
    rows = count * slots
    half = width // 2
    hidden_units = expand_weight.shape[1]
    half_units = hidden_units // 2
    unit_block = half_units // ns
    x, core = lax.axis_index("x"), lax.axis_index("core")
    ring = nx == 2 and ns == 8
    links = Ring(nx, ns) if ring else Plain(nx, ns)
    core_number = numbers([core])

    part_rows = width // (ns * nx)
    cut = lambda w, size: lax.dynamic_slice_in_dim(w, x * size, size, 0)
    joint_part = lax.dynamic_index_in_dim(
        cut(joint_weight, part_rows).reshape(part_rows, 3, 2, half), core, 2, keepdims=False
    ).reshape(part_rows, 3 * half)
    mixer_part = lax.dynamic_slice_in_dim(cut(mixer_weight, part_rows), core * half, half, 1)
    joint_part = jnp.concatenate([joint_part, mixer_part], axis=1).astype(BF)
    expand_part = lax.dynamic_index_in_dim(
        cut(expand_weight, part_rows).reshape(part_rows, ns, 2, unit_block), core, 2, keepdims=False
    ).reshape(part_rows, half_units).astype(BF)
    reduce_rows = unit_block // nx
    reduce_part = lax.dynamic_slice_in_dim(
        reduce_weight, core * unit_block + x * reduce_rows, reduce_rows, 0
    ).astype(BF)

    (gain_one, shift_one, joint_vector, mixer_vector, gain_two, shift_two, expand_vector, reduce_vector) = gather_vectors(
        (norm_gain, norm_shift, joint_bias, mixer_bias, ffnorm_gain, ffnorm_shift, expand_bias, reduce_bias)
    )
    flat = tokens.reshape(rows, width)
    grad_flat = cotangent.reshape(rows, width)
    far_lengths = swap(lengths)
    both_lengths = jnp.concatenate([lengths, far_lengths])
    positions = jnp.arange(slots)
    kept_all = (positions[None, :] < both_lengths[:, None]).reshape(2 * rows, 1).astype(F32)
    kept = kept_all[:rows]
    both_tokens = jnp.concatenate([flat, swap(flat)])
    both_grad = jnp.concatenate([grad_flat, swap(grad_flat)]) * kept_all.astype(BF)
    gain_one, shift_one, mixer_vector, gain_two, shift_two, reduce_vector = (
        v.reshape(1, width) for v in (gain_one, shift_one, mixer_vector, gain_two, shift_two, reduce_vector)
    )
    own_half = lambda v: lax.dynamic_slice_in_dim(v, core * half, half, 0)
    bias_one = jnp.concatenate(
        [own_half(joint_vector[:width]), jnp.zeros((half,), F32), own_half(joint_vector[width:])]
    ).reshape(1, 3 * half)
    bias_expand = lax.dynamic_index_in_dim(
        expand_vector.reshape(ns, 2, unit_block), core, 1, keepdims=False
    ).reshape(1, half_units)

    if ring:
        first = part_rows // 2
        joint_pieces = links.gather_first(joint_part[:first]) + links.gather_second(joint_part[first:])
        joint_table = numbers(links.table_first(part_rows, 0) + links.table_second(part_rows, first))
        expand_pieces = links.gather_first(expand_part)
        expand_table = numbers(links.table_first(part_rows, 0))
        reduce_pieces = links.gather_second(reduce_part)
        reduce_table = numbers(links.table_second(reduce_rows, 0))
        joint_out = numbers(links.out_first(part_rows, 0) + links.out_second(part_rows, first))
        expand_out = numbers(links.out_first(part_rows, 0))
        reduce_out = numbers(links.out_second(reduce_rows, 0))
        joint_shapes = [(4, first, 2 * width)] * 4 + [(8, first, 2 * width)] * 2
        expand_shapes = [(4, part_rows, half_units)] * 4
        reduce_shapes = [(8, reduce_rows, width)] * 2
    else:
        joint_pieces = links.gather(joint_part)
        expand_pieces = links.gather(expand_part)
        reduce_pieces = links.gather(reduce_part)
        joint_table = expand_table = reduce_table = joint_out = expand_out = reduce_out = numbers([0])
        joint_shapes = [(1, width, 2 * width)]
        expand_shapes = [(1, width, half_units)]
        reduce_shapes = [(1, half_units, width)]

    normed, joint, mixer_own = joint_call(
        joint_table, both_tokens, gain_one, shift_one, bias_one, joint_pieces, slots
    )
    mixer_far = swap(mixer_own)
    attended_far, logs_far = attend_call(both_lengths, joint, count, count, slots)
    attended_other = swap(attended_far)
    attended, logs = attend_call(both_lengths, joint, 0, count, slots)
    hidden, normed_two = mixer_call(
        core_number, attended, attended_other, mixer_own, mixer_far, flat, mixer_vector, gain_two, shift_two, slots
    )
    normed_two_far = swap(normed_two)
    active, slope, *dreduce_parts = expand_call(
        expand_table, reduce_out, normed_two, normed_two_far, both_grad, bias_expand, expand_pieces, reduce_shapes, 256
    )
    dreduce = links.sum_second(dreduce_parts) if ring else links.sums(dreduce_parts)

    grad_before, dexpand_bias, g_send, g_own = back_call(
        expand_table, reduce_table, both_grad, slope, expand_pieces, reduce_pieces, 256
    )
    g_far = swap(g_send)
    dexpand_parts = dexpand_call(expand_out, normed_two, normed_two_far, grad_before, expand_shapes, 256)
    dexpand = links.sum_first(dexpand_parts) if ring else links.sums(dexpand_parts)
    grad_hidden, grad_attn, grad_mine, grad_other, sums_two = attn_grad_call(
        core_number, g_own, g_far, hidden, grad_flat, kept, gain_two, mixer_own, mixer_far, slots
    )
    grad_far = swap(grad_other)
    dmixer_keep, dmixer_send = dmixer_call(core_number, attended, attended_other, grad_attn)
    dmixer_far = swap(dmixer_send)
    own_grads = attend_back_call(both_lengths, joint, grad_mine, logs, 0, slots)
    far_grads = attend_back_call(both_lengths, joint, grad_far, logs_far, count, slots)
    joint_sums, *djoint_parts = djoint_call(
        joint_out, normed, list(own_grads), list(far_grads), dmixer_keep, dmixer_far, joint_shapes
    )
    if ring:
        djoint = jnp.concatenate([links.sum_first(djoint_parts[:4]), links.sum_second(djoint_parts[4:])])
    else:
        djoint = links.sums(djoint_parts)

    joint_shape = (width, 3 * half)
    rows_far = split_call(
        joint_table, list(far_grads), joint_pieces, joint_shape, True, BF, slots, 0, count, [djoint_parts[0]], "grad_rows_far"
    )
    rows_far = swap(rows_far)
    rows_own = split_call(
        joint_table, list(own_grads), joint_pieces, joint_shape, True, F32, slots, 0, count, [djoint_parts[0]], "grad_rows"
    )
    branch_far = split_call(
        reduce_table, [active], reduce_pieces, (half_units, width), False, BF, slots, count, count, [djoint_parts[0]], "branch_far"
    )
    branch_far = swap(branch_far)
    branch_own = split_call(
        reduce_table, [active], reduce_pieces, (half_units, width), False, F32, slots, 0, count, [djoint_parts[0]], "branch"
    )
    layer_out = (kept * (hidden + branch_own + branch_far.astype(F32) + reduce_vector)).astype(BF)

    g = rows_own + rows_far.astype(F32)
    value = flat.astype(F32)
    centred = value - jnp.mean(value, axis=-1, keepdims=True)
    inverse = lax.rsqrt(jnp.mean(centred * centred, axis=-1, keepdims=True) + EPSILON)
    unit = centred * inverse
    scaled = g * gain_one
    back = inverse * (
        scaled
        - jnp.mean(scaled, axis=-1, keepdims=True)
        - unit * jnp.mean(scaled * unit, axis=-1, keepdims=True)
    )
    input_grad = (grad_hidden + back).astype(BF)

    zeros = jnp.zeros((half,), F32)
    place = lambda v: jnp.where(core == 0, jnp.concatenate([v, zeros]), jnp.concatenate([zeros, v]))
    expand_sums = dexpand_bias.reshape(ns, 1, unit_block)
    gap = jnp.zeros_like(expand_sums)
    expand_sums = jnp.where(
        core == 0, jnp.concatenate([expand_sums, gap], axis=1), jnp.concatenate([gap, expand_sums], axis=1)
    )
    grad_sum = jnp.sum(both_grad[:rows].astype(F32), axis=0)
    vectors = sum_vectors(
        (
            jnp.sum(g * unit, axis=0),
            jnp.sum(g, axis=0),
            jnp.concatenate([place(joint_sums[0]), place(joint_sums[2])]),
            sums_two[2],
            sums_two[0],
            sums_two[1],
            expand_sums.reshape(-1),
            grad_sum,
        ),
        ns,
    )

    djoint, dexpand, dreduce = links.spread(djoint), links.spread(dexpand), links.spread(dreduce)
    shard_rows = nx * part_rows
    dmixer = djoint[..., 3 * half :]
    djoint = djoint[..., : 3 * half].reshape(2, shard_rows, 3, half)
    djoint = djoint.transpose(1, 2, 0, 3).reshape(shard_rows, 3 * width)
    dmixer = dmixer.reshape(2, shard_rows, half).transpose(1, 0, 2).reshape(shard_rows, width)
    dexpand = dexpand.reshape(2, shard_rows, ns, unit_block).transpose(1, 2, 0, 3).reshape(shard_rows, hidden_units)
    dreduce = dreduce.reshape(2 * unit_block, width)
    return (
        layer_out.reshape(tokens.shape),
        input_grad.reshape(tokens.shape),
        vectors[0],
        vectors[1],
        djoint.astype(F32),
        vectors[2],
        dmixer.astype(F32),
        vectors[3],
        vectors[4],
        vectors[5],
        dexpand.astype(F32),
        vectors[6],
        dreduce.astype(F32),
        vectors[7],
    )


def solution(mesh):
    ns = mesh.shape["shard"]
    nx = mesh.shape["rep"] // 2
    split = Mesh(mesh.devices.reshape(nx, 2, ns), ALL)
    rows, vector, matrix = P(ALL), P("shard"), P("shard", None)
    return jax.shard_map(
        functools.partial(on_device, nx, ns),
        mesh=split,
        in_specs=(
            rows,
            rows,
            rows,
            vector,
            vector,
            matrix,
            vector,
            matrix,
            vector,
            vector,
            vector,
            matrix,
            vector,
            matrix,
            vector,
        ),
        out_specs=(
            rows,
            rows,
            vector,
            vector,
            matrix,
            vector,
            matrix,
            vector,
            vector,
            vector,
            matrix,
            vector,
            matrix,
            vector,
        ),
        check_vma=False,
    )
```

time: 926 us -> 571 us (0.62)
  waiting for transfers between devices: 488 us -> 113 us
  matrix products: 209 us -> 0 us
  Pallas kernels: 0 us -> 196 us
  starting transfers between devices: 0.41 us -> 71.2 us
  local copies, waits for them, and re-layouts: 91.4 us -> 53.2 us
  other arithmetic: 32.6 us -> 55.1 us
  blocking collectives: 84.7 us -> 70.4 us
  between operations: 15.1 us -> 2.14 us
    reduce_scatter x4 -> x0, waiting for transfers between devices: 299 us -> none  [scatter_matrix(): lax.psum_scatter(grad.astype(jnp.bfloat16), ('shard', 'rep'), scatter_dim...]
    dot_general x26 -> x0, matrix products: 209 us -> none  [the longest x4 38.2 us: back_product(): lax.dot_general(cotan, weight, (((1,), (1,)), ((), ())), preferred_elemen...]
    pallas_call x0 -> x16, Pallas kernels: none -> 196 us  [the longest x1 36.5 us: back_call(): pl.pallas_call(make_back_kernel(len(expand_pieces), len(reduce_pieces)),...]
    all_gather x6 -> x0, waiting for transfers between devices: 189 us -> none  [the longest x4 166 us: gather_matrix(): return lax.all_gather(narrow(part), ('shard', 'rep'), axis=0, tiled=True)]
    ppermute x0 -> x57, waiting for transfers between devices: none -> 113 us  [the longest x43 113 us: send(): return lax.ppermute(array, ALL, pairs)]
    ppermute x0 -> x57, starting transfers between devices: none -> 71.2 us  [the longest x43 66.4 us: send(): return lax.ppermute(array, ALL, pairs)]
    reshape x5 -> x3, local copies, waits for them, and re-layouts: 29.6 us -> 4.05 us  [the longest x1 2.03 us: on_device(): cut(joint_weight, part_rows).reshape(part_rows, 3, 2, half)]
    all_gather x3 -> x1, blocking collectives: 47.2 us -> 30.9 us  [gather_vectors(): every = lax.all_gather(packed, 'shard', axis=0, tiled=False).astype(F32)]
  transfers between devices with their start and end apart: 10 -> 57, of which waited for: 8 -> 15; matrix products, arithmetic and copies ran while one was open for 31% -> 14% of each run, Pallas kernels for 0% -> 28%
where the time goes in v2:
time: 571 us; the launch traced here: 561 us
  Pallas kernels  196 us (34%)
  waiting for transfers between devices  113 us (20%)
  starting transfers between devices  71.2 us (12%)
  blocking collectives  70.4 us (12%)
  other arithmetic  55.1 us (10%)
  local copies, waits for them, and re-layouts  53.2 us (9%)
    ppermute x43, waiting for transfers between devices, send(): return lax.ppermute(array, ALL, pairs)  113 us
    ppermute x43, starting transfers between devices, send(): return lax.ppermute(array, ALL, pairs)  66.4 us
    psum x1, blocking collectives, sum_vectors(): total = lax.psum(packed, ALL)  39.5 us
    pallas_call x1, Pallas kernels, back_call(): pl.pallas_call(make_back_kernel(len(expand_pieces), len(reduce_pieces)),...  36.5 us
    all_gather x1, blocking collectives, gather_vectors(): every = lax.all_gather(packed, 'shard', axis=0, tiled=False).astype(F32)  30.9 us
    pallas_call x4, Pallas kernels, split_call(): pl.pallas_call(kernel, grid_spec=pltpu.PrefetchScalarGridSpec(num_scalar_...  30.7 us
    pallas_call x1, Pallas kernels, expand_call(): pl.pallas_call(make_expand_kernel(len(pieces), len(store_shapes)), grid_s...  28 us
    pallas_call x2, Pallas kernels, attend_back_call(): pl.pallas_call(functools.partial(attend_back_kernel, base), grid_spec=plt...  25.1 us
  transfers between devices with their start and end apart: 57, of which 15 were waited for; matrix products, arithmetic and copies ran while one was open for 14% of the time, Pallas kernels for 28%

profile of v2, /device:TPU:0, one launch (start us, length us, event | category | flops | bytes accessed | tf_op | source)
XLA Modules:
  0.0 560.8 jit_solution(12309883470257451418)
XLA Ops:
  9.0 3.0 collective-permute-start.7
  23.7 30.9 %all-gather = bf16[8,1,1536]{2,1,0:T(2,128)(2,1)S(1)} all-gather(bf16[1,1,1536]{2,1,0:T(2,128)(2,1)S(1)} %bitcast.270), channel_id=1, replica_groups=mesh['x'=2,'core'=2,'shard'=8] {'shard'}, dimensions={0}, use_global_device_ids=true | all-gather | bytes 27648 | tf_op jit(solution)/shard_map/all_gather | solution.py:849
  62.8 4.6 collective-permute-done.9
  72.4 10.3 %collective-permute-done.10 = bf16[4,32,2048]{2,1,0:T(8,128)(2,1)S(1)} collective-permute-done((bf16[4,32,2048]{2,1,0:T(8,128)(2,1)S(1)}, bf16[4,32,2048]{2,1,0:T(8,128)(2,1)S(1)}, u32[]{:S(2)}, u32[]{:S(2)}) %collective-permute-start.10) | collective-permute-done | bytes 524320 | tf_op jit(solution)/shard_map/ppermute | solution.py:719
  96.2 3.1 pad_maximum_fusion.tokens
  99.3 4.1 collective-permute-done.5.rest_2_.rest_6_
  103.3 7.0 %collective-permute-done.6.rest_3_.rest_7_ = bf16[4,32,2048]{2,1,0:T(8,128)(2,1)S(1)} collective-permute-done((bf16[4,32,2048]{2,1,0:T(8,128)(2,1)}, bf16[4,32,2048]{2,1,0:T(8,128)(2,1)S(1)}, u32[]{:S(2)}, u32[]{:S(2)}) %collective-permute-start.6) | collective-permute-done | bytes 524320 | tf_op jit(solution)/shard_map/ppermute | solution.py:719
  110.8 2.4 collective-permute-start.23
  113.2 11.3 %joint_rows.1 = (bf16[1280,1024]{1,0:T(8,128)(2,1)}, bf16[1280,1536]{1,0:T(8,128)(2,1)}, bf16[1024,512]{1,0:T(8,128)(2,1)}) custom-call(s32[32]{0:T(128)} %stack.378.table, bf16[1280,1024]{1,0:T(8,128)(2,1)} %pad_maximum_fusion.tokens, f32[1,1024]{1,0:T(1,128)} %bitcast.274, f32[1,1024]{1,0:T(1,128)} %bitcast.273, f32[1,1536]{1,0:T(1,128)} %reshape.368.bias, ...), custom_call_target="tpu_custom_call" | custom-call | flops 4026531840 | bytes 12320768 | tf_op jit(solution)/shard_map/joint_rows/pallas_call | solution.py:109
  126.5 9.8 %attend.3 = (bf16[640,512]{1,0:T(8,128)(2,1)}, f32[2,4,2,320]{3,2,1,0:T(2,128)}) custom-call(s32[4]{0:T(128)} %pad_add_fusion.lengths, bf16[1280,1536]{1,0:T(8,128)(2,1)} %get-tuple-element.55.q_ref.k_ref.v_ref, bf16[1280,1536]{1,0:T(8,128)(2,1)} %get-tuple-element.55.q_ref.k_ref.v_ref, bf16[1280,1536]{1,0:T(8,128)(2,1)} %get-tuple-element.55.q_ref.k_ref.v_ref), custom_call_target="tpu_custom_call" | custom-call | flops 838860800 | bytes 2621440 | tf_op jit(solution)/shard_map/attend/pallas_call | solution.py:174
  138.9 2.8 collective-permute-start.18
  142.7 9.6 %attend.2 = (bf16[640,512]{1,0:T(8,128)(2,1)}, f32[2,4,2,320]{3,2,1,0:T(2,128)}) custom-call(s32[4]{0:T(128)} %pad_add_fusion.lengths, bf16[1280,1536]{1,0:T(8,128)(2,1)} %get-tuple-element.55.q_ref.k_ref.v_ref, bf16[1280,1536]{1,0:T(8,128)(2,1)} %get-tuple-element.55.q_ref.k_ref.v_ref, bf16[1280,1536]{1,0:T(8,128)(2,1)} %get-tuple-element.55.q_ref.k_ref.v_ref), custom_call_target="tpu_custom_call" | custom-call | flops 838860800 | bytes 2621440 | tf_op jit(solution)/shard_map/attend/pallas_call | solution.py:174
  153.3 5.7 %mixer.1 = (f32[640,1024]{1,0:T(8,128)}, bf16[640,1024]{1,0:T(8,128)(2,1)}) custom-call(s32[1]{0:T(128)} %bitcast.core, bf16[640,512]{1,0:T(8,128)(2,1)} %get-tuple-element.56.mine, bf16[640,512]{1,0:T(8,128)(2,1)} %collective-permute-done.12.other, bf16[1024,512]{1,0:T(8,128)(2,1)} %get-tuple-element.58.m_mine, bf16[1024,512]{1,0:T(8,128)(2,1)} %copy-done.17, ...), custom_call_target="tpu_custom_call" | custom-call | flops 1342177280 | bytes 6553600 | tf_op jit(solution)/shard_map/mixer/pallas_call | solution.py:214
  162.5 5.1 collective-permute-done.18.rest_1_
  172.2 3.3 maximum_multiply_fusion.grad
  175.5 26.0 %collective-permute-done.19.rest_2_ = bf16[4,64,2048]{2,1,0:T(8,128)(2,1)} collective-permute-done((bf16[4,64,2048]{2,1,0:T(8,128)(2,1)}, bf16[4,64,2048]{2,1,0:T(8,128)(2,1)}, u32[]{:S(2)}, u32[]{:S(2)}) %collective-permute-start.19) | collective-permute-done | bytes 1048608 | tf_op jit(solution)/shard_map/ppermute | solution.py:719
  201.5 10.2 %collective-permute-done.20.rest_3_ = bf16[4,64,2048]{2,1,0:T(8,128)(2,1)} collective-permute-done((bf16[4,64,2048]{2,1,0:T(8,128)(2,1)}, bf16[4,64,2048]{2,1,0:T(8,128)(2,1)}, u32[]{:S(2)}, u32[]{:S(2)}) %collective-permute-start.20) | collective-permute-done | bytes 1048608 | tf_op jit(solution)/shard_map/ppermute | solution.py:719
  211.7 28.0 %expand_and_dreduce.1 = (bf16[1280,2048]{1,0:T(8,128)(2,1)}, bf16[1280,2048]{1,0:T(8,128)(2,1)}, bf16[8,128,1024]{2,1,0:T(8,128)(2,1)}, bf16[8,128,1024]{2,1,0:T(8,128)(2,1)}) custom-call(s32[16]{0:T(128)} %stack.405.load_table.expand_table, s32[16]{0:T(128)} %stack.406.store_table, bf16[640,1024]{1,0:T(8,128)(2,1)} %get-tuple-element.61.n_own, ...), custom_call_target="tpu_custom_call" | custom-call | flops 10737418240 | bytes 24117248 | tf_op jit(solution)/shard_map/expand_and_dreduce/pallas_call | solution.py:285
  239.7 36.5 %grad_before.1 = (bf16[1280,2048]{1,0:T(8,128)(2,1)}, f32[1,2048]{1,0:T(1,128)}, bf16[640,1024]{1,0:T(8,128)(2,1)}, f32[640,1024]{1,0:T(8,128)}) custom-call(s32[16]{0:T(128)} %stack.405.load_table.expand_table, s32[16]{0:T(128)} %stack.403.reduce_table.table, bf16[1280,1024]{1,0:T(8,128)(2,1)} %maximum_multiply_fusion.grad, ...), custom_call_target="tpu_custom_call" | custom-call | flops 10737418240 | bytes 24117248 | tf_op jit(solution)/shard_map/grad_before/pallas_call | solution.py:363
  276.4 13.2 %dexpand.1 = (bf16[4,64,2048]{2,1,0:T(8,128)(2,1)}, bf16[4,64,2048]{2,1,0:T(8,128)(2,1)}, bf16[4,64,2048]{2,1,0:T(8,128)(2,1)}, bf16[4,64,2048]{2,1,0:T(8,128)(2,1)}) custom-call(s32[16]{0:T(128)} %stack.420.store_table, bf16[640,1024]{1,0:T(8,128)(2,1)} %get-tuple-element.61.n_own, bf16[640,1024]{1,0:T(8,128)(2,1)} %collective-permute-done.15.n_far, ...), custom_call_target="tpu_custom_call" | custom-call | flops 5368709120 | bytes 12058624 | tf_op jit(solution)/shard_map/dexpand/pallas_call | solution.py:419
  295.3 2.8 collective-permute-start.45
  299.2 8.4 %grad_attended.1 = (f32[640,1024]{1,0:T(8,128)}, bf16[640,1024]{1,0:T(8,128)(2,1)}, bf16[640,512]{1,0:T(8,128)(2,1)}, bf16[640,512]{1,0:T(8,128)(2,1)}, f32[3,1024]{1,0:T(4,128)}) custom-call(s32[1]{0:T(128)} %bitcast.core, f32[640,1024]{1,0:T(8,128)} %get-tuple-element.63.g_own, bf16[640,1024]{1,0:T(8,128)(2,1)} %copy-done.15, ...), custom_call_target="tpu_custom_call" | custom-call | flops 1342177280 | bytes 11796480 | tf_op jit(solution)/shard_map/grad_attended/pallas_call | solution.py:487
  307.6 10.5 %collective-permute-done.43 = bf16[4,64,2048]{2,1,0:T(8,128)(2,1)} collective-permute-done((bf16[4,64,2048]{2,1,0:T(8,128)(2,1)}, bf16[4,64,2048]{2,1,0:T(8,128)(2,1)}, u32[]{:S(2)}, u32[]{:S(2)}) %collective-permute-start.43) | collective-permute-done | bytes 1048608 | tf_op jit(solution)/shard_map/ppermute | solution.py:719
  319.7 10.2 %collective-permute-start.44 = (bf16[4,64,2048]{2,1,0:T(8,128)(2,1)S(1)}, bf16[4,64,2048]{2,1,0:T(8,128)(2,1)}, u32[]{:S(2)}, u32[]{:S(2)}) collective-permute-start(bf16[4,64,2048]{2,1,0:T(8,128)(2,1)S(1)} %add_convert_fusion.3), channel_id=1, source_target_pairs={{0,2},{1,3},{2,4},{3,5},{4,6},{5,7},{6,0},{7,1},{8,14},{9,15},{10,... | collective-permute-start | bytes 3145736 | tf_op jit(solution)/shard_map/ppermute | solution.py:719
  329.8 4.5 dmixer.1
  334.3 2.9 collective-permute-start.28
  337.2 12.5 %attend_back.2 = (bf16[640,512]{1,0:T(8,128)(2,1)}, bf16[640,512]{1,0:T(8,128)(2,1)}, bf16[640,512]{1,0:T(8,128)(2,1)}) custom-call(s32[4]{0:T(128)} %pad_add_fusion.lengths, bf16[1280,1536]{1,0:T(8,128)(2,1)} %get-tuple-element.55.q_ref.k_ref.v_ref, bf16[1280,1536]{1,0:T(8,128)(2,1)} %get-tuple-element.55.q_ref.k_ref.v_ref, ...), custom_call_target="tpu_custom_call" | custom-call | flops 2097152000 | bytes 4587520 | tf_op jit(solution)/shard_map/attend_back/pallas_call | solution.py:576
  350.6 12.6 %attend_back.3 = (bf16[640,512]{1,0:T(8,128)(2,1)}, bf16[640,512]{1,0:T(8,128)(2,1)}, bf16[640,512]{1,0:T(8,128)(2,1)}) custom-call(s32[4]{0:T(128)} %pad_add_fusion.lengths, bf16[1280,1536]{1,0:T(8,128)(2,1)} %get-tuple-element.55.q_ref.k_ref.v_ref, bf16[1280,1536]{1,0:T(8,128)(2,1)} %get-tuple-element.55.q_ref.k_ref.v_ref, ...), custom_call_target="tpu_custom_call" | custom-call | flops 2097152000 | bytes 4587520 | tf_op jit(solution)/shard_map/attend_back/pallas_call | solution.py:576
  363.2 3.6 add_convert_fusion.2
  366.8 2.4 collective-permute-start.51
  369.2 2.9 add_convert_fusion.5
  372.1 12.8 %djoint.1 = (f32[3,512]{1,0:T(4,128)}, bf16[4,32,2048]{2,1,0:T(8,128)(2,1)}, bf16[4,32,2048]{2,1,0:T(8,128)(2,1)}, bf16[4,32,2048]{2,1,0:T(8,128)(2,1)}, bf16[4,...) custom-call(s32[32]{0:T(128)} %stack.404.store_table, ...), custom_call_target="tpu_custom_call" | custom-call | flops 4026531840 | bytes 10747904 | tf_op jit(solution)/shard_map/djoint/pallas_call | solution.py:627
  384.9 3.1 collective-permute-start.31
  392.3 7.0 %grad_rows_far.1 = bf16[640,1024]{1,0:T(8,128)(2,1)} custom-call(s32[32]{0:T(128)} %stack.378.table, bf16[4,32,2048]{2,1,0:T(8,128)(2,1)} %get-tuple-element.78.rest_0_, bf16[640,512]{1,0:T(8,128)(2,1)} %get-tuple-element.72.rest_3_.rest_1_, bf16[640,512]{1,0:T(8,128)(2,1)} %get-tuple-element.73.rest_4_.rest_2_, ...), custom_call_target="tpu_custom_call" | custom-call | flops 2013265920 | bytes 7733248 | tf_op jit(solution)/shard_map/grad_rows_far/pallas_call | solution.py:677
  399.4 8.3 %branch.1 = f32[640,1024]{1,0:T(8,128)} custom-call(s32[16]{0:T(128)} %stack.403.reduce_table.table, bf16[4,32,2048]{2,1,0:T(8,128)(2,1)} %get-tuple-element.78.rest_0_, bf16[1280,2048]{1,0:T(8,128)(2,1)} %get-tuple-element.79.rest_1_, bf16[8,128,1024]{2,1,0:T(8,128)(2,1)} %copy-done.7, bf16[8,128,1024]{2,1,0:T(8,128)(2,1)} %collective-permute-done.25.rest_5_.rest_3_), custom_call_target="tpu_custom_call" | custom-call | flops 2684354560 | bytes 9437184 | tf_op jit(solution)/shard_map/branch/pallas_call | solution.py:677
  407.7 7.2 %grad_rows.1 = f32[640,1024]{1,0:T(8,128)} custom-call(s32[32]{0:T(128)} %stack.378.table, bf16[4,32,2048]{2,1,0:T(8,128)(2,1)} %get-tuple-element.78.rest_0_, bf16[640,512]{1,0:T(8,128)(2,1)} %get-tuple-element.67.rest_0_.rest_1_, bf16[640,512]{1,0:T(8,128)(2,1)} %get-tuple-element.68.rest_1_.rest_2_, bf16[640,512]{1,0:T(8,128)(2,1)} %get-tuple-element.69.rest_2_.rest_3_, ...), custom_call_target="tpu_custom_call" | custom-call | flops 2013265920 | bytes 7733248 | tf_op jit(solution)/shard_map/grad_rows/pallas_call | solution.py:677
  415.0 8.1 %branch_far.1 = bf16[640,1024]{1,0:T(8,128)(2,1)} custom-call(s32[16]{0:T(128)} %stack.403.reduce_table.table, bf16[4,32,2048]{2,1,0:T(8,128)(2,1)} %get-tuple-element.78.rest_0_, bf16[1280,2048]{1,0:T(8,128)(2,1)} %get-tuple-element.79.rest_1_, bf16[8,128,1024]{2,1,0:T(8,128)(2,1)} %copy-done.7, bf16[8,128,1024]{2,1,0:T(8,128)(2,1)} %collective-permute-done.25.rest_5_.rest_3_), custom_call_target="tpu_custom_call" | custom-call | flops 2684354560 | bytes 9437184 | tf_op jit(solution)/shard_map/branch_far/pallas_call | solution.py:677
  427.1 3.7 collective-permute-done.47
  436.9 2.4 add_convert_fusion.7
  439.3 14.4 %collective-permute-done.53 = bf16[128,1024]{1,0:T(8,128)(2,1)S(1)} collective-permute-done((bf16[128,1024]{1,0:T(8,128)(2,1)S(1)}, bf16[128,1024]{1,0:T(8,128)(2,1)S(1)}, u32[]{:S(2)}, u32[]{:S(2)}) %collective-permute-start.53) | collective-permute-done | bytes 262176 | tf_op jit(solution)/shard_map/ppermute | solution.py:719
  468.4 39.5 %psum.7 = f32[8,1536]{1,0:T(8,128)S(1)} all-reduce(f32[8,1536]{1,0:T(8,128)S(1)} %constant_dynamic-update-slice_fusion.18), channel_id=1, replica_groups=mesh['x'=2,'core'=2,'shard'=8] {'x','core','shard'}, use_global_device_ids=true, to_apply=%region_7.8 | all-reduce | flops 12288 | bytes 98304 | tf_op jit(solution)/shard_map/psum | solution.py:859
  519.2 4.0 collective-permute-done.39
  525.8 5.4 collective-permute-done.40
  532.5 6.1 %collective-permute-done.41 = bf16[64,2048]{1,0:T(8,128)(2,1)S(1)} collective-permute-done((bf16[64,2048]{1,0:T(8,128)(2,1)S(1)}, bf16[64,2048]{1,0:T(8,128)(2,1)S(1)}, u32[]{:S(2)}, u32[]{:S(2)}) %collective-permute-start.41) | collective-permute-done | bytes 262176 | tf_op jit(solution)/shard_map/ppermute | solution.py:719
  544.4 3.0 copy.43
  547.4 4.0 reshape.384
  554.5 2.9 copy.41
  557.4 3.0 copy.44
  (284 shorter events, 123.3 us)
Async XLA Ops:
  9.0 49.1 %collective-permute-start.7 = (bf16[32,2048]{1,0:T(8,128)(2,1)}, bf16[32,2048]{1,0:T(8,128)(2,1)}, u32[]{:S(2)}, u32[]{:S(2)}) collective-permute-start(bf16[32,2048]{1,0:T(8,128)(2,1)} %get-tuple-element.131), channel_id=1, source_target_pairs={{0,2},{1,3},{2,4},{3,5},{4,6},{5,7},{6,0},{7,1},{8,14},{9,15},{10,... | collective-permute-start | bytes 393224 | tf_op jit(solution)/shard_map/ppermute | solution.py:719
  12.0 48.1 %collective-permute-start.8 = (bf16[32,2048]{1,0:T(8,128)(2,1)}, bf16[32,2048]{1,0:T(8,128)(2,1)}, u32[]{:S(2)}, u32[]{:S(2)}) collective-permute-start(bf16[32,2048]{1,0:T(8,128)(2,1)} %get-tuple-element.131), channel_id=1, source_target_pairs={{0,6},{1,7},{2,0},{3,1},{4,2},{5,3},{6,4},{7,5},{8,10},{9,11},{10,... | collective-permute-start | bytes 393224 | tf_op jit(solution)/shard_map/ppermute | solution.py:719
  14.0 43.1 %collective-permute-start.2 = (bf16[32,2048]{1,0:T(8,128)(2,1)S(1)}, bf16[32,2048]{1,0:T(8,128)(2,1)}, u32[]{:S(2)}, u32[]{:S(2)}) collective-permute-start(bf16[32,2048]{1,0:T(8,128)(2,1)S(1)} %fusion.20), channel_id=1, source_target_pairs={{0,16},{1,17},{2,18},{3,19},{4,20},{5,21},{6,22},{7,23},{8,9},{9,8... | collective-permute-start | bytes 393224 | tf_op jit(solution)/shard_map/ppermute | solution.py:719
  15.8 78.4 %collective-permute-start.1 = (bf16[640,1024]{1,0:T(8,128)(2,1)S(1)}, bf16[640,1024]{1,0:T(8,128)(2,1)}, u32[]{:S(2)}, u32[]{:S(2)}) collective-permute-start(bf16[640,1024]{1,0:T(8,128)(2,1)S(1)} %bitcast.233), channel_id=1, source_target_pairs={{0,8},{8,0},{1,9},{9,1},{2,10},{10,2},{3,11},{11,3},{4,12},{12,4},... | collective-permute-start | bytes 3932168 | tf_op jit(solution)/shard_map/ppermute | solution.py:825
  20.4 70.7 %collective-permute-start.16 = (bf16[64,2048]{1,0:T(8,128)(2,1)}, bf16[64,2048]{1,0:T(8,128)(2,1)}, u32[]{:S(2)}, u32[]{:S(2)}) collective-permute-start(bf16[64,2048]{1,0:T(8,128)(2,1)} %bitcast.141), channel_id=1, source_target_pairs={{0,16},{1,17},{2,18},{3,19},{4,20},{5,21},{6,22},{7,23},{8,9},{9,8... | collective-permute-start | bytes 786440 | tf_op jit(solution)/shard_map/ppermute | solution.py:719
  57.1 42.2 %collective-permute-start.21 = (bf16[128,1024]{1,0:T(8,128)(2,1)}, bf16[128,1024]{1,0:T(8,128)(2,1)}, u32[]{:S(2)}, u32[]{:S(2)}) collective-permute-start(bf16[128,1024]{1,0:T(8,128)(2,1)} %get-tuple-element.129), channel_id=1, source_target_pairs={{0,2},{1,3},{2,4},{3,5},{4,6},{5,7},{6,0},{7,1},{8,14},{9,15},{10,... | collective-permute-start | bytes 786440 | tf_op jit(solution)/shard_map/ppermute | solution.py:719
  58.0 12.6 %collective-permute-start.3 = (bf16[2,32,2048]{2,1,0:T(8,128)(2,1)S(1)}, bf16[2,32,2048]{2,1,0:T(8,128)(2,1)S(1)}, u32[]{:S(2)}, u32[]{:S(2)}) collective-permute-start(bf16[2,32,2048]{2,1,0:T(8,128)(2,1)S(1)} %pad_maximum_fusion.11), channel_id=1, source_target_pairs={{0,1},{1,0},{2,3},{3,2},{4,5},{5,4},{6,7},{7,6},{8,24},{9,25},{10,... | collective-permute-start | bytes 786440 | tf_op jit(solution)/shard_map/ppermute | solution.py:719
  68.5 14.1 %collective-permute-start.10 = (bf16[4,32,2048]{2,1,0:T(8,128)(2,1)S(1)}, bf16[4,32,2048]{2,1,0:T(8,128)(2,1)S(1)}, u32[]{:S(2)}, u32[]{:S(2)}) collective-permute-start(bf16[4,32,2048]{2,1,0:T(8,128)(2,1)S(1)} %pad_maximum_fusion.5), channel_id=1, source_target_pairs={{0,1},{1,0},{2,3},{3,2},{4,5},{5,4},{6,7},{7,6},{8,24},{9,25},{10,... | collective-permute-start | bytes 1572872 | tf_op jit(solution)/shard_map/ppermute | solution.py:719
  72.3 18.8 %collective-permute-start.4 = (bf16[4,32,2048]{2,1,0:T(8,128)(2,1)}, bf16[4,32,2048]{2,1,0:T(8,128)(2,1)}, u32[]{:S(2)}, u32[]{:S(2)}) collective-permute-start(bf16[4,32,2048]{2,1,0:T(8,128)(2,1)} %pad_maximum_fusion.4.rest_0_.rest_4_), channel_id=1, source_target_pairs={{0,2},{1,3},{2,4},{3,5},{4,6},{5,7},{6,0},{7,1},{8,14},{9,15},{10,... | collective-permute-start | bytes 1572872 | tf_op jit(solution)/shard_map/ppermute | solution.py:719
  83.5 27.3 %collective-permute-start.11 = (bf16[8,32,2048]{2,1,0:T(8,128)(2,1)}, bf16[8,32,2048]{2,1,0:T(8,128)(2,1)}, u32[]{:S(2)}, u32[]{:S(2)}) collective-permute-start(bf16[8,32,2048]{2,1,0:T(8,128)(2,1)} %constant_dynamic-update-slice_fusion.8.rest_4_.rest_8_), channel_id=1, source_target_pairs={{0,16},{1,17},{2,18},{3,19},{4,20},{5,21},{6,22},{7,23},{8,9},{9,8... | collective-permute-start | bytes 3145736 | tf_op jit(solution)/shard_map/ppermute | solution.py:719
  91.1 12.2 %collective-permute-start.5 = (bf16[4,32,2048]{2,1,0:T(8,128)(2,1)}, bf16[4,32,2048]{2,1,0:T(8,128)(2,1)S(1)}, u32[]{:S(2)}, u32[]{:S(2)}) collective-permute-start(bf16[4,32,2048]{2,1,0:T(8,128)(2,1)} %pad_maximum_fusion.4.rest_0_.rest_4_), channel_id=1, source_target_pairs={{0,6},{1,7},{2,0},{3,1},{4,2},{5,3},{6,4},{7,5},{8,10},{9,11},{10,... | collective-permute-start | bytes 1572872 | tf_op jit(solution)/shard_map/ppermute | solution.py:719
  91.1 19.2 %collective-permute-start.6 = (bf16[4,32,2048]{2,1,0:T(8,128)(2,1)}, bf16[4,32,2048]{2,1,0:T(8,128)(2,1)S(1)}, u32[]{:S(2)}, u32[]{:S(2)}) collective-permute-start(bf16[4,32,2048]{2,1,0:T(8,128)(2,1)} %collective-permute-done.4.rest_1_.rest_5_), channel_id=1, source_target_pairs={{0,2},{1,3},{2,4},{3,5},{4,6},{5,7},{6,0},{7,1},{8,14},{9,15},{10,... | collective-permute-start | bytes 1572872 | tf_op jit(solution)/shard_map/ppermute | solution.py:719
  94.3 31.0 %collective-permute-start.22 = (bf16[128,1024]{1,0:T(8,128)(2,1)}, bf16[128,1024]{1,0:T(8,128)(2,1)S(1)}, u32[]{:S(2)}, u32[]{:S(2)}) collective-permute-start(bf16[128,1024]{1,0:T(8,128)(2,1)} %get-tuple-element.129), channel_id=1, source_target_pairs={{0,6},{1,7},{2,0},{3,1},{4,2},{5,3},{6,4},{7,5},{8,10},{9,11},{10,... | collective-permute-start | bytes 786440 | tf_op jit(solution)/shard_map/ppermute | solution.py:719
  99.3 25.3 %collective-permute-start = (s32[2]{0:T(128)S(1)}, s32[2]{0:T(128)S(1)}, u32[]{:S(2)}, u32[]{:S(2)}) collective-permute-start(s32[2]{0:T(128)S(1)} %copy-done.33), channel_id=1, source_target_pairs={{0,8},{8,0},{1,9},{9,1},{2,10},{10,2},{3,11},{11,3},{4,12},{12,4},... | collective-permute-start | bytes 32 | tf_op jit(solution)/shard_map/ppermute | solution.py:825
  103.3 68.9 %collective-permute-start.14 = (bf16[640,1024]{1,0:T(8,128)(2,1)}, bf16[640,1024]{1,0:T(8,128)(2,1)S(1)}, u32[]{:S(2)}, u32[]{:S(2)}) collective-permute-start(bf16[640,1024]{1,0:T(8,128)(2,1)} %bitcast.68.cotangent), channel_id=1, source_target_pairs={{0,8},{8,0},{1,9},{9,1},{2,10},{10,2},{3,11},{11,3},{4,12},{12,4},... | collective-permute-start | bytes 3932168 | tf_op jit(solution)/shard_map/ppermute | solution.py:825
  110.3 26.4 %collective-permute-start.17 = (bf16[2,64,2048]{2,1,0:T(8,128)(2,1)S(1)}, bf16[2,64,2048]{2,1,0:T(8,128)(2,1)}, u32[]{:S(2)}, u32[]{:S(2)}) collective-permute-start(bf16[2,64,2048]{2,1,0:T(8,128)(2,1)S(1)} %pad_maximum_fusion.6), channel_id=1, source_target_pairs={{0,1},{1,0},{2,3},{3,2},{4,5},{5,4},{6,7},{7,6},{8,24},{9,25},{10,... | collective-permute-start | bytes 1572872 | tf_op jit(solution)/shard_map/ppermute | solution.py:719
  110.8 14.4 %collective-permute-start.23 = (bf16[128,1024]{1,0:T(8,128)(2,1)}, bf16[128,1024]{1,0:T(8,128)(2,1)S(1)}, u32[]{:S(2)}, u32[]{:S(2)}) collective-permute-start(bf16[128,1024]{1,0:T(8,128)(2,1)} %collective-permute-done.21), channel_id=1, source_target_pairs={{0,2},{1,3},{2,4},{3,5},{4,6},{5,7},{6,0},{7,1},{8,14},{9,15},{10,... | collective-permute-start | bytes 786440 | tf_op jit(solution)/shard_map/ppermute | solution.py:719
  124.6 27.8 %collective-permute-start.13 = (bf16[1024,512]{1,0:T(8,128)(2,1)}, bf16[1024,512]{1,0:T(8,128)(2,1)S(1)}, u32[]{:S(2)}, u32[]{:S(2)}) collective-permute-start(bf16[1024,512]{1,0:T(8,128)(2,1)} %get-tuple-element.58.m_mine), channel_id=1, source_target_pairs={{0,8},{8,0},{1,9},{9,1},{2,10},{10,2},{3,11},{11,3},{4,12},{12,4},... | collective-permute-start | bytes 3145736 | tf_op jit(solution)/shard_map/ppermute | solution.py:825
  126.4 34.2 %collective-permute-start.24 = (bf16[4,128,1024]{2,1,0:T(8,128)(2,1)S(1)}, bf16[4,128,1024]{2,1,0:T(8,128)(2,1)S(1)}, u32[]{:S(2)}, u32[]{:S(2)}) collective-permute-start(bf16[4,128,1024]{2,1,0:T(8,128)(2,1)S(1)} %pad_maximum_fusion.2), channel_id=1, source_target_pairs={{0,1},{1,0},{2,3},{3,2},{4,5},{5,4},{6,7},{7,6},{8,24},{9,25},{10,... | collective-permute-start | bytes 3145736 | tf_op jit(solution)/shard_map/ppermute | solution.py:719
  136.3 16.1 %collective-permute-start.12 = (bf16[640,512]{1,0:T(8,128)(2,1)}, bf16[640,512]{1,0:T(8,128)(2,1)}, u32[]{:S(2)}, u32[]{:S(2)}) collective-permute-start(bf16[640,512]{1,0:T(8,128)(2,1)} %get-tuple-element.57), channel_id=1, source_target_pairs={{0,8},{8,0},{1,9},{9,1},{2,10},{10,2},{3,11},{11,3},{4,12},{12,4},... | collective-permute-start | bytes 1966088 | tf_op jit(solution)/shard_map/ppermute | solution.py:825
  138.9 28.7 %collective-permute-start.18 = (bf16[4,64,2048]{2,1,0:T(8,128)(2,1)}, bf16[4,64,2048]{2,1,0:T(8,128)(2,1)}, u32[]{:S(2)}, u32[]{:S(2)}) collective-permute-start(bf16[4,64,2048]{2,1,0:T(8,128)(2,1)} %pad_maximum_fusion.1.rest_0_), channel_id=1, source_target_pairs={{0,2},{1,3},{2,4},{3,5},{4,6},{5,7},{6,0},{7,1},{8,14},{9,15},{10,... | collective-permute-start | bytes 3145736 | tf_op jit(solution)/shard_map/ppermute | solution.py:719
  159.1 52.6 %collective-permute-start.15 = (bf16[640,1024]{1,0:T(8,128)(2,1)}, bf16[640,1024]{1,0:T(8,128)(2,1)}, u32[]{:S(2)}, u32[]{:S(2)}) collective-permute-start(bf16[640,1024]{1,0:T(8,128)(2,1)} %get-tuple-element.61.n_own), channel_id=1, source_target_pairs={{0,8},{8,0},{1,9},{9,1},{2,10},{10,2},{3,11},{11,3},{4,12},{12,4},... | collective-permute-start | bytes 3932168 | tf_op jit(solution)/shard_map/ppermute | solution.py:825
  159.6 42.0 %collective-permute-start.19 = (bf16[4,64,2048]{2,1,0:T(8,128)(2,1)}, bf16[4,64,2048]{2,1,0:T(8,128)(2,1)}, u32[]{:S(2)}, u32[]{:S(2)}) collective-permute-start(bf16[4,64,2048]{2,1,0:T(8,128)(2,1)} %pad_maximum_fusion.1.rest_0_), channel_id=1, source_target_pairs={{0,6},{1,7},{2,0},{3,1},{4,2},{5,3},{6,4},{7,5},{8,10},{9,11},{10,... | collective-permute-start | bytes 3145736 | tf_op jit(solution)/shard_map/ppermute | solution.py:719
  160.7 79.0 %collective-permute-start.25 = (bf16[8,128,1024]{2,1,0:T(8,128)(2,1)S(1)}, bf16[8,128,1024]{2,1,0:T(8,128)(2,1)}, u32[]{:S(2)}, u32[]{:S(2)}) collective-permute-start(bf16[8,128,1024]{2,1,0:T(8,128)(2,1)S(1)} %constant_dynamic-update-slice_fusion.13.rest_4_.rest_2_), channel_id=1, source_target_pairs={{0,16},{1,17},{2,18},{3,19},{4,20},{5,21},{6,22},{7,23},{8,9},{9,8... | collective-permute-start | bytes 6291464 | tf_op jit(solution)/shard_map/ppermute | solution.py:719
  167.6 44.1 %collective-permute-start.20 = (bf16[4,64,2048]{2,1,0:T(8,128)(2,1)}, bf16[4,64,2048]{2,1,0:T(8,128)(2,1)}, u32[]{:S(2)}, u32[]{:S(2)}) collective-permute-start(bf16[4,64,2048]{2,1,0:T(8,128)(2,1)} %collective-permute-done.18.rest_1_), channel_id=1, source_target_pairs={{0,2},{1,3},{2,4},{3,5},{4,6},{5,7},{6,0},{7,1},{8,14},{9,15},{10,... | collective-permute-start | bytes 3145736 | tf_op jit(solution)/shard_map/ppermute | solution.py:719
  276.3 21.8 %collective-permute-start.26 = (bf16[640,1024]{1,0:T(8,128)(2,1)}, bf16[640,1024]{1,0:T(8,128)(2,1)S(1)}, u32[]{:S(2)}, u32[]{:S(2)}) collective-permute-start(bf16[640,1024]{1,0:T(8,128)(2,1)} %get-tuple-element.64), channel_id=1, source_target_pairs={{0,8},{8,0},{1,9},{9,1},{2,10},{10,2},{3,11},{11,3},{4,12},{12,4},... | collective-permute-start | bytes 3932168 | tf_op jit(solution)/shard_map/ppermute | solution.py:825
  289.6 28.4 %collective-permute-start.43 = (bf16[4,64,2048]{2,1,0:T(8,128)(2,1)}, bf16[4,64,2048]{2,1,0:T(8,128)(2,1)}, u32[]{:S(2)}, u32[]{:S(2)}) collective-permute-start(bf16[4,64,2048]{2,1,0:T(8,128)(2,1)} %get-tuple-element.92), channel_id=1, source_target_pairs={{0,2},{1,3},{2,4},{3,5},{4,6},{5,7},{6,0},{7,1},{8,14},{9,15},{10,... | collective-permute-start | bytes 3145736 | tf_op jit(solution)/shard_map/ppermute | solution.py:719
  291.3 71.9 %collective-permute-start.50 = (bf16[8,128,1024]{2,1,0:T(8,128)(2,1)}, bf16[8,128,1024]{2,1,0:T(8,128)(2,1)}, u32[]{:S(2)}, u32[]{:S(2)}) collective-permute-start(bf16[8,128,1024]{2,1,0:T(8,128)(2,1)} %get-tuple-element.95), channel_id=1, source_target_pairs={{0,16},{1,17},{2,18},{3,19},{4,20},{5,21},{6,22},{7,23},{8,9},{9,8... | collective-permute-start | bytes 6291464 | tf_op jit(solution)/shard_map/ppermute | solution.py:719
  295.3 73.9 %collective-permute-start.45 = (bf16[4,64,2048]{2,1,0:T(8,128)(2,1)}, bf16[4,64,2048]{2,1,0:T(8,128)(2,1)}, u32[]{:S(2)}, u32[]{:S(2)}) collective-permute-start(bf16[4,64,2048]{2,1,0:T(8,128)(2,1)} %get-tuple-element.93), channel_id=1, source_target_pairs={{0,6},{1,7},{2,0},{3,1},{4,2},{5,3},{6,4},{7,5},{8,10},{9,11},{10,... | collective-permute-start | bytes 3145736 | tf_op jit(solution)/shard_map/ppermute | solution.py:719
  307.5 42.2 %collective-permute-start.27 = (bf16[640,512]{1,0:T(8,128)(2,1)}, bf16[640,512]{1,0:T(8,128)(2,1)S(1)}, u32[]{:S(2)}, u32[]{:S(2)}) collective-permute-start(bf16[640,512]{1,0:T(8,128)(2,1)} %get-tuple-element.70), channel_id=1, source_target_pairs={{0,8},{8,0},{1,9},{9,1},{2,10},{10,2},{3,11},{11,3},{4,12},{12,4},... | collective-permute-start | bytes 1966088 | tf_op jit(solution)/shard_map/ppermute | solution.py:825
  319.7 49.6 %collective-permute-start.44 = (bf16[4,64,2048]{2,1,0:T(8,128)(2,1)S(1)}, bf16[4,64,2048]{2,1,0:T(8,128)(2,1)}, u32[]{:S(2)}, u32[]{:S(2)}) collective-permute-start(bf16[4,64,2048]{2,1,0:T(8,128)(2,1)S(1)} %add_convert_fusion.3), channel_id=1, source_target_pairs={{0,2},{1,3},{2,4},{3,5},{4,6},{5,7},{6,0},{7,1},{8,14},{9,15},{10,... | collective-permute-start | bytes 3145736 | tf_op jit(solution)/shard_map/ppermute | solution.py:719
  334.3 37.8 %collective-permute-start.28 = (bf16[1024,512]{1,0:T(8,128)(2,1)}, bf16[1024,512]{1,0:T(8,128)(2,1)}, u32[]{:S(2)}, u32[]{:S(2)}) collective-permute-start(bf16[1024,512]{1,0:T(8,128)(2,1)} %get-tuple-element.77), channel_id=1, source_target_pairs={{0,8},{8,0},{1,9},{9,1},{2,10},{10,2},{3,11},{11,3},{4,12},{12,4},... | collective-permute-start | bytes 3145736 | tf_op jit(solution)/shard_map/ppermute | solution.py:825
  366.8 65.0 %collective-permute-start.51 = (bf16[4,128,1024]{2,1,0:T(8,128)(2,1)}, bf16[4,128,1024]{2,1,0:T(8,128)(2,1)}, u32[]{:S(2)}, u32[]{:S(2)}) collective-permute-start(bf16[4,128,1024]{2,1,0:T(8,128)(2,1)} %get-tuple-element.133), channel_id=1, source_target_pairs={{0,1},{1,0},{2,3},{3,2},{4,5},{5,4},{6,7},{7,6},{8,24},{9,25},{10,... | collective-permute-start | bytes 3145736 | tf_op jit(solution)/shard_map/ppermute | solution.py:719
  372.1 51.0 %collective-permute-start.46 = (bf16[2,64,2048]{2,1,0:T(8,128)(2,1)}, bf16[2,64,2048]{2,1,0:T(8,128)(2,1)}, u32[]{:S(2)}, u32[]{:S(2)}) collective-permute-start(bf16[2,64,2048]{2,1,0:T(8,128)(2,1)} %get-tuple-element.135), channel_id=1, source_target_pairs={{0,1},{1,0},{2,3},{3,2},{4,5},{5,4},{6,7},{7,6},{8,24},{9,25},{10,... | collective-permute-start | bytes 1572872 | tf_op jit(solution)/shard_map/ppermute | solution.py:719
  384.9 39.4 %collective-permute-start.31 = (bf16[4,32,2048]{2,1,0:T(8,128)(2,1)}, bf16[4,32,2048]{2,1,0:T(8,128)(2,1)}, u32[]{:S(2)}, u32[]{:S(2)}) collective-permute-start(bf16[4,32,2048]{2,1,0:T(8,128)(2,1)} %get-tuple-element.78.rest_0_), channel_id=1, source_target_pairs={{0,2},{1,3},{2,4},{3,5},{4,6},{5,7},{6,0},{7,1},{8,14},{9,15},{10,... | collective-permute-start | bytes 1572872 | tf_op jit(solution)/shard_map/ppermute | solution.py:719
  388.0 68.7 %collective-permute-start.33 = (bf16[4,32,2048]{2,1,0:T(8,128)(2,1)}, bf16[4,32,2048]{2,1,0:T(8,128)(2,1)}, u32[]{:S(2)}, u32[]{:S(2)}) collective-permute-start(bf16[4,32,2048]{2,1,0:T(8,128)(2,1)} %get-tuple-element.86), channel_id=1, source_target_pairs={{0,6},{1,7},{2,0},{3,1},{4,2},{5,3},{6,4},{7,5},{8,10},{9,11},{10,... | collective-permute-start | bytes 1572872 | tf_op jit(solution)/shard_map/ppermute | solution.py:719
  390.2 44.8 %collective-permute-start.36 = (bf16[8,32,2048]{2,1,0:T(8,128)(2,1)}, bf16[8,32,2048]{2,1,0:T(8,128)(2,1)}, u32[]{:S(2)}, u32[]{:S(2)}) collective-permute-start(bf16[8,32,2048]{2,1,0:T(8,128)(2,1)} %get-tuple-element.88), channel_id=1, source_target_pairs={{0,16},{1,17},{2,18},{3,19},{4,20},{5,21},{6,22},{7,23},{8,9},{9,8... | collective-permute-start | bytes 3145736 | tf_op jit(solution)/shard_map/ppermute | solution.py:719
  423.2 37.8 %collective-permute-start.30 = (bf16[640,1024]{1,0:T(8,128)(2,1)}, bf16[640,1024]{1,0:T(8,128)(2,1)S(1)}, u32[]{:S(2)}, u32[]{:S(2)}) collective-permute-start(bf16[640,1024]{1,0:T(8,128)(2,1)} %grad_rows_far.1), channel_id=1, source_target_pairs={{0,8},{8,0},{1,9},{9,1},{2,10},{10,2},{3,11},{11,3},{4,12},{12,4},... | collective-permute-start | bytes 3932168 | tf_op jit(solution)/shard_map/ppermute | solution.py:825
  430.8 34.8 %collective-permute-start.29 = (bf16[640,1024]{1,0:T(8,128)(2,1)S(1)}, bf16[640,1024]{1,0:T(8,128)(2,1)S(1)}, u32[]{:S(2)}, u32[]{:S(2)}) collective-permute-start(bf16[640,1024]{1,0:T(8,128)(2,1)S(1)} %copy-done.16), channel_id=1, source_target_pairs={{0,8},{8,0},{1,9},{9,1},{2,10},{10,2},{3,11},{11,3},{4,12},{12,4},... | collective-permute-start | bytes 3932168 | tf_op jit(solution)/shard_map/ppermute | solution.py:825
  431.9 27.0 %collective-permute-start.32 = (bf16[4,32,2048]{2,1,0:T(8,128)(2,1)S(1)}, bf16[4,32,2048]{2,1,0:T(8,128)(2,1)S(1)}, u32[]{:S(2)}, u32[]{:S(2)}) collective-permute-start(bf16[4,32,2048]{2,1,0:T(8,128)(2,1)S(1)} %add_convert_fusion.8), channel_id=1, source_target_pairs={{0,2},{1,3},{2,4},{3,5},{4,6},{5,7},{6,0},{7,1},{8,14},{9,15},{10,... | collective-permute-start | bytes 1572872 | tf_op jit(solution)/shard_map/ppermute | solution.py:719
  434.9 18.8 %collective-permute-start.53 = (bf16[128,1024]{1,0:T(8,128)(2,1)S(1)}, bf16[128,1024]{1,0:T(8,128)(2,1)S(1)}, u32[]{:S(2)}, u32[]{:S(2)}) collective-permute-start(bf16[128,1024]{1,0:T(8,128)(2,1)S(1)} %get-tuple-element.137), channel_id=1, source_target_pairs={{0,2},{1,3},{2,4},{3,5},{4,6},{5,7},{6,0},{7,1},{8,14},{9,15},{10,... | collective-permute-start | bytes 786440 | tf_op jit(solution)/shard_map/ppermute | solution.py:719
  453.8 78.7 %collective-permute-start.48 = (bf16[64,2048]{1,0:T(8,128)(2,1)S(1)}, bf16[64,2048]{1,0:T(8,128)(2,1)}, u32[]{:S(2)}, u32[]{:S(2)}) collective-permute-start(bf16[64,2048]{1,0:T(8,128)(2,1)S(1)} %fusion.4), channel_id=1, source_target_pairs={{0,16},{1,17},{2,18},{3,19},{4,20},{5,21},{6,22},{7,23},{8,24},{9,... | collective-permute-start | bytes 786440 | tf_op jit(solution)/shard_map/ppermute | solution.py:719
  456.7 53.1 %collective-permute-start.52 = (bf16[128,1024]{1,0:T(8,128)(2,1)}, bf16[128,1024]{1,0:T(8,128)(2,1)S(1)}, u32[]{:S(2)}, u32[]{:S(2)}) collective-permute-start(bf16[128,1024]{1,0:T(8,128)(2,1)} %get-tuple-element.136), channel_id=1, source_target_pairs={{0,6},{1,7},{2,0},{3,1},{4,2},{5,3},{6,4},{7,5},{8,10},{9,11},{10,... | collective-permute-start | bytes 786440 | tf_op jit(solution)/shard_map/ppermute | solution.py:719
  458.9 55.2 %collective-permute-start.37 = (bf16[4,32,2048]{2,1,0:T(8,128)(2,1)}, bf16[4,32,2048]{2,1,0:T(8,128)(2,1)}, u32[]{:S(2)}, u32[]{:S(2)}) collective-permute-start(bf16[4,32,2048]{2,1,0:T(8,128)(2,1)} %get-tuple-element.139), channel_id=1, source_target_pairs={{0,1},{1,0},{2,3},{3,2},{4,5},{5,4},{6,7},{7,6},{8,24},{9,25},{10,... | collective-permute-start | bytes 1572872 | tf_op jit(solution)/shard_map/ppermute | solution.py:719
  460.9 49.6 %collective-permute-start.54 = (bf16[128,1024]{1,0:T(8,128)(2,1)}, bf16[128,1024]{1,0:T(8,128)(2,1)}, u32[]{:S(2)}, u32[]{:S(2)}) collective-permute-start(bf16[128,1024]{1,0:T(8,128)(2,1)} %fusion.5), channel_id=1, source_target_pairs={{0,2},{1,3},{2,4},{3,5},{4,6},{5,7},{6,0},{7,1},{8,14},{9,15},{10,... | collective-permute-start | bytes 786440 | tf_op jit(solution)/shard_map/ppermute | solution.py:719
  465.5 51.7 %collective-permute-start.34 = (bf16[2,32,2048]{2,1,0:T(8,128)(2,1)}, bf16[2,32,2048]{2,1,0:T(8,128)(2,1)S(1)}, u32[]{:S(2)}, u32[]{:S(2)}) collective-permute-start(bf16[2,32,2048]{2,1,0:T(8,128)(2,1)} %get-tuple-element.141), channel_id=1, source_target_pairs={{0,1},{1,0},{2,3},{3,2},{4,5},{5,4},{6,7},{7,6},{8,24},{9,25},{10,... | collective-permute-start | bytes 786440 | tf_op jit(solution)/shard_map/ppermute | solution.py:719
  511.8 20.5 %collective-permute-start.55 = (bf16[128,1024]{1,0:T(8,128)(2,1)S(1)}, bf16[128,1024]{1,0:T(8,128)(2,1)S(1)}, u32[]{:S(2)}, u32[]{:S(2)}) collective-permute-start(bf16[128,1024]{1,0:T(8,128)(2,1)S(1)} %fusion.7), channel_id=1, source_target_pairs={{0,16},{1,17},{2,18},{3,19},{4,20},{5,21},{6,22},{7,23},{8,24},{9,... | collective-permute-start | bytes 786440 | tf_op jit(solution)/shard_map/ppermute | solution.py:719
  517.4 8.3 %collective-permute-start.38 = (bf16[32,2048]{1,0:T(8,128)(2,1)S(1)}, bf16[32,2048]{1,0:T(8,128)(2,1)S(1)}, u32[]{:S(2)}, u32[]{:S(2)}) collective-permute-start(bf16[32,2048]{1,0:T(8,128)(2,1)S(1)} %get-tuple-element.148), channel_id=1, source_target_pairs={{0,6},{1,7},{2,0},{3,1},{4,2},{5,3},{6,4},{7,5},{8,10},{9,11},{10,... | collective-permute-start | bytes 393224 | tf_op jit(solution)/shard_map/ppermute | solution.py:719
  (43 other events, 433.2 us)

commit v3 on v1

v3 whole, which is shorter than its diff:
```python
import functools

import jax
import jax.numpy as jnp
from jax import lax
from jax.experimental import pallas as pl
from jax.experimental.pallas import tpu as pltpu
from jax.sharding import Mesh
from jax.sharding import PartitionSpec as P

HD = 64
EPSILON = 1e-06
KEEP_MIN = 192
BF = jnp.bfloat16
F32 = jnp.float32
ALL = ("x", "core", "shard")
ANY = pl.BlockSpec(memory_space=pl.ANY)


def nn(a, b):
    return lax.dot_general(a, b, (((1,), (0,)), ((), ())), preferred_element_type=F32)


def nt(a, b):
    return lax.dot_general(a, b, (((1,), (1,)), ((), ())), preferred_element_type=F32)


def tn(a, b):
    return lax.dot_general(a, b, (((0,), (0,)), ((), ())), preferred_element_type=F32)


def params(mib=56, steps=1):
    return pltpu.CompilerParams(
        vmem_limit_bytes=mib * 2**20, dimension_semantics=("arbitrary",) * steps
    )


def cost(flops, moved, exps=0):
    return pl.CostEstimate(flops=int(flops), bytes_accessed=int(moved), transcendentals=int(exps))


class Order:
    token = None


def call(kernel, name, grid, prefetch, inputs, outputs, scratch=(), work=None, mib=56):
    lead, count = len(prefetch), len(inputs)
    skip = 0 if Order.token is None else 1

    def body(*refs):
        kernel(*refs[:lead], *refs[lead + skip : lead + skip + count + len(outputs)], *refs[lead + skip + count + len(outputs) + 1 :])

    *results, Order.token = pl.pallas_call(
        body,
        grid_spec=pltpu.PrefetchScalarGridSpec(
            num_scalar_prefetch=lead,
            grid=grid,
            in_specs=[ANY] * skip + [spec for _, spec in inputs],
            out_specs=[spec for _, _, spec in outputs] + [ANY],
            scratch_shapes=list(scratch),
        ),
        out_shape=[jax.ShapeDtypeStruct(shape, dtype) for shape, dtype, _ in outputs]
        + [jax.ShapeDtypeStruct((8, 128), F32)],
        compiler_params=params(mib, len(grid)),
        cost_estimate=work,
        name=name,
    )(*prefetch, *([Order.token] if skip else []), *[array for array, _ in inputs])
    return results


def fixed(shape):
    return pl.BlockSpec(tuple(shape), lambda *_: (0,) * len(shape))


def full(array):
    return (array, fixed(array.shape))


def anywhere(arrays):
    return [(array, ANY) for array in arrays]


def load_pieces(table, pieces, target, sem, first, last, how=(1, 0, 1)):
    step, phase, fold = how
    slot = 0
    for piece in pieces:
        rows = piece.shape[1]
        size = (last - first) // fold
        for index in range(phase, piece.shape[0], step):
            for part in range(fold):
                start = pl.multiple_of(table[slot] * fold + part * rows, 32)
                pltpu.make_async_copy(
                    piece.at[index, :, first + part * size : first + (part + 1) * size], target.at[pl.ds(start, rows)], sem
                ).start()
            slot += 1


def wait_all(target, sem):
    pltpu.make_async_copy(target, target, sem).wait()


def store_pieces(table, source, pieces, sem, fold=1):
    slot = 0
    for piece in pieces:
        rows = piece.shape[1]
        size = piece.shape[2] // fold
        for index in range(piece.shape[0]):
            for part in range(fold):
                start = pl.multiple_of(table[slot] * fold + part * rows, 32)
                pltpu.make_async_copy(
                    source.at[pl.ds(start, rows), 0:size], piece.at[index, :, part * size : (part + 1) * size], sem
                ).start()
            slot += 1


def pack_joint(place, joint_weight, mixer_weight, vectors, half, rows):
    width = 4 * half
    lines = vectors.shape[0]

    def kernel(place, joint, mixer, vectors, out_ref, held, sem):
        start = pl.multiple_of(place[1] * half, half)
        own = pl.ds(pl.multiple_of(place[0] * rows, rows), rows)
        for which in range(3):
            pltpu.make_async_copy(
                joint.at[own, pl.ds(which * 2 * half + start, half)],
                held.at[:, which * half : (which + 1) * half],
                sem,
            ).start()
        pltpu.make_async_copy(mixer.at[own, pl.ds(start, half)], held.at[:, 3 * half :], sem).start()
        out_ref[0, :lines, width:] = vectors[...].astype(BF)
        out_ref[0, lines:, width:] = jnp.zeros((rows - lines, 128), BF)
        pltpu.make_async_copy(held, held, sem).wait()
        out_ref[0, :, :width] = held[...].astype(BF)

    shape = (1, rows, width + 128)
    return call(
        kernel,
        "pack_joint",
        (1,),
        [place],
        anywhere([joint_weight, mixer_weight]) + [full(vectors)],
        [(shape, BF, fixed(shape))],
        [pltpu.VMEM((rows, width), F32), pltpu.SemaphoreType.DMA],
    )[0]


def pack_units(place, expand_weight, reduce_weight, block, rows):
    blocks = expand_weight.shape[1] // (2 * block)
    width = blocks * block
    size = reduce_weight.shape[1]
    fold = width // size

    def kernel(place, expand, reduce, expand_ref, reduce_ref, held, sem):
        first = pl.ds(pl.multiple_of(place[0] * rows, rows), rows)
        for index in range(blocks):
            start = pl.multiple_of(index * 2 * block + place[1] * block, block)
            pltpu.make_async_copy(
                expand.at[first, pl.ds(start, block)], held.at[0, :, index * block : (index + 1) * block], sem
            ).start()
        for part in range(fold):
            start = pl.multiple_of((place[1] * 2 + place[0]) * fold * rows + part * rows, rows)
            pltpu.make_async_copy(
                reduce.at[pl.ds(start, rows)], held.at[1, :, part * size : (part + 1) * size], sem
            ).start()
        pltpu.make_async_copy(held, held, sem).wait()
        expand_ref[...] = held[0:1].astype(BF)
        reduce_ref[...] = held[1:2].astype(BF)

    return call(
        kernel,
        "pack_units",
        (1,),
        [place],
        anywhere([expand_weight, reduce_weight]),
        [((1, rows, width), BF, fixed((1, rows, width)))] * 2,
        [pltpu.VMEM((2, rows, width), F32), pltpu.SemaphoreType.DMA],
        mib=16,
    )


def stack(*parts, wait=()):
    total = (sum(part.shape[0] for part in parts),) + parts[0].shape[1:]

    def kernel(*refs):
        sources, (out_ref, sem) = refs[: len(parts)], refs[-2:]
        start = 0
        for source in sources:
            size = source.shape[0]
            pltpu.make_async_copy(source, out_ref.at[pl.ds(start, size)], sem).start()
            start += size
        pltpu.make_async_copy(out_ref, out_ref, sem).wait()

    return call(
        kernel,
        "stack",
        (1,),
        [],
        anywhere(parts) + anywhere(wait),
        [(total, parts[0].dtype, fixed(total))],
        [pltpu.SemaphoreType.DMA],
        mib=16,
    )[0]


def add(count, *sums):
    rows, width = sums[0][0][0].shape[1:]
    step = max(count // 2, 1)

    def kernel(*refs):
        sources, results = refs[: -len(sums)], refs[-len(sums) :]
        start = 0
        for terms, result in zip(sums, results):
            total = sources[start][...].astype(F32)
            for source in sources[start + 1 : start + len(terms)]:
                total = total + source[...].astype(F32)
            result[...] = total.astype(BF)
            start += len(terms)

    def block(first):
        return pl.BlockSpec((step, rows, width), lambda i, *_: (first // step + i, 0, 0))

    return call(
        kernel,
        "add",
        (count // step,),
        [],
        [(array, block(first)) for terms in sums for array, first in terms],
        [((count, rows, width), BF, block(0))] * len(sums),
        mib=24,
    )


def add_pairs(one, other):
    count, rows, width = one[0][0].shape

    def kernel(*refs):
        sources, results = refs[:8], refs[8:]
        for which in range(2):
            for side in range(2):
                kept, came = sources[4 * side + 2 * which : 4 * side + 2 * which + 2]
                results[which][side] = (kept[0].astype(F32) + came[0].astype(F32)).astype(BF)

    def single(first):
        return pl.BlockSpec((1, rows, width), lambda i, *_: (first + i, 0, 0))

    double = pl.BlockSpec((2, rows, width), lambda i, *_: (i, 0, 0))
    inputs = []
    for pairs in (one, other):
        for kept, came, first in pairs:
            inputs += [(kept, single(0)), (came, single(first))]
    return call(
        kernel,
        "add_pairs",
        (count,),
        [],
        inputs,
        [((2 * count, rows, width), BF, double)] * 2,
        mib=24,
    )


def unpack_joint(place, mine, other):
    _, rows, wide = mine.shape
    width = wide - 128
    half = width // 4

    def kernel(place, mine, other, joint_ref, mixer_ref, vector_ref):
        x, core = place[0], place[1]
        vector_ref[...] = mine[x, :16, width:].astype(F32) + other[x, :16, width:].astype(F32)
        for owner, source in ((core, mine), (1 - core, other)):
            column = pl.multiple_of(owner * half, half)
            for part in range(2):
                span = pl.ds(pl.multiple_of((x if part == 0 else 1 - x) * rows, rows), rows)
                for which in range(3):
                    joint_ref[span, pl.ds(which * 2 * half + column, half)] = source[
                        part, :, which * half : (which + 1) * half
                    ].astype(F32)
                mixer_ref[span, pl.ds(column, half)] = source[part, :, 3 * half : width].astype(F32)

    return call(
        kernel,
        "unpack_joint",
        (1,),
        [place],
        [full(mine), full(other)],
        [
            ((2 * rows, 6 * half), F32, fixed((2 * rows, 6 * half))),
            ((2 * rows, 2 * half), F32, fixed((2 * rows, 2 * half))),
            ((16, 128), F32, fixed((16, 128))),
        ],
    )


def unpack_units(place, mine, other, block):
    _, rows, width = mine.shape
    blocks = width // block
    fold = block // (2 * rows)
    size = width // fold

    def kernel(place, mine, other, expand_ref, reduce_ref):
        x, core = place[0], place[1]
        for owner, source in ((core, mine), (1 - core, other)):
            column = pl.multiple_of(owner * block, block)
            for part in range(2):
                where = x if part == 0 else 1 - x
                span = pl.ds(pl.multiple_of(where * rows, rows), rows)
                for index in range(blocks):
                    expand_ref[span, pl.ds(index * 2 * block + column, block)] = source[
                        2 * part, :, index * block : (index + 1) * block
                    ].astype(F32)
                for index in range(fold):
                    start = pl.multiple_of((owner * 2 + where) * fold * rows + index * rows, rows)
                    reduce_ref[pl.ds(start, rows), :] = source[2 * part + 1, :, index * size : (index + 1) * size].astype(F32)

    return call(
        kernel,
        "unpack_units",
        (1,),
        [place],
        [full(mine), full(other)],
        [
            ((2 * rows, 2 * width), F32, fixed((2 * rows, 2 * width))),
            ((4 * fold * rows, size), F32, fixed((4 * fold * rows, size))),
        ],
        mib=24,
    )


def mask_call(own, far, kept, block):
    rows, width = own.shape
    blocks = rows // block

    def kernel(own, far, kept, out_ref, sums_ref):
        @pl.when(pl.program_id(0) < blocks)
        def _():
            value = own[...].astype(F32) * kept[...]
            out_ref[...] = value.astype(BF)

            @pl.when(pl.program_id(0) == 0)
            def _():
                sums_ref[...] = column_sum(value)

            @pl.when(pl.program_id(0) > 0)
            def _():
                sums_ref[...] += column_sum(value)

        @pl.when(pl.program_id(0) >= blocks)
        def _():
            out_ref[...] = (far[...].astype(F32) * kept[...]).astype(BF)

    return call(
        kernel,
        "kept_rows",
        (2 * blocks,),
        [],
        [
            (own, pl.BlockSpec((block, width), lambda i, *_: (jnp.minimum(i, blocks - 1), 0))),
            (far, pl.BlockSpec((block, width), lambda i, *_: (jnp.maximum(i - blocks, 0), 0))),
            (kept, pl.BlockSpec((block, 1), lambda i, *_: (i, 0))),
        ],
        [((2 * rows, width), BF, pl.BlockSpec((block, width), lambda i, *_: (i, 0))), ((1, width), F32, fixed((1, width)))],
    )


def normalise(value):
    centred = value - jnp.mean(value, axis=-1, keepdims=True)
    inverse = lax.rsqrt(jnp.mean(centred * centred, axis=-1, keepdims=True) + EPSILON)
    return centred * inverse, inverse


def joint_call(table, place, tokens, lines, pieces, block, columns, ns):
    rows, width = tokens.shape
    half = columns // 3
    row = lambda i, *_: (i, 0)
    count = len(pieces)
    ringed = lines is None
    vector_rows = 6 + 1 + 2
    unit = width // (2 * ns)

    def kernel(table, place, tokens, *rest):
        pieces = rest[:count]
        given = rest[count : len(rest) - 10]
        unit_ref, joint_ref, mixer_ref, vector_ref, weight, held, plain, sem, mixer_sem, vector_sem = rest[
            len(rest) - 10 :
        ]
        core = place[1]

        @pl.when(pl.program_id(0) == 0)
        def _():
            load_pieces(table, pieces, weight, sem, 0, columns)
            load_pieces(table, pieces, mixer_ref, mixer_sem, columns, columns + half)
            if ringed:
                slot = 0
                for piece in pieces:
                    if piece.shape[2] > columns + half:
                        for index in range(piece.shape[0]):
                            pltpu.make_async_copy(
                                piece.at[index, 0:16, columns + half :], held.at[table[slot + index] // unit], vector_sem
                            ).start()
                    slot += piece.shape[0]
                wait_all(held, vector_sem)
                plain[...] = held[...].astype(F32)
                line = lambda shard, index: plain[2 * shard, pl.ds(index, 1), :]
                wide = lambda index: jnp.concatenate([line(shard, index) for shard in range(ns)], axis=1)
                starts = (0, 1, 4, 5, 6, 11)
                for target, index in enumerate(starts):
                    vector_ref[target : target + 1, :] = wide(index)
                parts = [line(base + 2 * core + k, 2 + r) for base in (0, 4) for k in (0, 1) for r in (0, 1)]
                vector_ref[6:7, :] = jnp.concatenate(parts, axis=1)
                for side in range(2):
                    parts = [line(4 * side + k, 7 + 2 * core + r) for k in range(4) for r in (0, 1)]
                    vector_ref[7 + side : 8 + side, :] = jnp.concatenate(parts, axis=1)
            else:
                vector_ref[...] = given[0][...]

        unit_rows, _ = normalise(tokens[...].astype(F32))
        normed = (unit_rows * vector_ref[0:1, :] + vector_ref[1:2, :]).astype(BF)
        unit_ref[...] = unit_rows.astype(BF)

        @pl.when(pl.program_id(0) == 0)
        def _():
            wait_all(weight, sem)

        for which in range(3):
            span = slice(which * half, (which + 1) * half)
            product = nn(normed, weight[:, span])
            if which != 1:
                product = product + vector_ref[6:7, (which // 2) * half : (which // 2 + 1) * half]
            joint_ref[:, span] = product.astype(BF)

        @pl.when(pl.program_id(0) == pl.num_programs(0) - 1)
        def _():
            wait_all(mixer_ref, mixer_sem)

    return call(
        kernel,
        "joint_rows",
        (rows // block,),
        [table, place],
        [(tokens, pl.BlockSpec((block, width), row))] + anywhere(pieces) + ([] if ringed else [full(lines)]),
        [
            ((rows, width), BF, pl.BlockSpec((block, width), row)),
            ((rows, columns), BF, pl.BlockSpec((block, columns), row)),
            ((width, half), BF, fixed((width, half))),
            ((vector_rows, width), F32, fixed((vector_rows, width))),
        ],
        [
            pltpu.VMEM((width, columns), BF),
            pltpu.VMEM((2 * ns, 16, 128), BF),
            pltpu.VMEM((2 * ns, 16, 128), F32),
            pltpu.SemaphoreType.DMA,
            pltpu.SemaphoreType.DMA,
            pltpu.SemaphoreType.DMA,
        ],
        cost(2 * rows * width * columns, 2 * (rows * width + (rows + width) * columns)),
    )


def head_rows(array, head_of_lane):
    zero = jnp.zeros_like(array)
    heads = array.shape[1] // HD
    return jnp.concatenate([jnp.where(head_of_lane == head, array, zero) for head in range(heads)], axis=0)


def head_lanes(array, head_of_lane, slots):
    mixed = array[:slots]
    for head in range(1, array.shape[0] // slots):
        mixed = jnp.where(head_of_lane == head, array[head * slots : (head + 1) * slots], mixed)
    return mixed


def group_of(width):
    return 4 * HD if width % (4 * HD) == 0 else width


def attend_kernel(base, group, floor, lengths, q_ref, k_ref, v_ref, out_ref, log_ref):
    slots, width = q_ref.shape
    length = lengths[base + pl.program_id(0)]
    head_of_lane = lax.broadcasted_iota(jnp.int32, (1, group), 1) // HD
    kept = lax.broadcasted_iota(jnp.int32, (slots - floor, 1), 0) < length - floor
    for part in range(width // group):
        lanes = slice(part * group, (part + 1) * group)
        own = head_rows(q_ref[:, lanes] * jnp.asarray(HD**-0.5, BF), head_of_lane)
        scores = nt(k_ref[:, lanes], own)
        scores = jnp.concatenate([scores[:floor], jnp.where(kept, scores[floor:], -1e30)], axis=0)
        peak = jnp.max(scores, axis=0, keepdims=True)
        raised = jnp.exp(scores - peak)
        total = jnp.sum(raised, axis=0, keepdims=True)
        shares = (raised * (1.0 / total)).astype(BF)
        out_ref[:, lanes] = head_lanes(tn(shares, v_ref[:, lanes]), head_of_lane, slots).astype(BF)
        log_ref[0, part] = peak + jnp.log(total)


def attend_call(lengths, joint, base, count, slots):
    width = joint.shape[1] // 3
    group = group_of(width)
    floor = KEEP_MIN if slots > KEEP_MIN else 0
    part = lambda which: (joint, pl.BlockSpec((slots, width), lambda i, *_: (base + i, which)))
    logs = (width // group, 1, group // HD * slots)
    return call(
        functools.partial(attend_kernel, base, group, floor),
        "attend",
        (count,),
        [lengths],
        [part(0), part(1), part(2)],
        [
            ((count * slots, width), BF, pl.BlockSpec((slots, width), lambda i, *_: (i, 0))),
            ((count,) + logs, F32, pl.BlockSpec((1,) + logs, lambda i, *_: (i, 0, 0, 0))),
        ],
        (),
        cost(16 * count * slots * slots * width, 8 * count * slots * width, count * slots * slots * width // HD),
    )


def mixer_kernel(core, mine, other, m_mine, m_other, tokens, lines, hidden_ref, *normed_refs):
    half = mine.shape[1]
    own = pl.ds(pl.multiple_of(core[0] * half, half), half)
    far = pl.ds(pl.multiple_of((1 - core[0]) * half, half), half)
    hidden_ref[:, own] = nn(mine[...], m_mine[own, :]) + nn(other[...], m_mine[far, :])
    hidden_ref[:, far] = nn(mine[...], m_other[own, :]) + nn(other[...], m_other[far, :])
    hidden = tokens[...].astype(F32) + hidden_ref[...] + lines[2:3, :]
    hidden_ref[...] = hidden
    unit, _ = normalise(hidden)
    normed = (unit * lines[3:4, :] + lines[4:5, :]).astype(BF)
    for index, normed_ref in enumerate(normed_refs):

        @pl.when(pl.program_id(0) == index)
        def _(normed_ref=normed_ref):
            normed_ref[...] = normed


def mixer_call(core, mine, other, m_mine, m_other, tokens, lines, block):
    rows, half = mine.shape
    width = 2 * half
    slim = pl.BlockSpec((block, half), lambda i, *_: (i, 0))
    wide = pl.BlockSpec((block, width), lambda i, *_: (i, 0))
    return call(
        mixer_kernel,
        "mixer",
        (rows // block,),
        [core],
        [(mine, slim), (other, slim), full(m_mine), full(m_other), (tokens, wide), full(lines)],
        [((rows, width), F32, wide)] + [((block, width), BF, fixed((block, width)))] * (rows // block),
        (),
        cost(2 * rows * width * width, 10 * rows * width),
    )


def curve(before):
    square = before * before
    share = 1.0 / (1.0 + jnp.exp(before * (-1.5957691216057308 - 0.07135481627260025 * square)))
    active = before * share
    slope = share + active * (1.0 - share) * (1.5957691216057308 + 0.21406444881780075 * square)
    return active, slope


def expand_call(load_table, store_table, parts, grad, lines, pieces, store_shapes, tile, columns, how, fold):
    rows, width = grad.shape
    column = lambda i, *_: (0, i)
    n_load, n_store, n_parts = len(pieces), len(store_shapes), len(parts)

    def kernel(load_table, store_table, *rest):
        parts, (grad, lines), rest = rest[:n_parts], rest[n_parts : n_parts + 2], rest[n_parts + 2 :]
        pieces = rest[:n_load]
        active_ref, slope_ref = rest[n_load : n_load + 2]
        stores = rest[n_load + 2 : n_load + 2 + n_store]
        weight, total, sem, out_sem = rest[n_load + 2 + n_store :]
        step = pl.program_id(0)
        own = rows // n_parts

        @pl.when(step == 0)
        def _():
            load_pieces(load_table, pieces, weight, sem, 0, columns, how)
            wait_all(weight, sem)

        span = pl.ds(pl.multiple_of(step * tile, tile), tile)
        per_line = width // tile
        bias = lines[pl.ds(7 + step // per_line, 1), pl.ds(pl.multiple_of(step % per_line * tile, tile), tile)]
        for index, source in enumerate(parts):
            active, slope = curve(nn(source[...], weight[:, span]) + bias)
            part = slice(index * own, (index + 1) * own)
            active_ref[part, :] = active.astype(BF)
            slope_ref[part, :] = slope.astype(BF)
        total[span, :] = tn(active_ref[...], grad[...]).astype(BF)

        @pl.when(step == pl.num_programs(0) - 1)
        def _():
            store_pieces(store_table, total, stores, out_sem, fold)
            wait_all(total, out_sem)

    tall = pl.BlockSpec((rows, tile), column)
    return call(
        kernel,
        "expand_and_dreduce",
        (columns // tile,),
        [load_table, store_table],
        [full(a) for a in parts] + [full(grad), full(lines)] + anywhere(pieces),
        [((rows, columns), BF, tall), ((rows, columns), BF, tall)] + [(s, BF, ANY) for s in store_shapes],
        [
            pltpu.VMEM((width, columns), BF),
            pltpu.VMEM((columns, width), BF),
            pltpu.SemaphoreType.DMA,
            pltpu.SemaphoreType.DMA,
        ],
        cost(4 * rows * width * columns, 4 * rows * (columns + width) + 4 * width * columns),
    )


def back_call(expand_table, reduce_table, grad, slope, expand_pieces, reduce_pieces, tile, expand_how, reduce_how, block):
    rows, width = grad.shape
    columns = slope.shape[1]
    own = rows // 2
    tiles = columns // tile
    last = lambda i, *_: (0, jnp.minimum(i, tiles - 1))
    n_expand, n_reduce = len(expand_pieces), len(reduce_pieces)

    def kernel(expand_table, reduce_table, grad, slope, *rest):
        expand_pieces = rest[:n_expand]
        reduce_pieces = rest[n_expand : n_expand + n_reduce]
        before_ref, bias_ref, *far_refs = rest[n_expand + n_reduce : -7]
        own_ref, expand, reduce, before, sem, reduce_sem, out_sem = rest[-7:]
        step = pl.program_id(0)

        @pl.when(step == 0)
        def _():
            load_pieces(reduce_table, reduce_pieces, reduce, reduce_sem, 0, width * reduce_how[2], reduce_how)
            load_pieces(expand_table, expand_pieces, expand, sem, 0, columns, expand_how)
            wait_all(reduce, reduce_sem)

        @pl.when(step < tiles)
        def _():
            span = pl.ds(pl.multiple_of(step * tile, tile), tile)
            sums = None
            for start in (0, own):
                part = slice(start, start + own)
                low = (slope[part, :].astype(F32) * nt(grad[part, :], reduce[span, :])).astype(BF)
                before[part, span] = low
                column_sum = jnp.sum(low.astype(F32), axis=0, keepdims=True)
                sums = column_sum if sums is None else sums + column_sum
            bias_ref[...] = sums

        @pl.when(step == tiles)
        def _():
            pltpu.make_async_copy(before, before_ref, out_sem).start()
            wait_all(expand, sem)
            far = nt(before[own:, :], expand[...]).astype(BF)
            for index, far_ref in enumerate(far_refs):
                far_ref[...] = far[index * block : (index + 1) * block, :]

        @pl.when(step == tiles + 1)
        def _():
            own_ref[...] = nt(before[:own, :], expand[...])
            pltpu.make_async_copy(before, before_ref, out_sem).wait()

    return call(
        kernel,
        "grad_before",
        (tiles + 2,),
        [expand_table, reduce_table],
        [full(grad), (slope, pl.BlockSpec((rows, tile), last))] + anywhere(list(expand_pieces) + list(reduce_pieces)),
        [
            ((rows, columns), BF, ANY),
            ((1, columns), F32, pl.BlockSpec((1, tile), last)),
        ]
        + [((block, width), BF, fixed((block, width)))] * (own // block)
        + [((own, width), F32, fixed((own, width)))],
        [
            pltpu.VMEM((width, columns), BF),
            pltpu.VMEM((columns, width), BF),
            pltpu.VMEM((rows, columns), BF),
            pltpu.SemaphoreType.DMA,
            pltpu.SemaphoreType.DMA,
            pltpu.SemaphoreType.DMA,
        ],
        cost(4 * rows * width * columns, 4 * rows * (columns + width) + 4 * width * columns),
    )


def dexpand_call(store_table, parts, before, store_shapes, tile):
    rows, columns = before.shape
    width = parts[0].shape[1]
    n_store, n_parts = len(store_shapes), len(parts)

    def kernel(store_table, *rest):
        parts, before, rest = rest[:n_parts], rest[n_parts], rest[n_parts + 1 :]
        stores = rest[:n_store]
        total, out_sem = rest[n_store:]
        step = pl.program_id(0)
        own = rows // n_parts
        span = pl.ds(pl.multiple_of(step * tile, tile), tile)
        product = None
        for index, source in enumerate(parts):
            term = tn(source[...], before[index * own : (index + 1) * own, :])
            product = term if product is None else product + term
        total[:, span] = product.astype(BF)

        @pl.when(step == pl.num_programs(0) - 1)
        def _():
            store_pieces(store_table, total, stores, out_sem)
            wait_all(total, out_sem)

    return call(
        kernel,
        "dexpand",
        (columns // tile,),
        [store_table],
        [full(a) for a in parts] + [(before, pl.BlockSpec((rows, tile), lambda i, *_: (0, i)))],
        [(s, BF, ANY) for s in store_shapes],
        [pltpu.VMEM((width, columns), BF), pltpu.SemaphoreType.DMA],
        cost(2 * rows * width * columns, 2 * (rows * width + rows * columns + width * columns)),
    )


def this_block(parts):
    value = parts[0][...]
    for index in range(1, len(parts)):
        value = jnp.where(pl.program_id(0) == index, parts[index][...], value)
    return value


def norm_back(g, value, gain):
    unit, inverse = normalise(value)
    scaled = g * gain
    back = inverse * (
        scaled
        - jnp.mean(scaled, axis=-1, keepdims=True)
        - unit * jnp.mean(scaled * unit, axis=-1, keepdims=True)
    )
    return back, unit


def column_sum(array):
    return jnp.sum(array, axis=0, keepdims=True)


def attn_grad_kernel(
    core, g_own, hidden, cotangent, kept, lines, m_mine, m_other, *rest
):
    *g_far, hidden_grad_ref, low_ref, mine_ref, other_ref, sums_ref = rest
    half = mine_ref.shape[1]
    step = pl.program_id(0)
    own = pl.ds(pl.multiple_of(core[0] * half, half), half)
    far = pl.ds(pl.multiple_of((1 - core[0]) * half, half), half)
    g = g_own[...] + this_block(g_far).astype(F32)
    back, unit = norm_back(g, hidden[...], lines[3:4, :])
    total = cotangent[...].astype(F32) * kept[...] + back
    low = total.astype(BF)
    hidden_grad_ref[...] = total
    low_ref[...] = low
    sums = jnp.concatenate([column_sum(g * unit), column_sum(g), column_sum(low.astype(F32))], axis=0)

    @pl.when(step == 0)
    def _():
        sums_ref[...] = sums

    @pl.when(step > 0)
    def _():
        sums_ref[...] += sums

    left, right = low_ref[:, own], low_ref[:, far]
    mine_ref[...] = (nt(left, m_mine[own, :]) + nt(right, m_other[own, :])).astype(BF)
    other_ref[...] = (nt(left, m_mine[far, :]) + nt(right, m_other[far, :])).astype(BF)


def attn_grad_call(core, g_own, g_far, hidden, cotangent, kept, lines, m_mine, m_other, block):
    rows, width = hidden.shape
    half = width // 2
    row = lambda i, *_: (i, 0)
    wide, slim = pl.BlockSpec((block, width), row), pl.BlockSpec((block, half), row)
    return call(
        attn_grad_kernel,
        "grad_attended",
        (rows // block,),
        [core],
        [(g_own, wide), (hidden, wide), (cotangent, wide), (kept, pl.BlockSpec((block, 1), row))]
        + [full(lines), full(m_mine), full(m_other)]
        + [full(part) for part in g_far],
        [
            ((rows, width), F32, wide),
            ((rows, width), BF, wide),
            ((rows, half), BF, slim),
            ((rows, half), BF, slim),
            ((3, width), F32, fixed((3, width))),
        ],
        (),
        cost(2 * rows * width * width, 18 * rows * width),
    )


def dmixer_kernel(core, mine, other, low, keep_ref, send_ref):
    half = mine.shape[1]
    own = pl.ds(pl.multiple_of(core[0] * half, half), half)
    far = pl.ds(pl.multiple_of((1 - core[0]) * half, half), half)
    for source, rows in ((mine, own), (other, far)):
        keep_ref[rows, :] = tn(source[...], low[:, own]).astype(BF)
        send_ref[rows, :] = tn(source[...], low[:, far]).astype(BF)


def dmixer_call(core, mine, other, low):
    rows, width = low.shape
    target = ((width, width // 2), BF, fixed((width, width // 2)))
    return call(
        dmixer_kernel,
        "dmixer",
        (1,),
        [core],
        [full(mine), full(other), full(low)],
        [target, target],
        (),
        cost(2 * rows * width * width, 4 * rows * width + 2 * width * width),
    )


def attend_back_kernel(base, group, floor, lengths, q_ref, k_ref, v_ref, g_ref, log_ref, dq_ref, dk_ref, dv_ref):
    slots, width = q_ref.shape
    length = lengths[base + pl.program_id(0)]
    head_of_lane = lax.broadcasted_iota(jnp.int32, (1, group), 1) // HD
    kept = lax.broadcasted_iota(jnp.int32, (slots - floor, 1), 0) < length - floor
    for part in range(width // group):
        lanes = slice(part * group, (part + 1) * group)
        k = k_ref[:, lanes]
        own_q = head_rows(q_ref[:, lanes] * jnp.asarray(HD**-0.5, BF), head_of_lane)
        own_g = head_rows(g_ref[:, lanes], head_of_lane)
        probs = jnp.exp(nt(k, own_q) - log_ref[0, part])
        probs = jnp.concatenate([probs[:floor], jnp.where(kept, probs[floor:], 0.0)], axis=0)
        shares = nt(v_ref[:, lanes], own_g)
        raw = (probs * (shares - jnp.sum(probs * shares, axis=0, keepdims=True))).astype(BF)
        dv_ref[:, lanes] = nn(probs.astype(BF), own_g).astype(BF)
        dk_ref[:, lanes] = nn(raw, own_q).astype(BF)
        dq_ref[:, lanes] = (head_lanes(tn(raw, k), head_of_lane, slots) * HD**-0.5).astype(BF)


def attend_back_call(lengths, joint, grad, logs, base, slots):
    count = logs.shape[0]
    width = joint.shape[1] // 3
    group = group_of(width)
    floor = KEEP_MIN if slots > KEEP_MIN else 0
    part = lambda which: (joint, pl.BlockSpec((slots, width), lambda i, *_: (base + i, which)))
    block = pl.BlockSpec((slots, width), lambda i, *_: (i, 0))
    return call(
        functools.partial(attend_back_kernel, base, group, floor),
        "attend_back",
        (count,),
        [lengths],
        [part(0), part(1), part(2), (grad, block), (logs, pl.BlockSpec((1,) + logs.shape[1:], lambda i, *_: (i, 0, 0, 0)))],
        [((count * slots, width), BF, block)] * 3,
        (),
        cost(40 * count * slots * slots * width, 14 * count * slots * width, count * slots * slots * width // HD),
    )


def djoint_call(load_table, store_table, place, unit, lines, own, far, mixer_own, mixer_far, sums_two, expand_sums, grad_sums, pieces, store_shapes, ns):
    rows, width = unit.shape
    half = own[0].shape[1]
    columns = 3 * half + mixer_own.shape[1]
    shard_rows = width // ns
    lane = 128
    n_load, n_store = len(pieces), len(store_shapes)
    wide_pieces = [s for s in store_shapes if s[2] > columns]

    def kernel(load_table, store_table, place, unit, lines, *rest):
        own, far = rest[0:3], rest[3:6]
        mixer_own, mixer_far, sums_two, expand_sums, grad_sums = rest[6:11]
        pieces = rest[11 : 11 + n_load]
        sums = rest[11 + n_load]
        stores = rest[12 + n_load : 12 + n_load + n_store]
        total, weight, gains, shifts, turned, sem, out_sem = rest[12 + n_load + n_store :]
        step = pl.program_id(0)
        count = own[0].shape[0]

        @pl.when(step == 0)
        def _():
            load_pieces(load_table, pieces, weight, sem, 0, 3 * half)
            turned[...] = lines[0:8, :].T
            wait_all(weight, sem)

        for which in range(3):

            @pl.when(step == which)
            def _(which=which):
                a, b = own[which][...], far[which][...]
                column = column_sum(a.astype(F32)) + column_sum(b.astype(F32))
                sums[which : which + 1, :] = column
                product = tn(unit[:count, :], a) + tn(unit[count:, :], b)
                span = slice(which * half, (which + 1) * half)
                total[:, span] = (product * turned[:, 0:1] + turned[:, 1:2] * column).astype(BF)
                part = weight[:, span].astype(F32)
                gain_terms, shift_terms = product * part, part * column
                gain_lanes, shift_lanes = gain_terms[:, :lane], shift_terms[:, :lane]
                for start in range(lane, half, lane):
                    gain_lanes = gain_lanes + gain_terms[:, start : start + lane]
                    shift_lanes = shift_lanes + shift_terms[:, start : start + lane]
                if which == 0:
                    gains[...], shifts[...] = gain_lanes, shift_lanes
                else:
                    gains[...] += gain_lanes
                    shifts[...] += shift_lanes

        @pl.when(step == 2)
        def _():
            total[:, 3 * half : columns] = (mixer_own[...].astype(F32) + mixer_far[...].astype(F32)).astype(BF)
            if wide_pieces:
                core = place[1]
                zero = jnp.zeros((1, lane), F32)
                for shard in range(ns):
                    part = slice(shard * shard_rows, (shard + 1) * shard_rows)
                    spans = [slice(shard * lane, (shard + 1) * lane)]
                    here = []
                    here.append(column_sum(gains[part, :].T))
                    here.append(column_sum(shifts[part, :].T))
                    group, slot = shard // 4, shard % 4
                    mine = core == slot // 2
                    for line in range(2):
                        start = (slot % 2) * 2 * lane + line * lane
                        value = sums[2 * group : 2 * group + 1, start : start + lane]
                        here.append(jnp.where(mine, value, zero))
                    here.append(sums_two[2:3, spans[0]])
                    here.append(sums_two[0:1, spans[0]])
                    here.append(sums_two[1:2, spans[0]])
                    for line in range(4):
                        start = shard * 2 * lane + (line % 2) * lane
                        here.append(jnp.where(core == line // 2, expand_sums[0:1, start : start + lane], zero))
                    here.append(grad_sums[0:1, spans[0]])
                    here.extend([zero] * 4)
                    total[shard * shard_rows : shard * shard_rows + 16, columns:] = jnp.concatenate(here, axis=0).astype(BF)
                    total[shard * shard_rows + 16 : (shard + 1) * shard_rows, columns:] = jnp.zeros(
                        (shard_rows - 16, lane), BF
                    )
            store_pieces(store_table, total, stores, out_sem)
            wait_all(total, out_sem)

    return call(
        kernel,
        "djoint",
        (3,),
        [load_table, store_table, place],
        [full(a) for a in [unit, lines] + own + far + [mixer_own, mixer_far, sums_two, expand_sums, grad_sums]]
        + anywhere(pieces),
        [((3, half), F32, fixed((3, half)))] + [(s, BF, ANY) for s in store_shapes],
        [
            pltpu.VMEM((width, columns + (lane if wide_pieces else 0)), BF),
            pltpu.VMEM((width, 3 * half), BF),
            pltpu.VMEM((width, lane), F32),
            pltpu.VMEM((width, lane), F32),
            pltpu.VMEM((width, 8), F32),
            pltpu.SemaphoreType.DMA,
            pltpu.SemaphoreType.DMA,
        ],
        cost(6 * rows * width * half, 2 * (rows * width + 3 * rows * half + width * columns)),
    )


def split_call(
    table, sources, pieces, weight_shape, turned, block, first, count, name, extra=(), outputs=None, finish=None, how=(1, 0, 1)
):
    inner = weight_shape[1] if turned else weight_shape[0]
    width = weight_shape[0] if turned else weight_shape[1]
    rows = count * block
    n_sources, n_pieces, n_extra = len(sources), len(pieces), len(extra)
    if outputs is None:
        outputs = [((block, width), BF, fixed((block, width)))] * count

    def kernel(table, *rest):
        sources = rest[:n_sources]
        pieces = rest[n_sources : n_sources + n_pieces]
        extra = rest[n_sources + n_pieces : n_sources + n_pieces + n_extra]
        results = rest[n_sources + n_pieces + n_extra : -2]
        weight, sem = rest[-2:]

        @pl.when(pl.program_id(0) == 0)
        def _():
            load_pieces(table, pieces, weight, sem, 0, weight.shape[1] * how[2], how)
            wait_all(weight, sem)

        total, start = None, 0
        for source in sources:
            size = source.shape[1]
            if turned:
                product = nt(source[...], weight[:, start : start + size])
            else:
                product = nn(source[...], weight[start : start + size, :])
            total = product if total is None else total + product
            start += size
        if finish is None:
            for index, result in enumerate(results):

                @pl.when(pl.program_id(0) == index)
                def _(result=result):
                    result[...] = total.astype(BF)

        else:
            finish(total, extra, results)

    return call(
        kernel,
        name,
        (count,),
        [table],
        [(a, pl.BlockSpec((block, a.shape[1]), lambda i, *_: (first + i, 0))) for a in sources]
        + anywhere(pieces)
        + list(extra),
        outputs,
        [pltpu.VMEM(weight_shape, BF), pltpu.SemaphoreType.DMA],
        cost(2 * rows * inner * width, 2 * (rows * inner + inner * width) + 4 * rows * width),
    )


def rows_finish(total, extra, results):
    tokens, hidden_grad, lines, *rows_far = extra
    out_ref, sums_ref = results
    g = total + this_block(rows_far).astype(F32)
    back, unit = norm_back(g, tokens[...].astype(F32), lines[0:1, :])
    out_ref[...] = (hidden_grad[...] + back).astype(BF)
    sums = jnp.concatenate([column_sum(g * unit), column_sum(g)], axis=0)

    @pl.when(pl.program_id(0) == 0)
    def _():
        sums_ref[...] = sums

    @pl.when(pl.program_id(0) > 0)
    def _():
        sums_ref[...] += sums


def branch_finish(total, extra, results):
    hidden, kept, lines, *branch_far = extra
    branch = total + this_block(branch_far).astype(F32) + lines[5:6, :]
    results[0][...] = (kept[...] * (hidden[...] + branch)).astype(BF)


class Ring:
    def __init__(self):
        self.x, self.core = lax.axis_index("x"), lax.axis_index("core")
        shard = lax.axis_index("shard")
        self.z, self.y = shard // 2, shard % 2
        self.turn = jnp.where(self.core == 0, 1, -1)

    def send(self, array, step):
        index = lambda x, core, z, y: (x * 2 + core) * 8 + z * 2 + y
        pairs = []
        for x in range(2):
            for core in range(2):
                for z in range(4):
                    for y in range(2):
                        d = 1 - 2 * core
                        x_to, z_to, y_to = {
                            "x": (1 - x, z, y),
                            "y": (x, z, 1 - y),
                            "xy": (1 - x, z, y) if core == 0 else (x, z, 1 - y),
                            "yx": (x, z, 1 - y) if core == 0 else (1 - x, z, y),
                            "z1": (x, (z + d) % 4, y),
                            "z2": (x, (z - d) % 4, y),
                            "z3": (x, (z + 2) % 4, y),
                            "pair": (x, z ^ 1, y),
                            "d": (1 - x, z, 1 - y),
                        }[step]
                        pairs.append((index(x, core, z, y), index(x_to, core, z_to, y_to)))
        return lax.ppermute(array, ALL, pairs)

    def start_of(self, x, z, y, rows, offset):
        return (((z % 4) * 2 + y) * 2 + x) * rows + offset

    def pick(self, first, second):
        swap_x = jnp.where(self.core == 0, first, second)
        swap_y = jnp.where(self.core == 0, second, first)
        return (self.x + swap_x) % 2, (self.y + swap_y) % 2


    def table_first(self, rows, offset, backwards=False):
        found = []
        for dz in (2, -self.turn, self.turn, 0) if backwards else (0, -self.turn, self.turn, 2):
            for y in (1 - self.y, self.y) if backwards else (self.y, 1 - self.y):
                for x in (0, 1):
                    found.append(self.start_of(x, self.z + dz, y, rows, offset))
        return found

    def table_pairs(self, rows):
        found = []
        for first in (0, 1):
            for second in (0, 1):
                for flip in range(4):
                    x, y = self.pick(first, second)
                    found.append(self.start_of(x, self.z ^ flip, y, rows, 0))
        return found

    def table_second(self, rows, offset, backwards=False):
        found = []
        taken = (1, 0) if backwards else (0, 1)
        for first in taken:
            for second in taken:
                for dz in (2, -self.turn, self.turn, 0) if backwards else (0, -self.turn, self.turn, 2):
                    x, y = self.pick(first, second)
                    found.append(self.start_of(x, self.z + dz, y, rows, offset))
        return found


class Sum:
    def __init__(self, links, parts):
        self.links = links
        *give, self.keep_give, self.keep_stay = parts
        came = [links.send(part, "xy") for part in give]
        self.came = [(came[0], 0), (came[-1], 4 if len(came) == 1 else 0)]

    def second_step(self):
        (give,) = add(4, [(self.keep_give, 0), self.came[0]])
        (self.keep,) = add(4, [(self.keep_stay, 0), self.came[1]])
        self.came, self.slots = self.links.send(give, "yx"), 1

    def second_step_of_both(self, other):
        sides = [
            [(each.keep_give,) + each.came[0], (each.keep_stay,) + each.came[1]] for each in (self, other)
        ]
        give, self.keep = add_pairs(*sides)
        self.came, self.slots = self.links.send(give, "yx"), 2

    def third_step(self):
        parts = add(self.slots, *[[(self.keep, i * self.slots), (self.came, i * self.slots)] for i in range(4)])
        self.keep = parts[3]
        self.came = [self.links.send(part, step) for part, step in zip(parts, ("z3", "z2", "z1"))]

    def fourth_step(self):
        (self.keep,) = add(self.slots, [(self.keep, 0)] + [(array, 0) for array in self.came])
        self.came = self.links.send(self.keep, "x")

    def fifth_step(self):
        self.total = stack(self.keep, self.came)
        self.other = swap(self.total)


def swap(array):
    return lax.ppermute(array, "core", [(0, 1), (1, 0)])


def numbers(values):
    return jnp.stack([jnp.asarray(v, jnp.int32) for v in values])


def gather_plain(part):
    return [lax.all_gather(part, ("shard", "x"), axis=0, tiled=True)[None]]


def sum_plain(parts):
    own = lax.psum_scatter(parts[0][0], ("shard", "x"), scatter_dimension=0, tiled=True)
    return lax.all_gather(lax.all_gather(own, "x", axis=0, tiled=False), "core", axis=0, tiled=False)


def on_device(
    nx,
    ns,
    tokens,
    lengths,
    cotangent,
    norm_gain,
    norm_shift,
    joint_weight,
    joint_bias,
    mixer_weight,
    mixer_bias,
    ffnorm_gain,
    ffnorm_shift,
    expand_weight,
    expand_bias,
    reduce_weight,
    reduce_bias,
):
    Order.token = None
    count, slots, width = tokens.shape
    rows = count * slots
    half = width // 2
    hidden_units = expand_weight.shape[1]
    half_units = hidden_units // 2
    unit_block = half_units // ns
    part_rows = width // (ns * nx)
    reduce_rows = unit_block // nx
    tile = min(512, half_units)
    x, core = lax.axis_index("x"), lax.axis_index("core")
    vectors = (norm_gain, norm_shift, joint_bias, mixer_bias, ffnorm_gain, ffnorm_shift, expand_bias, reduce_bias)
    ring = nx == 2 and ns == 8 and width == 1024 and hidden_units == 4096
    core_number = numbers([core])
    place = numbers([x, core])
    flat = tokens.reshape(rows, width)
    grad_flat = cotangent.reshape(rows, width)
    both_lengths = jnp.concatenate([lengths, swap(lengths)])
    kept_all = (jnp.arange(slots)[None, :] < both_lengths[:, None]).reshape(2 * rows, 1).astype(F32)
    kept = kept_all[:rows]

    if ring:
        links = Ring()
        own_joint = pack_joint(
            place, joint_weight, mixer_weight, jnp.concatenate(vectors).reshape(-1, 128), half, part_rows
        )
        joint_came = [links.send(own_joint, step) for step in ("z1", "z2", "z3")]
        both_tokens = stack(flat, swap(flat))
        both_grad, grad_sums = mask_call(grad_flat, swap(grad_flat), kept_all, slots)
        joint_four = stack(own_joint, *joint_came)
        joint_across, joint_other = links.send(joint_four, "yx"), links.send(joint_four, "xy")
        joint_last = links.send(joint_across, "xy")
        joint_pieces = [joint_four, joint_across, joint_other, joint_last]
        own_expand, own_reduce = pack_units(place, expand_weight, reduce_weight, unit_block, part_rows)
        expand_came = [links.send(own_expand, step) for step in ("z1", "z2", "z3")]
        expand_four = stack(own_expand, *expand_came, wait=[joint_last])
        expand_across, expand_other = links.send(expand_four, "yx"), links.send(expand_four, "xy")
        reduce_came = [links.send(own_reduce, step) for step in ("z1", "z2", "z3")]
        joint_table = expand_table = reduce_table = numbers(links.table_second(part_rows, 0))
        joint_out = expand_out = reduce_out = numbers(links.table_second(part_rows, 0, True))
        expand_how, reduce_how, fold = (1, 0, 1), (1, 0, 2), 2
        joint_shapes = [(4, part_rows, 2 * width + 128)] * 4
        expand_shapes = [(4, part_rows, half_units)] * 4
        reduce_shapes = [(8, part_rows, half_units)] + expand_shapes[:2]
        lines = None
    else:
        both_tokens = jnp.concatenate([flat, swap(flat)])
        both_grad, grad_sums = mask_call(grad_flat, swap(grad_flat), kept_all, slots)
        cut = lambda w, size: lax.dynamic_slice_in_dim(w, x * size, size, 0)
        joint_part = lax.dynamic_index_in_dim(
            cut(joint_weight, part_rows).reshape(part_rows, 3, 2, half), core, 2, keepdims=False
        ).reshape(part_rows, 3 * half)
        mixer_part = lax.dynamic_slice_in_dim(cut(mixer_weight, part_rows), core * half, half, 1)
        joint_part = jnp.concatenate([joint_part, mixer_part], axis=1).astype(BF)
        expand_part = lax.dynamic_index_in_dim(
            cut(expand_weight, part_rows).reshape(part_rows, ns, 2, unit_block), core, 2, keepdims=False
        )
        expand_part = expand_part.reshape(part_rows, half_units).astype(BF)
        reduce_part = lax.dynamic_slice_in_dim(
            reduce_weight, core * unit_block + x * reduce_rows, reduce_rows, 0
        ).astype(BF)
        joint_pieces, expand_pieces, reduce_pieces = map(gather_plain, (joint_part, expand_part, reduce_part))
        joint_table = expand_table = reduce_table = joint_out = expand_out = reduce_out = numbers([0])
        expand_how = reduce_how = (1, 0, 1)
        fold = 1
        joint_shapes = [(1, width, 2 * width)]
        expand_shapes = [(1, width, half_units)]
        reduce_shapes = [(1, half_units, width)]
        every = lax.all_gather(jnp.concatenate(vectors).astype(BF), "shard", axis=0, tiled=False).astype(F32)
        found, start = [], 0
        for vector in vectors:
            found.append(every[:, start : start + vector.shape[0]].reshape(-1))
            start += vector.shape[0]
        own_half = lambda v: lax.dynamic_slice_in_dim(v, core * half, half, 0)
        joint_lines = jnp.concatenate([own_half(found[2][:width]), own_half(found[2][width:])])
        expand_lines = lax.dynamic_index_in_dim(found[6].reshape(ns, 2, unit_block), core, 1, keepdims=False)
        lines = jnp.concatenate(
            [jnp.stack([found[0], found[1], found[3], found[4], found[5], found[7], joint_lines])]
            + [expand_lines.reshape(-1, width)]
        )

    unit, joint, mixer_own, lines = joint_call(
        joint_table, place, both_tokens, lines, joint_pieces, slots, 3 * half, ns
    )
    mixer_far = swap(mixer_own)
    if ring:
        expand_across = stack(expand_across)
        expand_pieces = [expand_four, expand_across, expand_other, links.send(expand_across, "xy")]
    attended_far, logs_far = attend_call(both_lengths, joint, count, count, slots)
    attended_other = swap(attended_far)
    attended, logs = attend_call(both_lengths, joint, 0, count, slots)
    if ring:
        reduce_four = stack(own_reduce, *reduce_came)
        reduce_pieces = [reduce_four] + [links.send(reduce_four, step) for step in ("yx", "xy", "d")]
    hidden, *normed_two = mixer_call(
        core_number, attended, attended_other, mixer_own, mixer_far, flat, lines, slots
    )
    normed_two = normed_two + [swap(part) for part in normed_two]
    active, slope, *dreduce_parts = expand_call(
        expand_table, reduce_out, normed_two, both_grad, lines, expand_pieces, reduce_shapes, tile, half_units,
        expand_how, fold,
    )

    if ring:
        reduce_sum = Sum(links, dreduce_parts)
    grad_before, dexpand_bias, *g_send, g_own = back_call(
        expand_table, reduce_table, both_grad, slope, expand_pieces, reduce_pieces, tile, expand_how, reduce_how,
        slots,
    )
    g_far = [swap(part) for part in g_send]
    dexpand_parts = dexpand_call(expand_out, normed_two, grad_before, expand_shapes, tile)
    if ring:
        units_sum = Sum(links, dexpand_parts)
    grad_hidden, grad_attn, grad_mine, grad_other, sums_two = attn_grad_call(
        core_number, g_own, g_far, hidden, grad_flat, kept, lines, mixer_own, mixer_far, slots
    )
    grad_far = swap(grad_other)
    dmixer_keep, dmixer_send = dmixer_call(core_number, attended, attended_other, grad_attn)
    dmixer_far = swap(dmixer_send)
    far_grads = attend_back_call(both_lengths, joint, grad_far, logs_far, count, slots)
    if ring:
        units_sum.second_step_of_both(reduce_sum)
    own_grads = attend_back_call(both_lengths, joint, grad_mine, logs, 0, slots)
    joint_sums, *djoint_parts = djoint_call(
        joint_table, joint_out, place, unit, lines, list(own_grads), list(far_grads), dmixer_keep, dmixer_far,
        sums_two, dexpand_bias, grad_sums, joint_pieces, joint_shapes, ns,
    )
    if ring:
        joint_sum = Sum(links, djoint_parts)
        units_sum.third_step()

    joint_shape = (width, 3 * half)
    rows_far = split_call(
        joint_table, list(far_grads), joint_pieces, joint_shape, True, slots, 0, count, "grad_rows_far"
    )
    rows_far = [swap(part) for part in rows_far]
    branch_far = split_call(
        reduce_table, [active], reduce_pieces, (half_units, width), False, slots, count, count, "branch_far", how=reduce_how
    )
    branch_far = [swap(part) for part in branch_far]
    if ring:
        joint_sum.second_step()
    wide = pl.BlockSpec((slots, width), lambda i, *_: (i, 0))
    input_grad, sums_one = split_call(
        joint_table, list(own_grads), joint_pieces, joint_shape, True, slots, 0, count, "grad_rows",
        [(flat, wide), (grad_hidden, wide), full(lines)] + [full(part) for part in rows_far],
        [((rows, width), BF, wide), ((2, width), F32, fixed((2, width)))],
        rows_finish,
    )
    if ring:
        joint_sum.third_step()
    (layer_out,) = split_call(
        reduce_table, [active], reduce_pieces, (half_units, width), False, slots, 0, count, "branch",
        [(hidden, wide), (kept, pl.BlockSpec((slots, 1), lambda i, *_: (i, 0))), full(lines)]
        + [full(part) for part in branch_far],
        [((rows, width), BF, wide)],
        branch_finish,
        reduce_how,
    )

    if ring:
        units_sum.fourth_step()
        joint_sum.fourth_step()
        units_sum.fifth_step()
        dexpand, dreduce = unpack_units(place, units_sum.total, units_sum.other, unit_block)
        joint_sum.fifth_step()
        djoint, dmixer, small = unpack_joint(place, joint_sum.total, joint_sum.other)
        small = small.reshape(-1)
    else:
        shard_rows = nx * part_rows
        djoint, dexpand, dreduce = map(sum_plain, (djoint_parts, dexpand_parts, dreduce_parts))
        dmixer = djoint[..., 3 * half :].reshape(2, shard_rows, half)
        dmixer = dmixer.transpose(1, 0, 2).reshape(shard_rows, width).astype(F32)
        djoint = djoint[..., : 3 * half].reshape(2, shard_rows, 3, half)
        djoint = djoint.transpose(1, 2, 0, 3).reshape(shard_rows, 3 * width).astype(F32)
        dexpand = dexpand.reshape(2, shard_rows, ns, unit_block).transpose(1, 2, 0, 3)
        dexpand = dexpand.reshape(shard_rows, hidden_units).astype(F32)
        dreduce = dreduce.reshape(2 * unit_block, width).astype(F32)
        zeros = jnp.zeros((half,), F32)
        spot = lambda v: jnp.where(core == 0, jnp.concatenate([v, zeros]), jnp.concatenate([zeros, v]))
        expand_sums = dexpand_bias.reshape(ns, 1, unit_block)
        gap = jnp.zeros_like(expand_sums)
        expand_sums = jnp.where(
            core == 0, jnp.concatenate([expand_sums, gap], axis=1), jnp.concatenate([gap, expand_sums], axis=1)
        )
        sums = (
            sums_one[0],
            sums_one[1],
            jnp.concatenate([spot(joint_sums[0]), spot(joint_sums[2])]),
            sums_two[2],
            sums_two[0],
            sums_two[1],
            expand_sums,
            grad_sums,
        )
        total = lax.psum(jnp.concatenate([v.reshape(ns, -1) for v in sums], axis=1), ALL)
        small = lax.dynamic_index_in_dim(total, lax.axis_index("shard"), 0, keepdims=False)
    pieces, start = [], 0
    for vector in vectors:
        pieces.append(small[start : start + vector.shape[0]])
        start += vector.shape[0]
    small = pieces
    return (
        layer_out.reshape(tokens.shape),
        input_grad.reshape(tokens.shape),
        small[0],
        small[1],
        djoint,
        small[2],
        dmixer,
        small[3],
        small[4],
        small[5],
        dexpand,
        small[6],
        dreduce,
        small[7],
    )


def solution(mesh):
    ns = mesh.shape["shard"]
    nx = mesh.shape["rep"] // 2
    split = Mesh(mesh.devices.reshape(nx, 2, ns), ALL)
    rows, vector, matrix = P(ALL), P("shard"), P("shard", None)
    return jax.shard_map(
        functools.partial(on_device, nx, ns),
        mesh=split,
        in_specs=(
            rows,
            rows,
            rows,
            vector,
            vector,
            matrix,
            vector,
            matrix,
            vector,
            vector,
            vector,
            matrix,
            vector,
            matrix,
            vector,
        ),
        out_specs=(
            rows,
            rows,
            vector,
            vector,
            matrix,
            vector,
            matrix,
            vector,
            vector,
            vector,
            matrix,
            vector,
            matrix,
            vector,
        ),
        check_vma=False,
    )
```

time: 926 us -> 428 us (0.46)
  the two profiles are of different devices: /device:TPU:0 before, /device:TPU:9 now
where the time goes in v3:
time: 428 us; the launch traced here: 421 us
  Pallas kernels  198 us (46%)
  waiting for transfers between devices  125 us (29%)
  starting transfers between devices  57.5 us (13%)
  local copies, waits for them, and re-layouts  38.5 us (9%)
    pallas_call x35, Pallas kernels, call(): pl.pallas_call(body, grid_spec=pltpu.PrefetchScalarGridSpec(num_scalar_pr...  198 us
    ppermute x33, waiting for transfers between devices, send(): return lax.ppermute(array, ALL, pairs)  121 us
    ppermute x33, starting transfers between devices, send(): return lax.ppermute(array, ALL, pairs)  42.1 us
    unnamed x121, local copies, waits for them, and re-layouts  30.3 us
    ppermute x17, starting transfers between devices, swap(): return lax.ppermute(array, 'core', [(0, 1), (1, 0)])  15.4 us
  transfers between devices with their start and end apart: 50, of which 21 were waited for; matrix products, arithmetic and copies ran while one was open for 2% of the time, Pallas kernels for 46%

profile of v3, /device:TPU:9, one launch (start us, length us, event | category | flops | bytes accessed | tf_op | source)
XLA Modules:
  0.0 421.1 jit_solution(17170554559729506969)
XLA Ops:
  8.1 3.2 pack_joint.1
  11.3 1.5 collective-permute-start.4
  14.6 3.4 collective-permute-start.5
  21.0 1.5 copy-done.34
  22.6 4.8 %kept_rows.1 = (bf16[1280,1024]{1,0:T(8,128)(2,1)}, f32[1,1024]{1,0:T(1,128)}, f32[8,128]{1,0:T(8,128)}) custom-call(f32[8,128]{1,0:T(8,128)} %copy-done.31, bf16[640,1024]{1,0:T(8,128)(2,1)} %bitcast.44, bf16[640,1024]{1,0:T(8,128)(2,1)} %collective-permute-done.2.refs_2_, f32[1280,1]{1,0:T(8,128)} %convert_element_type.7.refs_3_), custom_call_target="tpu_custom_call" | custom-call | tf_op jit(solution)/shard_map/kept_rows/pallas_call | solution.py:53
  28.4 8.4 %collective-permute-done.5.refs_4_ = bf16[1,64,2176]{2,1,0:T(8,128)(2,1)} collective-permute-done((bf16[1,64,2176]{2,1,0:T(8,128)(2,1)}, bf16[1,64,2176]{2,1,0:T(8,128)(2,1)}, u32[]{:S(2)}, u32[]{:S(2)}) %collective-permute-start.5) | collective-permute-done | bytes 278560 | tf_op jit(solution)/shard_map/ppermute | solution.py:1058
  39.9 13.4 %collective-permute-done.9.refs_5_.refs_18_.refs_6_ = bf16[4,64,2176]{2,1,0:T(8,128)(2,1)S(1)} collective-permute-done((bf16[4,64,2176]{2,1,0:T(8,128)(2,1)S(1)}, bf16[4,64,2176]{2,1,0:T(8,128)(2,1)S(1)}, u32[]{:S(2)}, u32[]{:S(2)}) %collective-permute-start.9) | collective-permute-done | bytes 1114144 | tf_op jit(solution)/shard_map/ppermute | solution.py:1058
  57.1 4.9 %collective-permute-start.8 = (bf16[1,64,2048]{2,1,0:T(8,128)(2,1)S(1)}, bf16[1,64,2048]{2,1,0:T(8,128)(2,1)S(1)}, u32[]{:S(2)}, u32[]{:S(2)}) collective-permute-start(bf16[1,64,2048]{2,1,0:T(8,128)(2,1)S(1)} %get-tuple-element.133.refs_1_), channel_id=1, source_target_pairs={{0,4},{1,5},{2,6},{3,7},{4,0},{5,1},{6,2},{7,3},{8,12},{9,13},{10,... | collective-permute-start | bytes 786440 | tf_op jit(solution)/shard_map/ppermute | solution.py:1058
  62.0 10.2 %collective-permute-done.7.refs_3_ = bf16[1,64,2048]{2,1,0:T(8,128)(2,1)S(1)} collective-permute-done((bf16[1,64,2048]{2,1,0:T(8,128)(2,1)S(1)}, bf16[1,64,2048]{2,1,0:T(8,128)(2,1)S(1)}, u32[]{:S(2)}, u32[]{:S(2)}) %collective-permute-start.7) | collective-permute-done | bytes 262176 | tf_op jit(solution)/shard_map/ppermute | solution.py:1058
  72.2 6.3 %collective-permute-done.8.refs_4_ = bf16[1,64,2048]{2,1,0:T(8,128)(2,1)S(1)} collective-permute-done((bf16[1,64,2048]{2,1,0:T(8,128)(2,1)S(1)}, bf16[1,64,2048]{2,1,0:T(8,128)(2,1)S(1)}, u32[]{:S(2)}, u32[]{:S(2)}) %collective-permute-start.8) | collective-permute-done | bytes 262176 | tf_op jit(solution)/shard_map/ppermute | solution.py:1058
  82.0 12.3 %joint_rows.1 = (bf16[1280,1024]{1,0:T(8,128)(2,1)}, bf16[1280,1536]{1,0:T(8,128)(2,1)}, bf16[1024,512]{1,0:T(8,128)(2,1)}, f32[9,1024]{1,0:T(8,128)}, f32[8,128]{1,0:T(8,128)}) custom-call(s32[16]{0:T(128)} %stack.103.refs_0_.refs_1_, s32[2]{0:T(128)} %pad_add_fusion.refs_0_.refs_1_.refs_2_, f32[8,128]{1,0:T(8,128)} %copy-done.38, ...), custom_call_target="tpu_custom_call" | custom-call | flops 4026531840 | bytes 9699328 | tf_op jit(solution)/shard_map/joint_rows/pallas_call | solution.py:53
  94.3 2.5 collective-permute-start.17
  99.3 6.2 %attend.2 = (bf16[640,512]{1,0:T(8,128)(2,1)}, f32[2,2,1,1280]{3,2,1,0:T(1,128)}, f32[8,128]{1,0:T(8,128)}) custom-call(s32[4]{0:T(128)} %copy-done.50, f32[8,128]{1,0:T(8,128)} %copy-done.33, bf16[1280,1536]{1,0:T(8,128)(2,1)} %get-tuple-element.140.refs_2_.refs_3_.refs_4_, bf16[1280,1536]{1,0:T(8,128)(2,1)} %get-tuple-element.140.refs_2_.refs_3_.refs_4_, ...), custom_call_target="tpu_custom_call" | custom-call | flops 1677721600 | bytes 2621440 | tf_op jit(solution)/shard_map/attend/pallas_call | solution.py:53
  106.1 3.1 collective-permute-start.13
  110.7 9.5 %collective-permute-done.13.refs_2_ = bf16[1,64,2048]{2,1,0:T(8,128)(2,1)S(1)} collective-permute-done((bf16[1,64,2048]{2,1,0:T(8,128)(2,1)S(1)}, bf16[1,64,2048]{2,1,0:T(8,128)(2,1)S(1)}, u32[]{:S(2)}, u32[]{:S(2)}) %collective-permute-start.13) | collective-permute-done | bytes 262176 | tf_op jit(solution)/shard_map/ppermute | solution.py:1058
  122.9 6.2 %attend.3 = (bf16[640,512]{1,0:T(8,128)(2,1)}, f32[2,2,1,1280]{3,2,1,0:T(1,128)}, f32[8,128]{1,0:T(8,128)}) custom-call(s32[4]{0:T(128)} %copy-done.50, f32[8,128]{1,0:T(8,128)} %get-tuple-element.141.refs_1_, bf16[1280,1536]{1,0:T(8,128)(2,1)} %get-tuple-element.140.refs_2_.refs_3_.refs_4_, bf16[1280,1536]{1,0:T(8,128)(2,1)} %get-tuple-element.140.refs_2_.refs_3_.refs_4_, ...), custom_call_target="tpu_custom_call" | custom-call | flops 1677721600 | bytes 2621440 | tf_op jit(solution)/shard_map/attend/pallas_call | solution.py:53
  129.1 5.0 %collective-permute-done.15.refs_4_ = bf16[1,64,2048]{2,1,0:T(8,128)(2,1)S(1)} collective-permute-done((bf16[1,64,2048]{2,1,0:T(8,128)(2,1)S(1)}, bf16[1,64,2048]{2,1,0:T(8,128)(2,1)S(1)}, u32[]{:S(2)}, u32[]{:S(2)}) %collective-permute-start.15) | collective-permute-done | bytes 262176 | tf_op jit(solution)/shard_map/ppermute | solution.py:1058
  136.6 6.3 %mixer.1 = (f32[640,1024]{1,0:T(8,128)}, bf16[320,1024]{1,0:T(8,128)(2,1)}, bf16[320,1024]{1,0:T(8,128)(2,1)}, f32[8,128]{1,0:T(8,128)}) custom-call(s32[1]{0:T(128)} %bitcast.17.refs_0_, f32[8,128]{1,0:T(8,128)} %copy-done.40, bf16[640,512]{1,0:T(8,128)(2,1)} %get-tuple-element.145.refs_2_, bf16[640,512]{1,0:T(8,128)(2,1)} %copy-done.53, ...), custom_call_target="tpu_custom_call" | custom-call | flops 1342177280 | bytes 6553600 | tf_op jit(solution)/shard_map/mixer/pallas_call | solution.py:53
  149.3 25.6 %expand_and_dreduce.1 = (bf16[1280,2048]{1,0:T(8,128)(2,1)}, bf16[1280,2048]{1,0:T(8,128)(2,1)}, bf16[8,64,2048]{2,1,0:T(8,128)(2,1)}, bf16[4,64,2048]{2,1,0:T(8...) custom-call(s32[16]{0:T(128)} %stack.103.refs_0_.refs_1_, s32[16]{0:T(128)} %stack.104.refs_1_.refs_0_, ...), custom_call_target="tpu_custom_call" | custom-call | flops 10737418240 | bytes 24117248 | tf_op jit(solution)/shard_map/expand_and_dreduce/pallas_call | solution.py:53
  175.8 16.8 %collective-permute-done.23.refs_11_.refs_5_ = bf16[4,64,2048]{2,1,0:T(8,128)(2,1)} collective-permute-done((bf16[4,64,2048]{2,1,0:T(8,128)(2,1)S(1)}, bf16[4,64,2048]{2,1,0:T(8,128)(2,1)}, u32[]{:S(2)}, u32[]{:S(2)}) %collective-permute-start.23) | collective-permute-done | bytes 1048608 | tf_op jit(solution)/shard_map/ppermute | solution.py:1058
  192.6 21.2 %grad_before.1 = (bf16[1280,2048]{1,0:T(8,128)(2,1)}, f32[1,2048]{1,0:T(1,128)}, bf16[320,1024]{1,0:T(8,128)(2,1)}, bf16[320,1024]{1,0:T(8,128)(2,1)}, f32[640,1024]{1,0:T(8,128)}, /*index=5*/f32[8,128]{1,0:T(8,128)}) custom-call(s32[16]{0:T(128)} %stack.103.refs_0_.refs_1_, s32[16]{0:T(128)} %stack.103.refs_0_.refs_1_, ...), custom_call_target="tpu_custom_call" | custom-call | flops 10737418240 | bytes 24117248 | tf_op jit(solution)/shard_map/grad_before/pallas_call | solution.py:53
  215.3 14.3 %dexpand.1 = (bf16[4,64,2048]{2,1,0:T(8,128)(2,1)}, bf16[4,64,2048]{2,1,0:T(8,128)(2,1)}, bf16[4,64,2048]{2,1,0:T(8,128)(2,1)}, bf16[4,64,2048]{2,1,0:T(8,128)(2,1)}, f32[8,128]{1,0:T(8,128)}) custom-call(s32[16]{0:T(128)} %stack.104.refs_1_.refs_0_, f32[8,128]{1,0:T(8,128)} %get-tuple-element.157.refs_1_, ...), custom_call_target="tpu_custom_call" | custom-call | flops 5368709120 | bytes 12058624 | tf_op jit(solution)/shard_map/dexpand/pallas_call | solution.py:53
  231.4 8.8 %grad_attended.1 = (f32[640,1024]{1,0:T(8,128)}, bf16[640,1024]{1,0:T(8,128)(2,1)}, bf16[640,512]{1,0:T(8,128)(2,1)}, bf16[640,512]{1,0:T(8,128)(2,1)}, f32[3,1024]{1,0:T(4,128)}, /*index=5*/f32[8,128]{1,0:T(8,128)}) custom-call(s32[1]{0:T(128)} %bitcast.17.refs_0_, f32[8,128]{1,0:T(8,128)} %get-tuple-element.159.refs_1_, ...), custom_call_target="tpu_custom_call" | custom-call | flops 1342177280 | bytes 11796480 | tf_op jit(solution)/shard_map/grad_attended/pallas_call | solution.py:53
  242.0 4.5 %dmixer.1 = (bf16[1024,512]{1,0:T(8,128)(2,1)}, bf16[1024,512]{1,0:T(8,128)(2,1)}, f32[8,128]{1,0:T(8,128)}) custom-call(s32[1]{0:T(128)} %bitcast.17.refs_0_, f32[8,128]{1,0:T(8,128)} %get-tuple-element.164.refs_1_, bf16[640,512]{1,0:T(8,128)(2,1)} %get-tuple-element.145.refs_2_, bf16[640,512]{1,0:T(8,128)(2,1)} %copy-done.53, ...), custom_call_target="tpu_custom_call" | custom-call | flops 1342177280 | bytes 4718592 | tf_op jit(solution)/shard_map/dmixer/pallas_call | solution.py:53
  247.4 9.6 %attend_back.2 = (bf16[640,512]{1,0:T(8,128)(2,1)}, bf16[640,512]{1,0:T(8,128)(2,1)}, bf16[640,512]{1,0:T(8,128)(2,1)}, f32[8,128]{1,0:T(8,128)}) custom-call(s32[4]{0:T(128)} %copy-done.50, f32[8,128]{1,0:T(8,128)} %get-tuple-element.166.refs_1_, bf16[1280,1536]{1,0:T(8,128)(2,1)} %get-tuple-element.140.refs_2_.refs_3_.refs_4_, ...), custom_call_target="tpu_custom_call" | custom-call | flops 4194304000 | bytes 4587520 | tf_op jit(solution)/shard_map/attend_back/pallas_call | solution.py:53
  263.4 2.2 add_pairs.1
  266.5 9.0 %attend_back.3 = (bf16[640,512]{1,0:T(8,128)(2,1)}, bf16[640,512]{1,0:T(8,128)(2,1)}, bf16[640,512]{1,0:T(8,128)(2,1)}, f32[8,128]{1,0:T(8,128)}) custom-call(s32[4]{0:T(128)} %copy-done.50, f32[8,128]{1,0:T(8,128)} %copy-done.39, bf16[1280,1536]{1,0:T(8,128)(2,1)} %get-tuple-element.140.refs_2_.refs_3_.refs_4_, ...), custom_call_target="tpu_custom_call" | custom-call | flops 4194304000 | bytes 4587520 | tf_op jit(solution)/shard_map/attend_back/pallas_call | solution.py:53
  275.5 15.9 %djoint.1 = (f32[3,512]{1,0:T(4,128)}, bf16[4,64,2176]{2,1,0:T(8,128)(2,1)}, bf16[4,64,2176]{2,1,0:T(8,128)(2,1)}, bf16[4,64,2176]{2,1,0:T(8,128)(2,1)}, bf16[4,64,2176]{2,1,0:T(8,128)(2,1)}, /*index=5*/f32[8,128]{1,0:T(8,128)}) custom-call(s32[16]{0:T(128)} %stack.103.refs_0_.refs_1_, s32[16]{0:T(128)} %stack.104.refs_1_.refs_0_, ...), custom_call_target="tpu_custom_call" | custom-call | flops 4026531840 | bytes 10747904 | tf_op jit(solution)/shard_map/djoint/pallas_call | solution.py:53
  295.5 7.4 %grad_rows_far.1 = (bf16[320,1024]{1,0:T(8,128)(2,1)}, bf16[320,1024]{1,0:T(8,128)(2,1)}, f32[8,128]{1,0:T(8,128)}) custom-call(s32[16]{0:T(128)} %stack.103.refs_0_.refs_1_, f32[8,128]{1,0:T(8,128)} %copy-done.41, bf16[640,512]{1,0:T(8,128)(2,1)} %get-tuple-element.185.refs_9_.refs_2_, bf16[640,512]{1,0:T(8,128)(2,1)} %get-tuple-element.186.refs_10_.refs_3_, ...), custom_call_target="tpu_custom_call" | custom-call | flops 2013265920 | bytes 7733248 | tf_op jit(solution)/shard_map/grad_rows_far/pallas_call | solution.py:53
  303.0 8.7 %branch_far.1 = (bf16[320,1024]{1,0:T(8,128)(2,1)}, bf16[320,1024]{1,0:T(8,128)(2,1)}, f32[8,128]{1,0:T(8,128)}) custom-call(s32[16]{0:T(128)} %stack.103.refs_0_.refs_1_, f32[8,128]{1,0:T(8,128)} %get-tuple-element.197.refs_1_, bf16[1280,2048]{1,0:T(8,128)(2,1)} %get-tuple-element.198.refs_2_, bf16[4,64,2048]{2,1,0:T(8,128)(2,1)} %copy-done.7, ...), custom_call_target="tpu_custom_call" | custom-call | flops 2684354560 | bytes 9437184 | tf_op jit(solution)/shard_map/branch_far/pallas_call | solution.py:53
  313.4 1.5 collective-permute-start.35
  315.4 4.1 collective-permute-done.34.refs_2_
  319.5 3.6 collective-permute-start.39
  323.2 3.2 collective-permute-start.40
  326.3 1.5 collective-permute-start.41
  327.8 3.3 collective-permute-done.37.refs_2_.refs_4_.refs_6_.refs_8_
  331.1 3.4 collective-permute-start.42
  335.6 9.6 %grad_rows.1 = (bf16[640,1024]{1,0:T(8,128)(2,1)}, f32[2,1024]{1,0:T(2,128)}, f32[8,128]{1,0:T(8,128)}) custom-call(s32[16]{0:T(128)} %stack.103.refs_0_.refs_1_, f32[8,128]{1,0:T(8,128)} %copy-done.27, bf16[640,512]{1,0:T(8,128)(2,1)} %get-tuple-element.182.refs_6_.refs_2_, bf16[640,512]{1,0:T(8,128)(2,1)} %get-tuple-element.183.refs_7_.refs_3_, ...), custom_call_target="tpu_custom_call" | custom-call | flops 2013265920 | bytes 7733248 | tf_op jit(solution)/shard_map/grad_rows/pallas_call | solution.py:53
  346.8 9.5 %branch.1 = (bf16[640,1024]{1,0:T(8,128)(2,1)}, f32[8,128]{1,0:T(8,128)}) custom-call(s32[16]{0:T(128)} %stack.103.refs_0_.refs_1_, f32[8,128]{1,0:T(8,128)} %copy-done.20, bf16[1280,2048]{1,0:T(8,128)(2,1)} %get-tuple-element.198.refs_2_, bf16[4,64,2048]{2,1,0:T(8,128)(2,1)} %copy-done.7, bf16[4,64,2048]{2,1,0:T(8,128)(2,1)} %collective-permute-done.22.refs_10_.refs_4_, ...), custom_call_target="tpu_custom_call" | custom-call | flops 2684354560 | bytes 9437184 | tf_op jit(solution)/shard_map/branch/pallas_call | solution.py:53
  356.2 3.8 collective-permute-done.40.refs_2_
  360.1 11.6 %collective-permute-done.41.refs_3_ = bf16[2,64,2048]{2,1,0:T(8,128)(2,1)S(1)} collective-permute-done((bf16[2,64,2048]{2,1,0:T(8,128)(2,1)S(1)}, bf16[2,64,2048]{2,1,0:T(8,128)(2,1)S(1)}, u32[]{:S(2)}, u32[]{:S(2)}) %collective-permute-start.41) | collective-permute-done | bytes 524320 | tf_op jit(solution)/shard_map/ppermute | solution.py:1058
  376.8 10.4 %collective-permute-done.43.refs_2_ = bf16[1,64,2176]{2,1,0:T(8,128)(2,1)S(1)} collective-permute-done((bf16[1,64,2176]{2,1,0:T(8,128)(2,1)S(1)}, bf16[1,64,2176]{2,1,0:T(8,128)(2,1)S(1)}, u32[]{:S(2)}, u32[]{:S(2)}) %collective-permute-start.43) | collective-permute-done | bytes 278560 | tf_op jit(solution)/shard_map/ppermute | solution.py:1058
  387.2 10.7 %collective-permute-done.44.refs_3_ = bf16[1,64,2176]{2,1,0:T(8,128)(2,1)S(1)} collective-permute-done((bf16[1,64,2176]{2,1,0:T(8,128)(2,1)S(1)}, bf16[1,64,2176]{2,1,0:T(8,128)(2,1)S(1)}, u32[]{:S(2)}, u32[]{:S(2)}) %collective-permute-start.44) | collective-permute-done | bytes 278560 | tf_op jit(solution)/shard_map/ppermute | solution.py:1058
  397.9 2.0 collective-permute-done.45.refs_4_
  403.8 2.8 unpack_units.1
  406.6 3.1 collective-permute-done.48.refs_2_
  411.2 1.6 collective-permute-done.49.refs_3_
  413.6 3.3 unpack_joint.1
  (221 shorter events, 78.1 us)
Async XLA Ops:
  0.7 18.9 %collective-permute-start.1 = (bf16[640,1024]{1,0:T(8,128)(2,1)}, bf16[640,1024]{1,0:T(8,128)(2,1)S(1)}, u32[]{:S(2)}, u32[]{:S(2)}) collective-permute-start(bf16[640,1024]{1,0:T(8,128)(2,1)} %bitcast.39), channel_id=1, source_target_pairs={{0,8},{8,0},{1,9},{9,1},{2,10},{10,2},{3,11},{11,3},{4,12},{12,4},... | collective-permute-start | bytes 3932168 | tf_op jit(solution)/shard_map/ppermute | solution.py:1131
  1.4 21.1 %collective-permute-start.2 = (bf16[640,1024]{1,0:T(8,128)(2,1)}, bf16[640,1024]{1,0:T(8,128)(2,1)}, u32[]{:S(2)}, u32[]{:S(2)}) collective-permute-start(bf16[640,1024]{1,0:T(8,128)(2,1)} %bitcast.43), channel_id=1, source_target_pairs={{0,8},{8,0},{1,9},{9,1},{2,10},{10,2},{3,11},{11,3},{4,12},{12,4},... | collective-permute-start | bytes 3932168 | tf_op jit(solution)/shard_map/ppermute | solution.py:1131
  11.3 16.1 %collective-permute-start.3 = (bf16[1,64,2176]{2,1,0:T(8,128)(2,1)}, bf16[1,64,2176]{2,1,0:T(8,128)(2,1)S(1)}, u32[]{:S(2)}, u32[]{:S(2)}) collective-permute-start(bf16[1,64,2176]{2,1,0:T(8,128)(2,1)} %get-tuple-element.130.refs_1_), channel_id=1, source_target_pairs={{0,2},{1,3},{2,4},{3,5},{4,6},{5,7},{6,0},{7,1},{8,14},{9,15},{10,... | collective-permute-start | bytes 835592 | tf_op jit(solution)/shard_map/ppermute | solution.py:1058
  11.3 17.0 %collective-permute-start.4 = (bf16[1,64,2176]{2,1,0:T(8,128)(2,1)}, bf16[1,64,2176]{2,1,0:T(8,128)(2,1)S(1)}, u32[]{:S(2)}, u32[]{:S(2)}) collective-permute-start(bf16[1,64,2176]{2,1,0:T(8,128)(2,1)} %get-tuple-element.130.refs_1_), channel_id=1, source_target_pairs={{0,6},{1,7},{2,0},{3,1},{4,2},{5,3},{6,4},{7,5},{8,10},{9,11},{10,... | collective-permute-start | bytes 835592 | tf_op jit(solution)/shard_map/ppermute | solution.py:1058
  14.6 22.2 %collective-permute-start.5 = (bf16[1,64,2176]{2,1,0:T(8,128)(2,1)}, bf16[1,64,2176]{2,1,0:T(8,128)(2,1)}, u32[]{:S(2)}, u32[]{:S(2)}) collective-permute-start(bf16[1,64,2176]{2,1,0:T(8,128)(2,1)} %get-tuple-element.130.refs_1_), channel_id=1, source_target_pairs={{0,4},{1,5},{2,6},{3,7},{4,0},{5,1},{6,2},{7,3},{8,12},{9,13},{10,... | collective-permute-start | bytes 835592 | tf_op jit(solution)/shard_map/ppermute | solution.py:1058
  38.6 14.7 %collective-permute-start.9 = (bf16[4,64,2176]{2,1,0:T(8,128)(2,1)S(1)}, bf16[4,64,2176]{2,1,0:T(8,128)(2,1)S(1)}, u32[]{:S(2)}, u32[]{:S(2)}) collective-permute-start(bf16[4,64,2176]{2,1,0:T(8,128)(2,1)S(1)} %get-tuple-element.134.refs_4_.refs_17_.refs_5_), channel_id=1, source_target_pairs={{0,1},{1,0},{2,3},{3,2},{4,5},{5,4},{6,7},{7,6},{8,24},{9,25},{10,... | collective-permute-start | bytes 3342344 | tf_op jit(solution)/shard_map/ppermute | solution.py:1058
  53.3 25.2 %collective-permute-start.10 = (bf16[4,64,2176]{2,1,0:T(8,128)(2,1)S(1)}, bf16[4,64,2176]{2,1,0:T(8,128)(2,1)S(1)}, u32[]{:S(2)}, u32[]{:S(2)}) collective-permute-start(bf16[4,64,2176]{2,1,0:T(8,128)(2,1)S(1)} %collective-permute-done.9.refs_5_.refs_18_.refs_6_), channel_id=1, source_target_pairs={{0,16},{1,17},{2,18},{3,19},{4,20},{5,21},{6,22},{7,23},{8,9},{9,8... | collective-permute-start | bytes 3342344 | tf_op jit(solution)/shard_map/ppermute | solution.py:1058
  54.6 27.5 %collective-permute-start.11 = (bf16[4,64,2176]{2,1,0:T(8,128)(2,1)S(1)}, bf16[4,64,2176]{2,1,0:T(8,128)(2,1)}, u32[]{:S(2)}, u32[]{:S(2)}) collective-permute-start(bf16[4,64,2176]{2,1,0:T(8,128)(2,1)S(1)} %get-tuple-element.134.refs_4_.refs_17_.refs_5_), channel_id=1, source_target_pairs={{0,16},{1,17},{2,18},{3,19},{4,20},{5,21},{6,22},{7,23},{8,9},{9,8... | collective-permute-start | bytes 3342344 | tf_op jit(solution)/shard_map/ppermute | solution.py:1058
  55.6 6.4 %collective-permute-start.6 = (bf16[1,64,2048]{2,1,0:T(8,128)(2,1)S(1)}, bf16[1,64,2048]{2,1,0:T(8,128)(2,1)S(1)}, u32[]{:S(2)}, u32[]{:S(2)}) collective-permute-start(bf16[1,64,2048]{2,1,0:T(8,128)(2,1)S(1)} %get-tuple-element.133.refs_1_), channel_id=1, source_target_pairs={{0,2},{1,3},{2,4},{3,5},{4,6},{5,7},{6,0},{7,1},{8,14},{9,15},{10,... | collective-permute-start | bytes 786440 | tf_op jit(solution)/shard_map/ppermute | solution.py:1058
  56.3 16.0 %collective-permute-start.7 = (bf16[1,64,2048]{2,1,0:T(8,128)(2,1)S(1)}, bf16[1,64,2048]{2,1,0:T(8,128)(2,1)S(1)}, u32[]{:S(2)}, u32[]{:S(2)}) collective-permute-start(bf16[1,64,2048]{2,1,0:T(8,128)(2,1)S(1)} %get-tuple-element.133.refs_1_), channel_id=1, source_target_pairs={{0,6},{1,7},{2,0},{3,1},{4,2},{5,3},{6,4},{7,5},{8,10},{9,11},{10,... | collective-permute-start | bytes 786440 | tf_op jit(solution)/shard_map/ppermute | solution.py:1058
  57.1 21.4 %collective-permute-start.8 = (bf16[1,64,2048]{2,1,0:T(8,128)(2,1)S(1)}, bf16[1,64,2048]{2,1,0:T(8,128)(2,1)S(1)}, u32[]{:S(2)}, u32[]{:S(2)}) collective-permute-start(bf16[1,64,2048]{2,1,0:T(8,128)(2,1)S(1)} %get-tuple-element.133.refs_1_), channel_id=1, source_target_pairs={{0,4},{1,5},{2,6},{3,7},{4,0},{5,1},{6,2},{7,3},{8,12},{9,13},{10,... | collective-permute-start | bytes 786440 | tf_op jit(solution)/shard_map/ppermute | solution.py:1058
  80.2 16.6 %collective-permute-start.12 = (bf16[4,64,2048]{2,1,0:T(8,128)(2,1)}, bf16[4,64,2048]{2,1,0:T(8,128)(2,1)}, u32[]{:S(2)}, u32[]{:S(2)}) collective-permute-start(bf16[4,64,2048]{2,1,0:T(8,128)(2,1)} %get-tuple-element.138.refs_9_.refs_5_), channel_id=1, source_target_pairs={{0,1},{1,0},{2,3},{3,2},{4,5},{5,4},{6,7},{7,6},{8,24},{9,25},{10,... | collective-permute-start | bytes 3145736 | tf_op jit(solution)/shard_map/ppermute | solution.py:1058
  94.3 41.1 %collective-permute-start.17 = (bf16[1024,512]{1,0:T(8,128)(2,1)}, bf16[1024,512]{1,0:T(8,128)(2,1)S(1)}, u32[]{:S(2)}, u32[]{:S(2)}) collective-permute-start(bf16[1024,512]{1,0:T(8,128)(2,1)} %get-tuple-element.147.refs_4_.refs_7_), channel_id=1, source_target_pairs={{0,8},{8,0},{1,9},{9,1},{2,10},{10,2},{3,11},{11,3},{4,12},{12,4},... | collective-permute-start | bytes 3145736 | tf_op jit(solution)/shard_map/ppermute | solution.py:1131
  105.5 29.9 %collective-permute-start.16 = (bf16[640,512]{1,0:T(8,128)(2,1)}, bf16[640,512]{1,0:T(8,128)(2,1)S(1)}, u32[]{:S(2)}, u32[]{:S(2)}) collective-permute-start(bf16[640,512]{1,0:T(8,128)(2,1)} %get-tuple-element.146), channel_id=1, source_target_pairs={{0,8},{8,0},{1,9},{9,1},{2,10},{10,2},{3,11},{11,3},{4,12},{12,4},... | collective-permute-start | bytes 1966088 | tf_op jit(solution)/shard_map/ppermute | solution.py:1131
  106.1 14.1 %collective-permute-start.13 = (bf16[1,64,2048]{2,1,0:T(8,128)(2,1)S(1)}, bf16[1,64,2048]{2,1,0:T(8,128)(2,1)S(1)}, u32[]{:S(2)}, u32[]{:S(2)}) collective-permute-start(bf16[1,64,2048]{2,1,0:T(8,128)(2,1)S(1)} %get-tuple-element.143.refs_1_), channel_id=1, source_target_pairs={{0,2},{1,3},{2,4},{3,5},{4,6},{5,7},{6,0},{7,1},{8,14},{9,15},{10,... | collective-permute-start | bytes 786440 | tf_op jit(solution)/shard_map/ppermute | solution.py:1058
  109.2 12.7 %collective-permute-start.14 = (bf16[1,64,2048]{2,1,0:T(8,128)(2,1)S(1)}, bf16[1,64,2048]{2,1,0:T(8,128)(2,1)S(1)}, u32[]{:S(2)}, u32[]{:S(2)}) collective-permute-start(bf16[1,64,2048]{2,1,0:T(8,128)(2,1)S(1)} %get-tuple-element.143.refs_1_), channel_id=1, source_target_pairs={{0,6},{1,7},{2,0},{3,1},{4,2},{5,3},{6,4},{7,5},{8,10},{9,11},{10,... | collective-permute-start | bytes 786440 | tf_op jit(solution)/shard_map/ppermute | solution.py:1058
  109.4 35.9 %collective-permute-start.20 = (bf16[4,64,2048]{2,1,0:T(8,128)(2,1)}, bf16[4,64,2048]{2,1,0:T(8,128)(2,1)S(1)}, u32[]{:S(2)}, u32[]{:S(2)}) collective-permute-start(bf16[4,64,2048]{2,1,0:T(8,128)(2,1)} %get-tuple-element.138.refs_9_.refs_5_), channel_id=1, source_target_pairs={{0,16},{1,17},{2,18},{3,19},{4,20},{5,21},{6,22},{7,23},{8,9},{9,8... | collective-permute-start | bytes 3145736 | tf_op jit(solution)/shard_map/ppermute | solution.py:1058
  120.2 25.7 %collective-permute-start.21 = (bf16[4,64,2048]{2,1,0:T(8,128)(2,1)S(1)}, bf16[4,64,2048]{2,1,0:T(8,128)(2,1)S(1)}, u32[]{:S(2)}, u32[]{:S(2)}) collective-permute-start(bf16[4,64,2048]{2,1,0:T(8,128)(2,1)S(1)} %get-tuple-element.153.refs_10_.refs_6_), channel_id=1, source_target_pairs={{0,16},{1,17},{2,18},{3,19},{4,20},{5,21},{6,22},{7,23},{8,9},{9,8... | collective-permute-start | bytes 3145736 | tf_op jit(solution)/shard_map/ppermute | solution.py:1058
  121.9 12.2 %collective-permute-start.15 = (bf16[1,64,2048]{2,1,0:T(8,128)(2,1)S(1)}, bf16[1,64,2048]{2,1,0:T(8,128)(2,1)S(1)}, u32[]{:S(2)}, u32[]{:S(2)}) collective-permute-start(bf16[1,64,2048]{2,1,0:T(8,128)(2,1)S(1)} %get-tuple-element.143.refs_1_), channel_id=1, source_target_pairs={{0,4},{1,5},{2,6},{3,7},{4,0},{5,1},{6,2},{7,3},{8,12},{9,13},{10,... | collective-permute-start | bytes 786440 | tf_op jit(solution)/shard_map/ppermute | solution.py:1058
  143.0 5.5 %collective-permute-start.18 = (bf16[320,1024]{1,0:T(8,128)(2,1)}, bf16[320,1024]{1,0:T(8,128)(2,1)S(1)}, u32[]{:S(2)}, u32[]{:S(2)}) collective-permute-start(bf16[320,1024]{1,0:T(8,128)(2,1)} %get-tuple-element.150.refs_3_.refs_2_), channel_id=1, source_target_pairs={{0,8},{8,0},{1,9},{9,1},{2,10},{10,2},{3,11},{11,3},{4,12},{12,4},... | collective-permute-start | bytes 1966088 | tf_op jit(solution)/shard_map/ppermute | solution.py:1131
  144.0 4.5 %collective-permute-start.19 = (bf16[320,1024]{1,0:T(8,128)(2,1)}, bf16[320,1024]{1,0:T(8,128)(2,1)}, u32[]{:S(2)}, u32[]{:S(2)}) collective-permute-start(bf16[320,1024]{1,0:T(8,128)(2,1)} %get-tuple-element.151.refs_4_.refs_3_), channel_id=1, source_target_pairs={{0,8},{8,0},{1,9},{9,1},{2,10},{10,2},{3,11},{11,3},{4,12},{12,4},... | collective-permute-start | bytes 1966088 | tf_op jit(solution)/shard_map/ppermute | solution.py:1131
  144.0 31.8 %collective-permute-start.22 = (bf16[4,64,2048]{2,1,0:T(8,128)(2,1)S(1)}, bf16[4,64,2048]{2,1,0:T(8,128)(2,1)}, u32[]{:S(2)}, u32[]{:S(2)}) collective-permute-start(bf16[4,64,2048]{2,1,0:T(8,128)(2,1)S(1)} %get-tuple-element.156.refs_9_.refs_3_), channel_id=1, source_target_pairs={{0,1},{1,0},{2,3},{3,2},{4,5},{5,4},{6,7},{7,6},{8,24},{9,25},{10,... | collective-permute-start | bytes 3145736 | tf_op jit(solution)/shard_map/ppermute | solution.py:1058
  145.3 47.3 %collective-permute-start.23 = (bf16[4,64,2048]{2,1,0:T(8,128)(2,1)S(1)}, bf16[4,64,2048]{2,1,0:T(8,128)(2,1)}, u32[]{:S(2)}, u32[]{:S(2)}) collective-permute-start(bf16[4,64,2048]{2,1,0:T(8,128)(2,1)S(1)} %get-tuple-element.156.refs_9_.refs_3_), channel_id=1, source_target_pairs={{0,16},{1,17},{2,18},{3,19},{4,20},{5,21},{6,22},{7,23},{8,9},{9,8... | collective-permute-start | bytes 3145736 | tf_op jit(solution)/shard_map/ppermute | solution.py:1058
  147.3 45.3 %collective-permute-start.24 = (bf16[4,64,2048]{2,1,0:T(8,128)(2,1)S(1)}, bf16[4,64,2048]{2,1,0:T(8,128)(2,1)}, u32[]{:S(2)}, u32[]{:S(2)}) collective-permute-start(bf16[4,64,2048]{2,1,0:T(8,128)(2,1)S(1)} %get-tuple-element.156.refs_9_.refs_3_), channel_id=1, source_target_pairs={{0,17},{1,16},{2,19},{3,18},{4,21},{5,20},{6,23},{7,22},{8,25},{9,... | collective-permute-start | bytes 3145736 | tf_op jit(solution)/shard_map/ppermute | solution.py:1058
  175.0 84.1 %collective-permute-start.30 = (bf16[8,64,2048]{2,1,0:T(8,128)(2,1)}, bf16[8,64,2048]{2,1,0:T(8,128)(2,1)S(1)}, u32[]{:S(2)}, u32[]{:S(2)}) collective-permute-start(bf16[8,64,2048]{2,1,0:T(8,128)(2,1)} %get-tuple-element.175), channel_id=1, source_target_pairs={{0,16},{1,17},{2,18},{3,19},{4,20},{5,21},{6,22},{7,23},{8,9},{9,8... | collective-permute-start | bytes 6291464 | tf_op jit(solution)/shard_map/ppermute | solution.py:1058
  213.8 16.6 %collective-permute-start.25 = (bf16[320,1024]{1,0:T(8,128)(2,1)}, bf16[320,1024]{1,0:T(8,128)(2,1)S(1)}, u32[]{:S(2)}, u32[]{:S(2)}) collective-permute-start(bf16[320,1024]{1,0:T(8,128)(2,1)} %get-tuple-element.162), channel_id=1, source_target_pairs={{0,8},{8,0},{1,9},{9,1},{2,10},{10,2},{3,11},{11,3},{4,12},{12,4},... | collective-permute-start | bytes 1966088 | tf_op jit(solution)/shard_map/ppermute | solution.py:1131
  214.0 16.3 %collective-permute-start.26 = (bf16[320,1024]{1,0:T(8,128)(2,1)}, bf16[320,1024]{1,0:T(8,128)(2,1)S(1)}, u32[]{:S(2)}, u32[]{:S(2)}) collective-permute-start(bf16[320,1024]{1,0:T(8,128)(2,1)} %get-tuple-element.163), channel_id=1, source_target_pairs={{0,8},{8,0},{1,9},{9,1},{2,10},{10,2},{3,11},{11,3},{4,12},{12,4},... | collective-permute-start | bytes 1966088 | tf_op jit(solution)/shard_map/ppermute | solution.py:1131
  229.6 27.4 %collective-permute-start.28 = (bf16[4,64,2048]{2,1,0:T(8,128)(2,1)}, bf16[4,64,2048]{2,1,0:T(8,128)(2,1)S(1)}, u32[]{:S(2)}, u32[]{:S(2)}) collective-permute-start(bf16[4,64,2048]{2,1,0:T(8,128)(2,1)} %get-tuple-element.171), channel_id=1, source_target_pairs={{0,16},{1,17},{2,18},{3,19},{4,20},{5,21},{6,22},{7,23},{8,9},{9,8... | collective-permute-start | bytes 3145736 | tf_op jit(solution)/shard_map/ppermute | solution.py:1058
  240.2 6.4 %collective-permute-start.27 = (bf16[640,512]{1,0:T(8,128)(2,1)}, bf16[640,512]{1,0:T(8,128)(2,1)S(1)}, u32[]{:S(2)}, u32[]{:S(2)}) collective-permute-start(bf16[640,512]{1,0:T(8,128)(2,1)} %get-tuple-element.167), channel_id=1, source_target_pairs={{0,8},{8,0},{1,9},{9,1},{2,10},{10,2},{3,11},{11,3},{4,12},{12,4},... | collective-permute-start | bytes 1966088 | tf_op jit(solution)/shard_map/ppermute | solution.py:1131
  241.1 16.8 %collective-permute-start.29 = (bf16[4,64,2048]{2,1,0:T(8,128)(2,1)}, bf16[4,64,2048]{2,1,0:T(8,128)(2,1)S(1)}, u32[]{:S(2)}, u32[]{:S(2)}) collective-permute-start(bf16[4,64,2048]{2,1,0:T(8,128)(2,1)} %get-tuple-element.173), channel_id=1, source_target_pairs={{0,16},{1,17},{2,18},{3,19},{4,20},{5,21},{6,22},{7,23},{8,9},{9,8... | collective-permute-start | bytes 3145736 | tf_op jit(solution)/shard_map/ppermute | solution.py:1058
  246.5 29.0 %collective-permute-start.31 = (bf16[1024,512]{1,0:T(8,128)(2,1)}, bf16[1024,512]{1,0:T(8,128)(2,1)}, u32[]{:S(2)}, u32[]{:S(2)}) collective-permute-start(bf16[1024,512]{1,0:T(8,128)(2,1)} %get-tuple-element.189), channel_id=1, source_target_pairs={{0,8},{8,0},{1,9},{9,1},{2,10},{10,2},{3,11},{11,3},{4,12},{12,4},... | collective-permute-start | bytes 3145736 | tf_op jit(solution)/shard_map/ppermute | solution.py:1131
  265.6 27.4 %collective-permute-start.32 = (bf16[8,64,2048]{2,1,0:T(8,128)(2,1)}, bf16[8,64,2048]{2,1,0:T(8,128)(2,1)S(1)}, u32[]{:S(2)}, u32[]{:S(2)}) collective-permute-start(bf16[8,64,2048]{2,1,0:T(8,128)(2,1)} %get-tuple-element.195), channel_id=1, source_target_pairs={{0,1},{1,0},{2,3},{3,2},{4,5},{5,4},{6,7},{7,6},{8,24},{9,25},{10,... | collective-permute-start | bytes 6291464 | tf_op jit(solution)/shard_map/ppermute | solution.py:1058
  291.4 20.2 %collective-permute-start.33 = (bf16[4,64,2176]{2,1,0:T(8,128)(2,1)}, bf16[4,64,2176]{2,1,0:T(8,128)(2,1)S(1)}, u32[]{:S(2)}, u32[]{:S(2)}) collective-permute-start(bf16[4,64,2176]{2,1,0:T(8,128)(2,1)} %get-tuple-element.201), channel_id=1, source_target_pairs={{0,16},{1,17},{2,18},{3,19},{4,20},{5,21},{6,22},{7,23},{8,9},{9,8... | collective-permute-start | bytes 3342344 | tf_op jit(solution)/shard_map/ppermute | solution.py:1058
  292.3 27.2 %collective-permute-start.34 = (bf16[4,64,2176]{2,1,0:T(8,128)(2,1)}, bf16[4,64,2176]{2,1,0:T(8,128)(2,1)S(1)}, u32[]{:S(2)}, u32[]{:S(2)}) collective-permute-start(bf16[4,64,2176]{2,1,0:T(8,128)(2,1)} %get-tuple-element.204), channel_id=1, source_target_pairs={{0,16},{1,17},{2,18},{3,19},{4,20},{5,21},{6,22},{7,23},{8,9},{9,8... | collective-permute-start | bytes 3342344 | tf_op jit(solution)/shard_map/ppermute | solution.py:1058
  312.7 18.4 %collective-permute-start.37 = (bf16[4,64,2176]{2,1,0:T(8,128)(2,1)S(1)}, bf16[4,64,2176]{2,1,0:T(8,128)(2,1)S(1)}, u32[]{:S(2)}, u32[]{:S(2)}) collective-permute-start(bf16[4,64,2176]{2,1,0:T(8,128)(2,1)S(1)} %get-tuple-element.211), channel_id=1, source_target_pairs={{0,1},{1,0},{2,3},{3,2},{4,5},{5,4},{6,7},{7,6},{8,24},{9,25},{10,... | collective-permute-start | bytes 3342344 | tf_op jit(solution)/shard_map/ppermute | solution.py:1058
  313.4 9.8 %collective-permute-start.35 = (bf16[320,1024]{1,0:T(8,128)(2,1)}, bf16[320,1024]{1,0:T(8,128)(2,1)S(1)}, u32[]{:S(2)}, u32[]{:S(2)}) collective-permute-start(bf16[320,1024]{1,0:T(8,128)(2,1)} %get-tuple-element.207), channel_id=1, source_target_pairs={{0,8},{8,0},{1,9},{9,1},{2,10},{10,2},{3,11},{11,3},{4,12},{12,4},... | collective-permute-start | bytes 1966088 | tf_op jit(solution)/shard_map/ppermute | solution.py:1131
  314.9 11.4 %collective-permute-start.36 = (bf16[320,1024]{1,0:T(8,128)(2,1)}, bf16[320,1024]{1,0:T(8,128)(2,1)S(1)}, u32[]{:S(2)}, u32[]{:S(2)}) collective-permute-start(bf16[320,1024]{1,0:T(8,128)(2,1)} %get-tuple-element.208), channel_id=1, source_target_pairs={{0,8},{8,0},{1,9},{9,1},{2,10},{10,2},{3,11},{11,3},{4,12},{12,4},... | collective-permute-start | bytes 1966088 | tf_op jit(solution)/shard_map/ppermute | solution.py:1131
  314.9 31.9 %collective-permute-start.38 = (bf16[320,1024]{1,0:T(8,128)(2,1)}, bf16[320,1024]{1,0:T(8,128)(2,1)}, u32[]{:S(2)}, u32[]{:S(2)}) collective-permute-start(bf16[320,1024]{1,0:T(8,128)(2,1)} %get-tuple-element.213), channel_id=1, source_target_pairs={{0,8},{8,0},{1,9},{9,1},{2,10},{10,2},{3,11},{11,3},{4,12},{12,4},... | collective-permute-start | bytes 1966088 | tf_op jit(solution)/shard_map/ppermute | solution.py:1131
  319.5 27.2 %collective-permute-start.39 = (bf16[320,1024]{1,0:T(8,128)(2,1)}, bf16[320,1024]{1,0:T(8,128)(2,1)}, u32[]{:S(2)}, u32[]{:S(2)}) collective-permute-start(bf16[320,1024]{1,0:T(8,128)(2,1)} %get-tuple-element.214), channel_id=1, source_target_pairs={{0,8},{8,0},{1,9},{9,1},{2,10},{10,2},{3,11},{11,3},{4,12},{12,4},... | collective-permute-start | bytes 1966088 | tf_op jit(solution)/shard_map/ppermute | solution.py:1131
  323.2 36.9 %collective-permute-start.40 = (bf16[2,64,2048]{2,1,0:T(8,128)(2,1)S(1)}, bf16[2,64,2048]{2,1,0:T(8,128)(2,1)S(1)}, u32[]{:S(2)}, u32[]{:S(2)}) collective-permute-start(bf16[2,64,2048]{2,1,0:T(8,128)(2,1)S(1)} %copy-done.37), channel_id=1, source_target_pairs={{0,4},{1,5},{2,6},{3,7},{4,0},{5,1},{6,2},{7,3},{8,12},{9,13},{10,... | collective-permute-start | bytes 1572872 | tf_op jit(solution)/shard_map/ppermute | solution.py:1058
  326.3 45.4 %collective-permute-start.41 = (bf16[2,64,2048]{2,1,0:T(8,128)(2,1)S(1)}, bf16[2,64,2048]{2,1,0:T(8,128)(2,1)S(1)}, u32[]{:S(2)}, u32[]{:S(2)}) collective-permute-start(bf16[2,64,2048]{2,1,0:T(8,128)(2,1)S(1)} %get-tuple-element.220), channel_id=1, source_target_pairs={{0,6},{1,7},{2,0},{3,1},{4,2},{5,3},{6,4},{7,5},{8,10},{9,11},{10,... | collective-permute-start | bytes 1572872 | tf_op jit(solution)/shard_map/ppermute | solution.py:1058
  331.1 41.4 %collective-permute-start.42 = (bf16[2,64,2048]{2,1,0:T(8,128)(2,1)S(1)}, bf16[2,64,2048]{2,1,0:T(8,128)(2,1)S(1)}, u32[]{:S(2)}, u32[]{:S(2)}) collective-permute-start(bf16[2,64,2048]{2,1,0:T(8,128)(2,1)S(1)} %get-tuple-element.221), channel_id=1, source_target_pairs={{0,2},{1,3},{2,4},{3,5},{4,6},{5,7},{6,0},{7,1},{8,14},{9,15},{10,... | collective-permute-start | bytes 1572872 | tf_op jit(solution)/shard_map/ppermute | solution.py:1058
  373.5 26.5 %collective-permute-start.46 = (bf16[2,64,2048]{2,1,0:T(8,128)(2,1)S(1)}, bf16[2,64,2048]{2,1,0:T(8,128)(2,1)S(1)}, u32[]{:S(2)}, u32[]{:S(2)}) collective-permute-start(bf16[2,64,2048]{2,1,0:T(8,128)(2,1)S(1)} %get-tuple-element.228.refs_1_), channel_id=1, source_target_pairs={{0,16},{1,17},{2,18},{3,19},{4,20},{5,21},{6,22},{7,23},{8,24},{9,... | collective-permute-start | bytes 1572872 | tf_op jit(solution)/shard_map/ppermute | solution.py:1058
  374.4 12.8 %collective-permute-start.43 = (bf16[1,64,2176]{2,1,0:T(8,128)(2,1)S(1)}, bf16[1,64,2176]{2,1,0:T(8,128)(2,1)S(1)}, u32[]{:S(2)}, u32[]{:S(2)}) collective-permute-start(bf16[1,64,2176]{2,1,0:T(8,128)(2,1)S(1)} %get-tuple-element.224), channel_id=1, source_target_pairs={{0,4},{1,5},{2,6},{3,7},{4,0},{5,1},{6,2},{7,3},{8,12},{9,13},{10,... | collective-permute-start | bytes 835592 | tf_op jit(solution)/shard_map/ppermute | solution.py:1058
  374.4 23.5 %collective-permute-start.44 = (bf16[1,64,2176]{2,1,0:T(8,128)(2,1)S(1)}, bf16[1,64,2176]{2,1,0:T(8,128)(2,1)S(1)}, u32[]{:S(2)}, u32[]{:S(2)}) collective-permute-start(bf16[1,64,2176]{2,1,0:T(8,128)(2,1)S(1)} %get-tuple-element.225), channel_id=1, source_target_pairs={{0,6},{1,7},{2,0},{3,1},{4,2},{5,3},{6,4},{7,5},{8,10},{9,11},{10,... | collective-permute-start | bytes 835592 | tf_op jit(solution)/shard_map/ppermute | solution.py:1058
  375.6 24.3 %collective-permute-start.45 = (bf16[1,64,2176]{2,1,0:T(8,128)(2,1)S(1)}, bf16[1,64,2176]{2,1,0:T(8,128)(2,1)S(1)}, u32[]{:S(2)}, u32[]{:S(2)}) collective-permute-start(bf16[1,64,2176]{2,1,0:T(8,128)(2,1)S(1)} %get-tuple-element.226), channel_id=1, source_target_pairs={{0,2},{1,3},{2,4},{3,5},{4,6},{5,7},{6,0},{7,1},{8,14},{9,15},{10,... | collective-permute-start | bytes 835592 | tf_op jit(solution)/shard_map/ppermute | solution.py:1058
  400.1 3.6 collective-permute-start.47
  401.5 8.2 %collective-permute-start.48 = (bf16[1,64,2176]{2,1,0:T(8,128)(2,1)S(1)}, bf16[1,64,2176]{2,1,0:T(8,128)(2,1)S(1)}, u32[]{:S(2)}, u32[]{:S(2)}) collective-permute-start(bf16[1,64,2176]{2,1,0:T(8,128)(2,1)S(1)} %get-tuple-element.232.refs_1_), channel_id=1, source_target_pairs={{0,16},{1,17},{2,18},{3,19},{4,20},{5,21},{6,22},{7,23},{8,24},{9,... | collective-permute-start | bytes 835592 | tf_op jit(solution)/shard_map/ppermute | solution.py:1058
  (59 other events, 370.0 us)
